TPU v7x, 32 devices: a whole 2x2x4 slice. The times are simulated.
32 devices in a mesh: grp: 2 (over y), tm: 4 (over z), row: 4 (over x, core).
Axes of the slice: x: 2, y: 2, z: 4, core: 2. Of those that a mesh axis runs over, the one named last changes fastest.
Arguments:
- terminal: bfloat16 [8, 2, 2048, 2048], P(('grp', 'tm'), None, None, 'row'), parts along dimension 0, may hold values from -12 to 12, as said below
- controls: float32 [8, 2], P(('grp', 'tm')), parts along dimension 0, may hold values from -3 to 3
- ham_blocks: bfloat16 [2, 64, 2, 32, 32], replicated, may hold values from -0.5 to 0.5
- ham_cols: int32 [2, 64], replicated, may hold values from 0 to 63, each once within a row
- jump_blocks: bfloat16 [64, 2, 32, 32], replicated, may hold values from -0.75 to 0.75
- jump_cols: int32 [2, 64], replicated, may hold values from 0 to 63, each once within a row
Outputs:
- new_cpoint: bfloat16 [8, 2, 2048, 2048], P(('grp', 'tm'), None, None, 'row'), parts along dimension 0
- new_fpoint: bfloat16 [8, 2, 2048, 2048], P(('grp', 'tm'), None, None, 'row'), parts along dimension 0
There are 2 independent parts, one for each index of `grp`. A program takes and returns all parts, laid end to end along the dimension named above; an argument that names none is the same for every part. Nothing has to cross between parts.
Inputs may be any that keep to these rules, and one draw needn't show every extreme that they name: `terminal`: every interval's state is Hermitian: the real part is symmetric and the imaginary part antisymmetric. Each row of ham_cols names every block column once. Each row of jump_cols names every block column once.
All inputs are finite; a program needn't handle non-finite values.
Results may differ from a plain program's by a relative error of at most 0.0041.
Values may be sent and summed in bfloat16 or wider, within the bound.
No kernel may reach another device: no remote copies, remote signals or barrier semaphores. Data moves between devices by JAX's collectives and lax.ppermute only.
A program may use at most 192 MiB of HBM per device.

v0:
```python
import functools

import jax
import jax.numpy as jnp
from jax import lax
from jax.experimental import pallas as pl
from jax.experimental.pallas import tpu as pltpu
from jax.sharding import PartitionSpec as P

time_step = 0.2
F32 = jnp.float32
BF16 = jnp.bfloat16


def shifted_down(block, axis):
    route = [(i, i - 1) for i in range(1, lax.axis_size(axis))]
    return lax.ppermute(block, axis, route)


def table_kernel(ham_cols, jump_cols, amplitudes, ham, jump, rows, jump_row, *tables):
    layers_h, count = ham_cols.shape
    layers_j = jump_cols.shape[0]
    size = ham.shape[-1]
    crossed = [(k, other) for k in range(layers_j) for other in range(layers_j) if k != other]
    first_k = 2 * layers_h
    first_j = first_k + 1 + len(crossed)

    @pl.loop(0, count)
    def _(b):
        for k in range(layers_h):
            rows[k, b] = ham_cols[k, b] * size
            rows[layers_h + k, ham_cols[k, b]] = b * size
        for k in range(layers_j):
            rows[first_j + k, jump_cols[k, b]] = b * size

    @pl.loop(0, count, unroll=2)
    def _(c):
        came_h = [rows[layers_h + k, c] // size for k in range(layers_h)]
        came_j = [rows[first_j + k, c] // size for k in range(layers_j)]
        rows[first_k, c] = c * size
        for at, (k, other) in enumerate(crossed):
            rows[first_k + 1 + at, c] = jump_cols[other, came_j[k]] * size

        def ham_row(term):
            parts = [ham[term, c, k].astype(F32) for k in range(layers_h)]
            parts += [ham[term, came_h[k], k].astype(F32).T for k in range(layers_h)]
            return jnp.concatenate(parts, axis=1)

        turned = [jump[came_j[k], k].astype(F32).T.astype(BF16) for k in range(layers_j)]
        jump_row[c] = jnp.concatenate(turned, axis=1)
        square = sum(
            jnp.dot(turned[k], jump[came_j[k], k], preferred_element_type=F32) for k in range(layers_j)
        )
        blocks = [square] + [
            jnp.dot(turned[k], jump[came_j[k], other], preferred_element_type=F32) for k, other in crossed
        ]
        decay = -0.5 * jnp.concatenate(blocks, axis=1)
        drift, steer = ham_row(0), ham_row(1)
        for at in range(len(tables) // 2):
            coeffs = drift + amplitudes[at] * steer
            tables[2 * at][c] = jnp.concatenate([coeffs, decay], axis=1).astype(BF16)
            tables[2 * at + 1][c] = jnp.concatenate([-coeffs, decay], axis=1).astype(BF16)


def operator_tables(ham_blocks, ham_cols, jump_blocks, jump_cols, amplitudes):
    layers_h, count = ham_cols.shape
    layers_j = jump_cols.shape[0]
    size = ham_blocks.shape[-1]
    layers_k = 1 + layers_j * (layers_j - 1)
    smem = pl.BlockSpec(memory_space=pltpu.SMEM)
    vmem = pl.BlockSpec(memory_space=pltpu.VMEM)
    table = jax.ShapeDtypeStruct((count, size, (2 * layers_h + layers_k) * size), BF16)
    number = amplitudes.shape[0]
    rows, jump_row, *tables = pl.pallas_call(
        table_kernel,
        out_shape=[
            jax.ShapeDtypeStruct((2 * layers_h + layers_k + layers_j, count), jnp.int32),
            jax.ShapeDtypeStruct((count, size, layers_j * size), BF16),
        ] + [table] * (2 * number),
        in_specs=[smem, smem, smem, vmem, vmem],
        out_specs=[smem, vmem] + [vmem] * (2 * number),
        compiler_params=pltpu.CompilerParams(vmem_limit_bytes=60 * 2**20),
        cost_estimate=pl.CostEstimate(flops=10**9, bytes_accessed=10 * 2**20, transcendentals=0),
        name="operator_tables",
    )(ham_cols, jump_cols, amplitudes, ham_blocks, jump_blocks)
    return (2 * layers_h, layers_k, layers_j), rows, jump_row, tables[0::2], tables[1::2]


class Step:
    def __init__(self, rows, counts, size, plus, minus, jump):
        self.rows, self.counts, self.size = rows, counts, size
        self.plus, self.minus, self.jump = plus, minus, jump

    def take(self, ref, kind, c, cols):
        first = sum(self.counts[:kind])
        return [
            ref[pl.ds(pl.multiple_of(self.rows[first + k, c], self.size), self.size), cols]
            for k in range(self.counts[kind])
        ]

    def ham(self, table, c, ham_ref, decay_ref, cols):
        met = jnp.concatenate(self.take(ham_ref, 0, c, cols) + self.take(decay_ref, 1, c, cols), axis=0)
        return jnp.dot(table[c], met, preferred_element_type=F32)

    def pull(self, c, ref, cols):
        met = jnp.concatenate(self.take(ref, 2, c, cols), axis=0)
        return jnp.dot(self.jump[c], met, preferred_element_type=F32)


def turned_tile(tile):
    return tile.T


def turn_whole(source, target, tile):
    n = source.shape[0] // tile

    @pl.loop(0, n)
    def _(i):
        near = pl.ds(pl.multiple_of(i * tile, tile), tile)
        for j in range(n):
            far = pl.ds(j * tile, tile)
            target[far, near] = turned_tile(source[near, far])


def turn_whole_in_place(ref, tile):
    n = ref.shape[0] // tile
    for i in range(n):
        near = pl.ds(i * tile, tile)
        ref[near, near] = turned_tile(ref[near, near])

        @pl.loop(i + 1, n)
        def _(j):
            far = pl.ds(pl.multiple_of(j * tile, tile), tile)
            upper = turned_tile(ref[near, far])
            lower = turned_tile(ref[far, near])
            ref[far, near] = upper
            ref[near, far] = lower


def whole_step(step, c_ref, d_ref, r_ref, x_ref, c_new, tile):
    n = c_ref.shape[0]
    count = n // step.size

    @pl.loop(0, count)
    def _(c):
        own = pl.ds(pl.multiple_of(c * step.size, step.size), step.size)
        for s in range(n // tile):
            cols = pl.ds(s * tile, tile)
            r_ref[own, cols] = step.ham(step.minus, c, c_ref, d_ref, cols).astype(BF16)
            x_ref[own, cols] = step.pull(c, d_ref, cols).astype(BF16)

    turn_whole_in_place(r_ref, tile)
    turn_whole_in_place(x_ref, tile)

    @pl.loop(0, count)
    def _(c):
        own = pl.ds(pl.multiple_of(c * step.size, step.size), step.size)
        for s in range(n // tile):
            cols = pl.ds(s * tile, tile)
            change = step.ham(step.plus, c, d_ref, c_ref, cols) + step.pull(c, x_ref, cols)
            change = change + r_ref[own, cols].astype(F32)
            c_new[own, cols] = (c_ref[own, cols].astype(F32) + time_step * change).astype(BF16)

    turn_whole(c_new, r_ref, tile)


def own_step(step, start, width, c_ref, d_ref, flat, turned, tile, base, out):
    n = c_ref.shape[0]
    part = min(tile, width)

    @pl.loop(0, width // step.size)
    def _(t):
        c = start // step.size + t
        for s in range(n // tile):
            cols = pl.ds(s * tile, tile)
            products = (
                step.ham(step.minus, c, c_ref, d_ref, cols),
                step.ham(step.plus, c, d_ref, c_ref, cols),
                step.pull(c, d_ref, cols),
                step.pull(c, c_ref, cols),
            )
            for k, product in enumerate(products):
                flat[pl.ds(pl.multiple_of(k * width + t * step.size, step.size), step.size), cols] = product.astype(BF16)

    @pl.loop(0, n // part)
    def _(i):
        near = pl.ds(pl.multiple_of(i * part, part), part)
        for j in range(4 * width // part):
            far = pl.ds(j * part, part)
            turned[near, far] = turned_tile(flat[far, near])

    @pl.loop(0, n // step.size)
    def _(c):
        own = pl.ds(pl.multiple_of(c * step.size, step.size), step.size)
        for s in range(width // part):
            cols = pl.ds(pl.multiple_of(start + s * part, part), part)
            of = [pl.ds(k * width + s * part, part) for k in range(4)]
            first = step.ham(step.plus, c, d_ref, c_ref, cols) + step.pull(c, turned, of[2])
            second = step.ham(step.minus, c, c_ref, d_ref, cols) + step.pull(c, turned, of[3])
            first = first + turned[own, of[0]].astype(F32)
            second = second + turned[own, of[1]].astype(F32)
            real, imag = base(own, cols, pl.ds(s * part, part))
            out[0, 0, own, pl.ds(s * part, part)] = (real + 0.5 * time_step * (first + second)).astype(BF16)
            out[0, 1, own, pl.ds(s * part, part)] = (imag + 0.5 * time_step * (first - second)).astype(BF16)


def inner_kernel(counts, tile, rows, place, c_hbm, terminal, plus, minus, jump, out, c_ref, d_ref, flat, turned, sem):
    load = pltpu.make_async_copy(c_hbm, c_ref, sem)
    load.start()
    load.wait()
    turn_whole(c_ref, d_ref, tile)
    step = Step(rows, counts, plus.shape[1], plus, minus, jump)

    def base(own, _, cols):
        return terminal[0, 0, own, cols].astype(F32), terminal[0, 1, own, cols].astype(F32)

    own_step(step, place[0], out.shape[3], c_ref, d_ref, flat, turned, tile, base, out)


def start_kernel(
    counts, tile, rows, place, c_hbm, terminal, plus_one, minus_one, plus_two, minus_two, jump, out,
    c_ref, d_ref, r_ref, x_ref, c_new, sem,
):
    @pl.when(place[1] == 1)
    def _():
        keep = pltpu.make_async_copy(terminal, out, sem)
        keep.start()
        keep.wait()

    @pl.when(place[1] == 0)
    def _():
        load = pltpu.make_async_copy(c_hbm, c_ref, sem)
        load.start()
        load.wait()
        turn_whole(c_ref, d_ref, tile)
        size = plus_one.shape[1]
        whole_step(Step(rows, counts, size, plus_one, minus_one, jump), c_ref, d_ref, r_ref, x_ref, c_new, tile)

        def base(own, cols, _):
            first, second = c_new[own, cols].astype(F32), r_ref[own, cols].astype(F32)
            return 0.5 * (first + second), 0.5 * (first - second)

        step = Step(rows, counts, size, plus_two, minus_two, jump)
        own_step(step, place[0], out.shape[3], c_new, r_ref, x_ref, c_ref, tile, base, out)


def on_device(terminal, controls, ham_blocks, ham_cols, jump_blocks, jump_cols):
    n, width = terminal.shape[2], terminal.shape[3]
    tile = 256
    mixed = (terminal[0, 0].astype(F32) + terminal[0, 1].astype(F32)).astype(BF16)
    mixed_next = shifted_down(mixed, "tm")
    controls_next = shifted_down(controls, "tm")
    whole = lax.all_gather(mixed, "row", axis=1, tiled=True)
    whole_next = lax.all_gather(mixed_next, "row", axis=1, tiled=True)

    amplitudes = jnp.stack([controls[0, 1], controls_next[0, 1], controls_next[0, 0]])
    counts, rows, jump_row, plus, minus = operator_tables(ham_blocks, ham_cols, jump_blocks, jump_cols, amplitudes)
    is_last = lax.axis_index("tm") == lax.axis_size("tm") - 1
    place = jnp.stack([lax.axis_index("row") * width, is_last.astype(jnp.int32)]).astype(jnp.int32)

    smem = pl.BlockSpec(memory_space=pltpu.SMEM)
    vmem = pl.BlockSpec(memory_space=pltpu.VMEM)
    anywhere = pl.BlockSpec(memory_space=pl.ANY)
    square = pltpu.VMEM((n, n), BF16)
    params = pltpu.CompilerParams(vmem_limit_bytes=60 * 2**20)
    out_shape = jax.ShapeDtypeStruct(terminal.shape, BF16)
    new_fpoint = pl.pallas_call(
        functools.partial(inner_kernel, counts, tile),
        out_shape=out_shape,
        in_specs=[smem, smem, anywhere, vmem, vmem, vmem, vmem],
        out_specs=vmem,
        scratch_shapes=[square, square, pltpu.VMEM((4 * width, n), BF16), pltpu.VMEM((n, 4 * width), BF16), pltpu.SemaphoreType.DMA],
        compiler_params=params,
        cost_estimate=pl.CostEstimate(flops=2 * 10**10, bytes_accessed=16 * 2**20, transcendentals=0),
        name="inner_point",
    )(rows, place, whole, terminal, plus[0], minus[0], jump_row)
    new_cpoint = pl.pallas_call(
        functools.partial(start_kernel, counts, tile),
        out_shape=out_shape,
        in_specs=[smem, smem, anywhere, anywhere, vmem, vmem, vmem, vmem, vmem],
        out_specs=vmem,
        scratch_shapes=[square] * 5 + [pltpu.SemaphoreType.DMA],
        compiler_params=params,
        cost_estimate=pl.CostEstimate(flops=6 * 10**10, bytes_accessed=16 * 2**20, transcendentals=0),
        name="left_end",
    )(rows, place, whole_next, terminal, plus[1], minus[1], plus[2], minus[2], jump_row)
    return (new_cpoint, new_fpoint)


def solution(mesh):
    in_specs = (P(("grp", "tm"), None, None, "row"), P(("grp", "tm"), None), P(), P(), P(), P())
    out_specs = (P(("grp", "tm"), None, None, "row"), P(("grp", "tm"), None, None, "row"))
    return jax.shard_map(
        on_device, mesh=mesh, in_specs=in_specs, out_specs=out_specs, check_vma=False
    )
```

profile of v0, /device:TPU:0, one launch (start us, length us, event | category | flops | bytes accessed | tf_op | source)
XLA Modules:
  0.0 227.8 jit_solution(7349394796447094283)
XLA Ops:
  7.2 0.0 all-gather.6.cloned.1.call-start
  7.2 4.1 %add_convert_fusion = bf16[1,1,2048,512]{3,2,1,0:T(8,128)(2,1)} fusion(bf16[1,2,2048,512]{3,2,1,0:T(8,128)(2,1)} %terminal.3), kind=kLoop, calls=%fused_computation | loop fusion | flops 4194304 | bytes 6291456 | tf_op jit(solution)/shard_map/convert_element_type | solution.py:250
  11.3 0.0 all-gather.6.cloned.1.call-update
  11.4 0.0 copy-start.2
  11.4 0.0 copy-start.1
  11.4 0.0 all-gather.4.cloned.1.call-start
  11.4 2.9 %fusion.1 = bf16[2048,512]{1,0:T(8,128)(2,1)S(1)} fusion(bf16[1,2,2048,512]{3,2,1,0:T(8,128)(2,1)} %terminal.3), kind=kLoop, calls=%fused_computation.4 | loop fusion | flops 4194304 | bytes 6291456 | tf_op jit(solution)/shard_map/convert_element_type | solution.py:250
  14.3 1.3 collective-permute-start.1
  15.6 49.3 %collective-permute-done.1 = bf16[2048,512]{1,0:T(8,128)(2,1)S(1)} collective-permute-done((bf16[2048,512]{1,0:T(8,128)(2,1)S(1)}, bf16[2048,512]{1,0:T(8,128)(2,1)S(1)}, u32[]{:S(2)}, u32[]{:S(2)}) %collective-permute-start.1) | collective-permute-done | bytes 2097184 | tf_op jit(solution)/shard_map/ppermute | solution.py:17
  64.9 0.0 copy-start
  64.9 1.3 copy-done
  66.2 0.0 all-gather.4.cloned.1.call-update
  66.2 0.0 copy-done.2
  66.2 1.3 collective-permute-start
  67.5 0.7 slice.15
  68.2 0.0 copy-done.1
  68.2 3.9 %copy.8.ham = bf16[2,64,2,32,32]{4,3,2,1,0:T(8,128)(2,1)} copy(bf16[2,64,2,32,32]{1,4,3,2,0:T(8,128)(2,1)S(1)} %copy-done.1) | data formatting | bytes 1048576 | tf_op args[2]
  72.1 3.4 %copy.9.jump = bf16[64,2,32,32]{3,2,1,0:T(8,128)(2,1)} copy(bf16[64,2,32,32]{0,3,2,1:T(8,128)(2,1)} %param.10) | data formatting | bytes 524288 | tf_op args[4]
  75.5 0.7 pad_add_fusion.place
  76.2 0.0 collective-permute-done
  76.2 0.6 fusion
  76.8 2.5 %pad_maximum_fusion.amplitudes = f32[3]{0:T(128)} fusion(f32[1]{0:T(128)} %bitcast.2, f32[1]{0:T(128)} %bitcast.1, f32[1]{0:T(128)} %bitcast), kind=kLoop, calls=%fused_computation.1 | loop fusion | flops 6 | bytes 24 | tf_op jit(solution)/shard_map/stack | solution.py:256
  79.4 17.2 %operator_tables.1 = (s32[9,64]{1,0:T(8,128)}, bf16[64,32,64]{2,1,0:T(8,128)(2,1)}, bf16[64,32,224]{2,1,0:T(8,128)(2,1)}, bf16[64,32,224]{2,1,0:T(8,128)(2,1)}, ...) custom-call(s32[2,64]{1,0:T(2,128)} %ham_cols.1, ...), custom_call_target="tpu_custom_call" | custom-call | flops 1000000000 | bytes 10485760 | tf_op jit(solution)/shard_map/operator_tables/pallas_call | solution.py:74
  96.6 0.0 all-gather.6.cloned.1.call-done
  96.6 37.0 %inner_point.1 = bf16[1,2,2048,512]{3,2,1,0:T(8,128)(2,1)} custom-call(s32[9,64]{1,0:T(8,128)} %get-tuple-element.10.rows, s32[2]{0:T(128)} %pad_add_fusion.place, bf16[2048,2048]{1,0:T(8,128)(2,1)} %bitcast.8, bf16[1,2,2048,512]{3,2,1,0:T(8,128)(2,1)} %terminal.3, bf16[64,32,224]{2,1,0:T(8,128)(2,1)} %get-tuple-element.16.plus, ...), custom_call_target="tpu_custom_call" | custom-call | flops 20000000000 | bytes 16777216 | tf_op jit(solution)/shard_map/inner_point/pallas_call | solution.py:267
  133.6 0.0 all-gather.4.cloned.1.call-done.c_hbm
  133.6 87.3 %left_end.1 = bf16[1,2,2048,512]{3,2,1,0:T(8,128)(2,1)} custom-call(s32[9,64]{1,0:T(8,128)} %get-tuple-element.10.rows, s32[2]{0:T(128)} %pad_add_fusion.place, bf16[2048,2048]{1,0:T(8,128)(2,1)} %all-gather.4.cloned.1.call-done.c_hbm, bf16[1,2,2048,512]{3,2,1,0:T(8,128)(2,1)} %terminal.3, bf16[64,32,224]{2,1,0:T(8,128)(2,1)} %get-tuple-element.11.plus_one, ...), custom_call_target="tpu_custom_call" | custom-call | flops 60000002048 | bytes 16777216 | tf_op jit(solution)/shard_map/left_end/pallas_call | solution.py:277
Async XLA Ops:
  7.2 89.4 %all-gather.6.cloned.1.call-start = ((), (), s32[]{:S(2)}) async-start(), calls=%async_computation.1 | async-start | bytes 10485760 | tf_op jit(solution)/shard_map/all_gather | solution.py:253
  11.4 54.9 %copy-start.2 = (f32[1,2]{1,0:T(1,128)S(1)}, f32[1,2]{1,0:T(1,128)}, u32[]{:S(2)}) copy-start(f32[1,2]{1,0:T(1,128)} %param.7) | copy-start | bytes 28
  11.4 56.8 %copy-start.1 = (bf16[2,64,2,32,32]{1,4,3,2,0:T(8,128)(2,1)S(1)}, bf16[2,64,2,32,32]{1,4,3,2,0:T(8,128)(2,1)}, u32[]{:S(2)}) copy-start(bf16[2,64,2,32,32]{1,4,3,2,0:T(8,128)(2,1)} %param.8) | copy-start | bytes 1572868
  11.4 122.2 %all-gather.4.cloned.1.call-start = ((), (), s32[]{:S(2)}) async-start(), calls=%async_computation | async-start | bytes 10485760 | tf_op jit(solution)/shard_map/all_gather | solution.py:254
  14.3 50.6 %collective-permute-start.1 = (bf16[2048,512]{1,0:T(8,128)(2,1)S(1)}, bf16[2048,512]{1,0:T(8,128)(2,1)S(1)}, u32[]{:S(2)}, u32[]{:S(2)}) collective-permute-start(bf16[2048,512]{1,0:T(8,128)(2,1)S(1)} %fusion.1), channel_id=1, source_target_pairs={{4,0},{8,4},{12,8},{5,1},{9,5},{13,9},{6,2},{10,6},{14,10},{7,3},{... | collective-permute-start | bytes 6291464 | tf_op jit(solution)/shard_map/ppermute | solution.py:17
  64.9 1.3 copy-start
  66.2 9.9 %collective-permute-start = (f32[1,2]{1,0:T(1,128)S(1)}, f32[1,2]{1,0:T(1,128)S(1)}, u32[]{:S(2)}, u32[]{:S(2)}) collective-permute-start(f32[1,2]{1,0:T(1,128)S(1)} %copy-done.2), channel_id=1, source_target_pairs={{4,0},{8,4},{12,8},{5,1},{9,5},{13,9},{6,2},{10,6},{14,10},{7,3},{... | collective-permute-start | bytes 32 | tf_op jit(solution)/shard_map/ppermute | solution.py:17
Sparse Core Ops, SparseCore 0:
  11.5 60.9 all-gather.5
  74.6 58.2 all-gather.3
where the time goes:
time: 228 us
  Pallas kernels  141 us (62%)
  waiting for transfers between devices  49.3 us (22%)
  between operations  14.1 us (6%)
  other arithmetic  10.2 us (4%)
  local copies, waits for them, and re-layouts  9.91 us (4%)
  starting transfers between devices  2.66 us (1%)
    pallas_call x1, Pallas kernels, on_device(): pl.pallas_call(functools.partial(start_kernel, counts, tile), out_shape=o...  87.3 us
    ppermute x2, waiting for transfers between devices, shifted_down(): return lax.ppermute(block, axis, route)  49.3 us
    pallas_call x1, Pallas kernels, on_device(): pl.pallas_call(functools.partial(inner_kernel, counts, tile), out_shape=o...  37 us
    pallas_call x1, Pallas kernels, operator_tables(): pl.pallas_call(table_kernel, out_shape=[jax.ShapeDtypeStruct((2 * layers_...  17.2 us
    unnamed x8, local copies, waits for them, and re-layouts  8.63 us
    convert_element_type x2, other arithmetic, on_device(): (terminal[0, 0].astype(F32) + terminal[0, 1].astype(F32)).astype(BF16)  7.03 us
  transfers between devices with their start and end apart: 4, of which 1 were waited for; matrix products, arithmetic and copies ran while one was open for 6% of the time, Pallas kernels for 24%

commit v1 on v0

--- a/solution.py
+++ b/solution.py
@@ -122,46 +122,46 @@
             target[far, near] = turned_tile(source[near, far])
 
 
-def turn_whole_in_place(ref, tile):
-    n = ref.shape[0] // tile
-    for i in range(n):
-        near = pl.ds(i * tile, tile)
-        ref[near, near] = turned_tile(ref[near, near])
-
-        @pl.loop(i + 1, n)
-        def _(j):
-            far = pl.ds(pl.multiple_of(j * tile, tile), tile)
-            upper = turned_tile(ref[near, far])
-            lower = turned_tile(ref[far, near])
-            ref[far, near] = upper
-            ref[near, far] = lower
-
-
-def whole_step(step, c_ref, d_ref, r_ref, x_ref, c_new, tile):
-    n = c_ref.shape[0]
-    count = n // step.size
-
-    @pl.loop(0, count)
-    def _(c):
-        own = pl.ds(pl.multiple_of(c * step.size, step.size), step.size)
-        for s in range(n // tile):
-            cols = pl.ds(s * tile, tile)
-            r_ref[own, cols] = step.ham(step.minus, c, c_ref, d_ref, cols).astype(BF16)
-            x_ref[own, cols] = step.pull(c, d_ref, cols).astype(BF16)
-
-    turn_whole_in_place(r_ref, tile)
-    turn_whole_in_place(x_ref, tile)
-
-    @pl.loop(0, count)
-    def _(c):
-        own = pl.ds(pl.multiple_of(c * step.size, step.size), step.size)
-        for s in range(n // tile):
-            cols = pl.ds(s * tile, tile)
-            change = step.ham(step.plus, c, d_ref, c_ref, cols) + step.pull(c, x_ref, cols)
-            change = change + r_ref[own, cols].astype(F32)
-            c_new[own, cols] = (c_ref[own, cols].astype(F32) + time_step * change).astype(BF16)
-
-    turn_whole(c_new, r_ref, tile)
+def assemble(place, near, near_pair, far, far_pair, c_ref, d_ref, stage, sems, tile):
+    half, width = far.shape
+    here, there = place[2], half - place[2]
+    own, pair = place[3], width - place[3]
+    chip_rows, other_rows = (pl.ds(pl.multiple_of(first, half), half) for first in (here, there))
+
+    def cols(first):
+        return pl.ds(pl.multiple_of(first, width), width)
+
+    copies = [
+        (near.at[0], c_ref.at[chip_rows, cols(here + own)]),
+        (near_pair.at[0], c_ref.at[chip_rows, cols(here + pair)]),
+        (far, c_ref.at[other_rows, cols(there + own)]),
+        (far_pair, c_ref.at[other_rows, cols(there + pair)]),
+    ]
+    for k in range(2):
+        copies.append((near.at[1 + k], stage.at[pl.ds(k * half, half), cols(own)]))
+        copies.append((near_pair.at[1 + k], stage.at[pl.ds(k * half, half), cols(pair)]))
+    copies = [pltpu.make_async_copy(a, b, sems.at[k]) for k, (a, b) in enumerate(copies)]
+    for copy in copies:
+        copy.start()
+    for copy in copies:
+        copy.wait()
+
+    def part(first, k):
+        return pl.ds(pl.multiple_of(first + k * tile, tile), tile)
+
+    @pl.loop(0, half // tile)
+    def _(i):
+        for first in (0, half):
+            for j in range(half // tile):
+                d_ref[part(first, j), part(first, i)] = c_ref[part(first, i), part(first, j)].T
+        for j in range(half // tile):
+            real = stage[part(0, i), part(0, j)].astype(F32)
+            imag = stage[part(half, i), part(0, j)].astype(F32)
+            total, less = (real + imag).astype(BF16), (real - imag).astype(BF16)
+            c_ref[part(there, i), part(here, j)] = total
+            d_ref[part(there, i), part(here, j)] = less
+            c_ref[part(here, j), part(there, i)] = less.T
+            d_ref[part(here, j), part(there, i)] = total.T
 
 
 def own_step(step, start, width, c_ref, d_ref, flat, turned, tile, base, out):
@@ -204,86 +204,110 @@
             out[0, 1, own, pl.ds(s * part, part)] = (imag + 0.5 * time_step * (first - second)).astype(BF16)
 
 
-def inner_kernel(counts, tile, rows, place, c_hbm, terminal, plus, minus, jump, out, c_ref, d_ref, flat, turned, sem):
-    load = pltpu.make_async_copy(c_hbm, c_ref, sem)
-    load.start()
-    load.wait()
-    turn_whole(c_ref, d_ref, tile)
-    step = Step(rows, counts, plus.shape[1], plus, minus, jump)
-
-    def base(own, _, cols):
-        return terminal[0, 0, own, cols].astype(F32), terminal[0, 1, own, cols].astype(F32)
-
-    own_step(step, place[0], out.shape[3], c_ref, d_ref, flat, turned, tile, base, out)
-
-
-def start_kernel(
-    counts, tile, rows, place, c_hbm, terminal, plus_one, minus_one, plus_two, minus_two, jump, out,
-    c_ref, d_ref, r_ref, x_ref, c_new, sem,
-):
-    @pl.when(place[1] == 1)
-    def _():
-        keep = pltpu.make_async_copy(terminal, out, sem)
-        keep.start()
-        keep.wait()
-
-    @pl.when(place[1] == 0)
-    def _():
-        load = pltpu.make_async_copy(c_hbm, c_ref, sem)
+def fill(place, pieces, c_ref, d_ref, flat, sems, tile):
+    if len(pieces) == 1:
+        load = pltpu.make_async_copy(pieces[0], c_ref, sems.at[0])
         load.start()
         load.wait()
         turn_whole(c_ref, d_ref, tile)
-        size = plus_one.shape[1]
-        whole_step(Step(rows, counts, size, plus_one, minus_one, jump), c_ref, d_ref, r_ref, x_ref, c_new, tile)
+    else:
+        assemble(place, *pieces, c_ref, d_ref, flat, sems, tile)
+
+
+def inner_kernel(counts, tile, rows, place, terminal, plus, minus, jump, *refs):
+    *pieces, out, c_ref, d_ref, flat, turned, sems = refs
+    fill(place, pieces, c_ref, d_ref, flat, sems, tile)
+    step = Step(rows, counts, plus.shape[1], plus, minus, jump)
+
+    def base(own, _, cols):
+        return terminal[0, 0, own, cols].astype(F32), terminal[0, 1, own, cols].astype(F32)
+
+    own_step(step, place[0], out.shape[3], c_ref, d_ref, flat, turned, tile, base, out)
+
+
+def start_kernel(counts, tile, rows, place, terminal, plus, minus, jump, *refs):
+    *pieces, out, c_ref, d_ref, flat, turned, sems = refs
+
+    @pl.when(place[1] == 1)
+    def _():
+        keep = pltpu.make_async_copy(terminal, out, sems.at[0])
+        keep.start()
+        keep.wait()
+
+    @pl.when(place[1] == 0)
+    def _():
+        fill(place, pieces, c_ref, d_ref, flat, sems, tile)
+        step = Step(rows, counts, plus.shape[1], plus, minus, jump)
 
         def base(own, cols, _):
-            first, second = c_new[own, cols].astype(F32), r_ref[own, cols].astype(F32)
+            first, second = c_ref[own, cols].astype(F32), d_ref[own, cols].astype(F32)
             return 0.5 * (first + second), 0.5 * (first - second)
 
-        step = Step(rows, counts, size, plus_two, minus_two, jump)
-        own_step(step, place[0], out.shape[3], c_new, r_ref, x_ref, c_ref, tile, base, out)
+        own_step(step, place[0], out.shape[3], c_ref, d_ref, flat, turned, tile, base, out)
+
+
+def swapped(block, bit):
+    return lax.ppermute(block, "row", [(i, i ^ bit) for i in range(lax.axis_size("row"))])
 
 
 def on_device(terminal, controls, ham_blocks, ham_cols, jump_blocks, jump_cols):
     n, width = terminal.shape[2], terminal.shape[3]
     tile = 256
-    mixed = (terminal[0, 0].astype(F32) + terminal[0, 1].astype(F32)).astype(BF16)
-    mixed_next = shifted_down(mixed, "tm")
+    two_chips = lax.axis_size("row") == 4
+    row = lax.axis_index("row")
+    here = row // 2 * 2 * width
     controls_next = shifted_down(controls, "tm")
-    whole = lax.all_gather(mixed, "row", axis=1, tiled=True)
-    whole_next = lax.all_gather(mixed_next, "row", axis=1, tiled=True)
-
-    amplitudes = jnp.stack([controls[0, 1], controls_next[0, 1], controls_next[0, 0]])
+    is_last = lax.axis_index("tm") == lax.axis_size("tm") - 1
+    place = jnp.stack([row * width, is_last.astype(jnp.int32), here, row % 2 * width]).astype(jnp.int32)
+    amplitudes = jnp.stack([controls[0, 1], controls_next[0, 0]])
     counts, rows, jump_row, plus, minus = operator_tables(ham_blocks, ham_cols, jump_blocks, jump_cols, amplitudes)
-    is_last = lax.axis_index("tm") == lax.axis_size("tm") - 1
-    place = jnp.stack([lax.axis_index("row") * width, is_last.astype(jnp.int32)]).astype(jnp.int32)
+
+    def packed(state):
+        mine = lax.dynamic_slice_in_dim(state[0], here, 2 * width, 1).astype(F32)
+        rest = lax.dynamic_slice_in_dim(state[0], 2 * width - here, 2 * width, 1)
+        return (mine[0] + mine[1]).astype(BF16)[None], rest
+
+    def gathered(mixed, rest):
+        near = jnp.concatenate([mixed, rest], axis=0)
+        far = swapped(mixed[0], 2)
+        return [near, swapped(near, 1), far, swapped(far, 1)]
+
+    def whole(state):
+        return (state[0, 0].astype(F32) + state[0, 1].astype(F32)).astype(BF16)
 
     smem = pl.BlockSpec(memory_space=pltpu.SMEM)
     vmem = pl.BlockSpec(memory_space=pltpu.VMEM)
     anywhere = pl.BlockSpec(memory_space=pl.ANY)
-    square = pltpu.VMEM((n, n), BF16)
-    params = pltpu.CompilerParams(vmem_limit_bytes=60 * 2**20)
-    out_shape = jax.ShapeDtypeStruct(terminal.shape, BF16)
-    new_fpoint = pl.pallas_call(
-        functools.partial(inner_kernel, counts, tile),
-        out_shape=out_shape,
-        in_specs=[smem, smem, anywhere, vmem, vmem, vmem, vmem],
-        out_specs=vmem,
-        scratch_shapes=[square, square, pltpu.VMEM((4 * width, n), BF16), pltpu.VMEM((n, 4 * width), BF16), pltpu.SemaphoreType.DMA],
-        compiler_params=params,
-        cost_estimate=pl.CostEstimate(flops=2 * 10**10, bytes_accessed=16 * 2**20, transcendentals=0),
-        name="inner_point",
-    )(rows, place, whole, terminal, plus[0], minus[0], jump_row)
-    new_cpoint = pl.pallas_call(
-        functools.partial(start_kernel, counts, tile),
-        out_shape=out_shape,
-        in_specs=[smem, smem, anywhere, anywhere, vmem, vmem, vmem, vmem, vmem],
-        out_specs=vmem,
-        scratch_shapes=[square] * 5 + [pltpu.SemaphoreType.DMA],
-        compiler_params=params,
-        cost_estimate=pl.CostEstimate(flops=6 * 10**10, bytes_accessed=16 * 2**20, transcendentals=0),
-        name="left_end",
-    )(rows, place, whole_next, terminal, plus[1], minus[1], plus[2], minus[2], jump_row)
+
+    def step_call(kernel, name, state_spec, k, pieces):
+        return pl.pallas_call(
+            functools.partial(kernel, counts, tile),
+            out_shape=jax.ShapeDtypeStruct(terminal.shape, BF16),
+            in_specs=[smem, smem, state_spec, vmem, vmem, vmem] + [anywhere] * len(pieces),
+            out_specs=vmem,
+            scratch_shapes=[
+                pltpu.VMEM((n, n), BF16),
+                pltpu.VMEM((n, n), BF16),
+                pltpu.VMEM((4 * width, n), BF16),
+                pltpu.VMEM((n, 4 * width), BF16),
+                pltpu.SemaphoreType.DMA((8,)),
+            ],
+            compiler_params=pltpu.CompilerParams(vmem_limit_bytes=60 * 2**20),
+            cost_estimate=pl.CostEstimate(flops=2 * 10**10, bytes_accessed=16 * 2**20, transcendentals=0),
+            name=name,
+        )(rows, place, terminal, plus[k], minus[k], jump_row, *pieces)
+
+    if two_chips:
+        pieces = gathered(*packed(terminal))
+    else:
+        pieces = [lax.all_gather(whole(terminal), "row", axis=1, tiled=True)]
+    new_fpoint = step_call(inner_kernel, "inner_point", vmem, 0, pieces)
+    if two_chips:
+        mixed, rest = packed(new_fpoint)
+        pieces = gathered(shifted_down(mixed, "tm"), shifted_down(rest, "tm"))
+    else:
+        pieces = [lax.all_gather(shifted_down(whole(new_fpoint), "tm"), "row", axis=1, tiled=True)]
+    new_cpoint = step_call(start_kernel, "left_end", anywhere, 1, pieces)
     return (new_cpoint, new_fpoint)
 
 

time: 228 us -> 241 us (1.057)
  waiting for transfers between devices: 49.3 us -> 121 us
  Pallas kernels: 141 us -> 90.2 us
  between operations: 14.1 us -> 0.82 us
  starting transfers between devices: 2.66 us -> 8.73 us
    ppermute x0 -> x6, waiting for transfers between devices: none -> 50.5 us  [swapped(): lax.ppermute(block, 'row', [(i, i ^ bit) for i in range(lax.axis_size('ro...]
    pallas_call x2, Pallas kernels: 124 us -> 74.2 us  [step_call(): pl.pallas_call(functools.partial(kernel, counts, tile), out_shape=jax.Sha...]
    ppermute x2 -> x3, waiting for transfers between devices: 49.3 us -> 70.3 us  [shifted_down(): return lax.ppermute(block, axis, route)]
    ppermute x0 -> x6, starting transfers between devices: none -> 4.87 us  [swapped(): lax.ppermute(block, 'row', [(i, i ^ bit) for i in range(lax.axis_size('ro...]
    convert_element_type x2 -> x4, other arithmetic: 7.03 us -> 3.98 us  [the longest x1 2.92 us: packed(): mine = lax.dynamic_slice_in_dim(state[0], here, 2 * width, 1).astype(F32)]
    dynamic_slice x0 -> x1, other arithmetic: none -> 2.92 us  [packed(): rest = lax.dynamic_slice_in_dim(state[0], 2 * width - here, 2 * width, 1)]
    unnamed x8 -> x15, local copies, waits for them, and re-layouts: 8.63 us -> 10.4 us
  transfers between devices with their start and end apart: 4 -> 9, of which waited for: 1 -> 4; matrix products, arithmetic and copies ran while one was open for 6% -> 5% of each run, Pallas kernels for 24% -> 7%
where the time goes in v1:
time: 241 us
  waiting for transfers between devices  121 us (50%)
  Pallas kernels  90.2 us (37%)
  local copies, waits for them, and re-layouts  11.1 us (5%)
  other arithmetic  9 us (4%)
  starting transfers between devices  8.73 us (4%)
    pallas_call x2, Pallas kernels, step_call(): pl.pallas_call(functools.partial(kernel, counts, tile), out_shape=jax.Sha...  74.2 us
    ppermute x3, waiting for transfers between devices, shifted_down(): return lax.ppermute(block, axis, route)  70.3 us
    ppermute x6, waiting for transfers between devices, swapped(): lax.ppermute(block, 'row', [(i, i ^ bit) for i in range(lax.axis_size('ro...  50.5 us
    pallas_call x1, Pallas kernels, operator_tables(): pl.pallas_call(table_kernel, out_shape=[jax.ShapeDtypeStruct((2 * layers_...  16 us
    unnamed x15, local copies, waits for them, and re-layouts  10.4 us
    ppermute x6, starting transfers between devices, swapped(): lax.ppermute(block, 'row', [(i, i ^ bit) for i in range(lax.axis_size('ro...  4.87 us
  transfers between devices with their start and end apart: 9, of which 4 were waited for; matrix products, arithmetic and copies ran while one was open for 5% of the time, Pallas kernels for 7%

profile of v1, /device:TPU:0, one launch (start us, length us, event | category | flops | bytes accessed | tf_op | source)
XLA Modules:
  0.0 240.7 jit_solution(7544382224171413432)
XLA Ops:
  0.7 2.9 %dynamic-slice_convert_fusion.1 = (f32[1,2,1024,512]{3,2,1,0:T(8,128)S(1)}, bf16[2,1024,512]{2,1,0:T(8,128)(2,1)S(1)}) fusion(bf16[1,2,2048,512]{3,2,1,0:T(8,128)(2,1)} %terminal.3, s32[]{:T(128)S(6)} %select_n.21, s32[]{:T(128)S(6)} %select_n.22), kind=kLoop, calls=%fused_computation.8 | loop fusion | flops 1048576 | bytes 10485768 | tf_op jit(solution)/shard_map/convert_element_type | solution.py:266
  3.6 0.4 fusion.4
  3.9 0.3 pad_maximum_fusion.refs_0_
  4.2 0.0 copy-start
  4.2 0.0 copy-start.5
  4.2 0.5 collective-permute-start.1
  4.8 0.4 fusion.3
  5.1 2.6 %collective-permute-start.2 = (bf16[1024,512]{1,0:T(8,128)(2,1)S(1)}, bf16[1024,512]{1,0:T(8,128)(2,1)}, u32[]{:S(2)}, u32[]{:S(2)}) collective-permute-start(bf16[1024,512]{1,0:T(8,128)(2,1)S(1)} %fusion.3), channel_id=1, source_target_pairs={{0,2},{1,3},{2,0},{3,1},{4,6},{5,7},{6,4},{7,5},{8,10},{9,11},{10,... | collective-permute-start | bytes 3145736 | tf_op jit(solution)/shard_map/ppermute | solution.py:250
  7.7 23.9 %collective-permute-done.2.refs_2_ = bf16[1024,512]{1,0:T(8,128)(2,1)} collective-permute-done((bf16[1024,512]{1,0:T(8,128)(2,1)S(1)}, bf16[1024,512]{1,0:T(8,128)(2,1)}, u32[]{:S(2)}, u32[]{:S(2)}) %collective-permute-start.2) | collective-permute-done | bytes 1048608 | tf_op jit(solution)/shard_map/ppermute | solution.py:250
  31.6 0.0 collective-permute-start.3
  31.6 0.0 copy-done.5
  31.6 1.3 collective-permute-start
  32.9 0.6 slice.22
  33.5 3.5 %copy.9.jump = bf16[64,2,32,32]{3,2,1,0:T(8,128)(2,1)} copy(bf16[64,2,32,32]{0,3,2,1:T(8,128)(2,1)} %param.10) | data formatting | bytes 524288 | tf_op args[4]
  37.0 0.0 copy-done
  37.0 4.8 %copy.8.ham = bf16[2,64,2,32,32]{4,3,2,1,0:T(8,128)(2,1)} copy(bf16[2,64,2,32,32]{1,4,3,2,0:T(8,128)(2,1)} %param.8) | data formatting | bytes 1048576 | tf_op args[2]
  41.8 0.6 pad_add_fusion.place
  42.4 0.0 collective-permute-done
  42.4 1.2 pad_maximum_fusion.1.amplitudes
  43.6 16.0 %operator_tables.1 = (s32[9,64]{1,0:T(8,128)}, bf16[64,32,64]{2,1,0:T(8,128)(2,1)}, bf16[64,32,224]{2,1,0:T(8,128)(2,1)}, bf16[64,32,224]{2,1,0:T(8,128)(2,1)}, ...) custom-call(s32[2,64]{1,0:T(2,128)} %ham_cols.1, s32[2,64]{1,0:T(2,128)} %jump_cols.1, ...), custom_call_target="tpu_custom_call" | custom-call | flops 1000000000 | bytes 10485760 | tf_op jit(solution)/shard_map/operator_tables/pallas_call | solution.py:74
  59.6 0.0 collective-permute-done.3.refs_3_
  59.6 0.0 collective-permute-done.1.refs_1_
  59.6 37.7 %inner_point.1 = bf16[1,2,2048,512]{3,2,1,0:T(8,128)(2,1)} custom-call(s32[9,64]{1,0:T(8,128)} %get-tuple-element.8.rows, s32[4]{0:T(128)} %pad_add_fusion.place, bf16[1,2,2048,512]{3,2,1,0:T(8,128)(2,1)} %terminal.3, bf16[64,32,224]{2,1,0:T(8,128)(2,1)} %get-tuple-element.12.plus, bf16[64,32,224]{2,1,0:T(8,128)(2,1)} %get-tuple-element.13.minus, ...), custom_call_target="tpu_custom_call" | custom-call | flops 20000000000 | bytes 16777216 | tf_op jit(solution)/shard_map/inner_point/pallas_call | solution.py:283
  97.4 2.9 %dynamic-slice_bitcast_fusion = (bf16[2,1024,512]{2,1,0:T(8,128)(2,1)S(1)}, f32[1,2,1024,512]{3,2,1,0:T(8,128)S(1)}) fusion(bf16[1,2,2048,512]{3,2,1,0:T(8,128)(2,1)} %inner_point.1, s32[]{:T(128)S(6)} %select_n.22, s32[]{:T(128)S(6)} %select_n.21), kind=kLoop, calls=%fused_computation.5 | loop fusion | flops 1048576 | bytes 10485768 | tf_op jit(solution)/shard_map/dynamic_slice | solution.py:267
  100.3 1.3 collective-permute-start.5
  101.6 0.4 fusion.2
  102.0 1.3 collective-permute-start.4
  103.3 70.3 %collective-permute-done.4 = bf16[1,1024,512]{2,1,0:T(8,128)(2,1)S(1)} collective-permute-done((bf16[1,1024,512]{2,1,0:T(8,128)(2,1)S(1)}, bf16[1,1024,512]{2,1,0:T(8,128)(2,1)S(1)}, u32[]{:S(2)}, u32[]{:S(2)}) %collective-permute-start.4) | collective-permute-done | bytes 1048608 | tf_op jit(solution)/shard_map/ppermute | solution.py:17
  173.6 0.1 constant_dynamic-update-slice_fusion.1
  173.6 0.0 collective-permute-done.5
  173.6 0.1 constant_dynamic-update-slice_fusion.refs_0_
  173.8 0.0 copy-start.1
  173.8 0.1 collective-permute-start.6
  173.9 1.7 collective-permute-start.7
  175.6 23.9 %collective-permute-done.7.refs_2_ = bf16[1024,512]{1,0:T(8,128)(2,1)S(1)} collective-permute-done((bf16[1024,512]{1,0:T(8,128)(2,1)S(1)}, bf16[1024,512]{1,0:T(8,128)(2,1)S(1)}, u32[]{:S(2)}, u32[]{:S(2)}) %collective-permute-start.7) | collective-permute-done | bytes 1048608 | tf_op jit(solution)/shard_map/ppermute | solution.py:250
  199.4 0.0 copy-start.3
  199.5 0.0 collective-permute-start.8
  199.5 2.7 %collective-permute-done.8.refs_3_ = bf16[1024,512]{1,0:T(8,128)(2,1)S(1)} collective-permute-done((bf16[1024,512]{1,0:T(8,128)(2,1)S(1)}, bf16[1024,512]{1,0:T(8,128)(2,1)S(1)}, u32[]{:S(2)}, u32[]{:S(2)}) %collective-permute-start.8) | collective-permute-done | bytes 1048608 | tf_op jit(solution)/shard_map/ppermute | solution.py:250
  202.1 0.0 copy-start.4
  202.1 0.0 collective-permute-done.6.refs_1_
  202.1 0.0 copy-start.2
  202.1 1.7 copy-done.2
  203.8 0.0 copy-done.3
  203.8 0.3 copy-done.4
  204.1 0.0 copy-done.1
  204.1 36.5 %left_end.1 = bf16[1,2,2048,512]{3,2,1,0:T(8,128)(2,1)} custom-call(s32[9,64]{1,0:T(8,128)} %get-tuple-element.8.rows, s32[4]{0:T(128)} %pad_add_fusion.place, bf16[1,2,2048,512]{3,2,1,0:T(8,128)(2,1)} %terminal.3, bf16[64,32,224]{2,1,0:T(8,128)(2,1)} %get-tuple-element.9.plus, bf16[64,32,224]{2,1,0:T(8,128)(2,1)} %get-tuple-element.10.minus, ...), custom_call_target="tpu_custom_call" | custom-call | flops 20000000000 | bytes 16777216 | tf_op jit(solution)/shard_map/left_end/pallas_call | solution.py:283
Async XLA Ops:
  4.2 32.8 %copy-start = (bf16[3,1024,512]{2,1,0:T(8,128)(2,1)}, bf16[3,1024,512]{2,1,0:T(8,128)(2,1)S(1)}, u32[]{:S(2)}) copy-start(bf16[3,1024,512]{2,1,0:T(8,128)(2,1)S(1)} %pad_maximum_fusion.refs_0_) | copy-start | bytes 9437188
  4.2 27.4 %copy-start.5 = (f32[1,2]{1,0:T(1,128)S(1)}, f32[1,2]{1,0:T(1,128)}, u32[]{:S(2)}) copy-start(f32[1,2]{1,0:T(1,128)} %param.7) | copy-start | bytes 28
  4.2 55.4 %collective-permute-start.1 = (bf16[3,1024,512]{2,1,0:T(8,128)(2,1)S(1)}, bf16[3,1024,512]{2,1,0:T(8,128)(2,1)}, u32[]{:S(2)}, u32[]{:S(2)}) collective-permute-start(bf16[3,1024,512]{2,1,0:T(8,128)(2,1)S(1)} %pad_maximum_fusion.refs_0_), channel_id=1, source_target_pairs={{0,1},{1,0},{2,3},{3,2},{4,5},{5,4},{6,7},{7,6},{8,9},{9,8},{10,11... | collective-permute-start | bytes 9437192 | tf_op jit(solution)/shard_map/ppermute | solution.py:250
  5.1 26.5 %collective-permute-start.2 = (bf16[1024,512]{1,0:T(8,128)(2,1)S(1)}, bf16[1024,512]{1,0:T(8,128)(2,1)}, u32[]{:S(2)}, u32[]{:S(2)}) collective-permute-start(bf16[1024,512]{1,0:T(8,128)(2,1)S(1)} %fusion.3), channel_id=1, source_target_pairs={{0,2},{1,3},{2,0},{3,1},{4,6},{5,7},{6,4},{7,5},{8,10},{9,11},{10,... | collective-permute-start | bytes 3145736 | tf_op jit(solution)/shard_map/ppermute | solution.py:250
  31.6 28.0 %collective-permute-start.3 = (bf16[1024,512]{1,0:T(8,128)(2,1)}, bf16[1024,512]{1,0:T(8,128)(2,1)}, u32[]{:S(2)}, u32[]{:S(2)}) collective-permute-start(bf16[1024,512]{1,0:T(8,128)(2,1)} %collective-permute-done.2.refs_2_), channel_id=1, source_target_pairs={{0,1},{1,0},{2,3},{3,2},{4,5},{5,4},{6,7},{7,6},{8,9},{9,8},{10,11... | collective-permute-start | bytes 3145736 | tf_op jit(solution)/shard_map/ppermute | solution.py:250
  31.6 10.8 %collective-permute-start = (f32[1,2]{1,0:T(1,128)S(1)}, f32[1,2]{1,0:T(1,128)S(1)}, u32[]{:S(2)}, u32[]{:S(2)}) collective-permute-start(f32[1,2]{1,0:T(1,128)S(1)} %copy-done.5), channel_id=1, source_target_pairs={{4,0},{8,4},{12,8},{5,1},{9,5},{13,9},{6,2},{10,6},{14,10},{7,3},{... | collective-permute-start | bytes 32 | tf_op jit(solution)/shard_map/ppermute | solution.py:17
  100.3 73.3 %collective-permute-start.5 = (bf16[2,1024,512]{2,1,0:T(8,128)(2,1)S(1)}, bf16[2,1024,512]{2,1,0:T(8,128)(2,1)S(1)}, u32[]{:S(2)}, u32[]{:S(2)}) collective-permute-start(bf16[2,1024,512]{2,1,0:T(8,128)(2,1)S(1)} %get-tuple-element.14), channel_id=1, source_target_pairs={{4,0},{8,4},{12,8},{5,1},{9,5},{13,9},{6,2},{10,6},{14,10},{7,3},{... | collective-permute-start | bytes 6291464 | tf_op jit(solution)/shard_map/ppermute | solution.py:17
  102.0 71.6 %collective-permute-start.4 = (bf16[1,1024,512]{2,1,0:T(8,128)(2,1)S(1)}, bf16[1,1024,512]{2,1,0:T(8,128)(2,1)S(1)}, u32[]{:S(2)}, u32[]{:S(2)}) collective-permute-start(bf16[1,1024,512]{2,1,0:T(8,128)(2,1)S(1)} %fusion.2), channel_id=1, source_target_pairs={{4,0},{8,4},{12,8},{5,1},{9,5},{13,9},{6,2},{10,6},{14,10},{7,3},{... | collective-permute-start | bytes 3145736 | tf_op jit(solution)/shard_map/ppermute | solution.py:17
  173.8 30.4 %copy-start.1 = (bf16[3,1024,512]{2,1,0:T(8,128)(2,1)}, bf16[3,1024,512]{2,1,0:T(8,128)(2,1)S(1)}, u32[]{:S(2)}) copy-start(bf16[3,1024,512]{2,1,0:T(8,128)(2,1)S(1)} %constant_dynamic-update-slice_fusion.refs_0_) | copy-start | bytes 9437188
  173.8 28.3 %collective-permute-start.6 = (bf16[3,1024,512]{2,1,0:T(8,128)(2,1)S(1)}, bf16[3,1024,512]{2,1,0:T(8,128)(2,1)S(1)}, u32[]{:S(2)}, u32[]{:S(2)}) collective-permute-start(bf16[3,1024,512]{2,1,0:T(8,128)(2,1)S(1)} %constant_dynamic-update-slice_fusion.refs_0_), channel_id=1, source_target_pairs={{0,1},{1,0},{2,3},{3,2},{4,5},{5,4},{6,7},{7,6},{8,9},{9,8},{10,11... | collective-permute-start | bytes 9437192 | tf_op jit(solution)/shard_map/ppermute | solution.py:250
  173.9 25.6 %collective-permute-start.7 = (bf16[1024,512]{1,0:T(8,128)(2,1)S(1)}, bf16[1024,512]{1,0:T(8,128)(2,1)S(1)}, u32[]{:S(2)}, u32[]{:S(2)}) collective-permute-start(bf16[1024,512]{1,0:T(8,128)(2,1)S(1)} %bitcast.18), channel_id=1, source_target_pairs={{0,2},{1,3},{2,0},{3,1},{4,6},{5,7},{6,4},{7,5},{8,10},{9,11},{10,... | collective-permute-start | bytes 3145736 | tf_op jit(solution)/shard_map/ppermute | solution.py:250
  199.4 4.4 %copy-start.3 = (bf16[1024,512]{1,0:T(8,128)(2,1)}, bf16[1024,512]{1,0:T(8,128)(2,1)S(1)}, u32[]{:S(2)}) copy-start(bf16[1024,512]{1,0:T(8,128)(2,1)S(1)} %collective-permute-done.7.refs_2_) | copy-start | bytes 3145732
  199.5 2.7 %collective-permute-start.8 = (bf16[1024,512]{1,0:T(8,128)(2,1)S(1)}, bf16[1024,512]{1,0:T(8,128)(2,1)S(1)}, u32[]{:S(2)}, u32[]{:S(2)}) collective-permute-start(bf16[1024,512]{1,0:T(8,128)(2,1)S(1)} %collective-permute-done.7.refs_2_), channel_id=1, source_target_pairs={{0,1},{1,0},{2,3},{3,2},{4,5},{5,4},{6,7},{7,6},{8,9},{9,8},{10,11... | collective-permute-start | bytes 3145736 | tf_op jit(solution)/shard_map/ppermute | solution.py:250
  202.1 2.0 copy-start.4
  202.1 1.7 copy-start.2

commit v2 on v1

--- a/solution.py
+++ b/solution.py
@@ -122,49 +122,91 @@
             target[far, near] = turned_tile(source[near, far])
 
 
-def assemble(place, near, near_pair, far, far_pair, c_ref, d_ref, stage, sems, tile):
+def load_all(copies, sems):
+    copies = [pltpu.make_async_copy(source, target, sems.at[k]) for k, (source, target) in enumerate(copies)]
+    for copy in copies:
+        copy.start()
+    for copy in copies:
+        copy.wait()
+
+
+def part_of(first, k, tile):
+    return pl.ds(pl.multiple_of(first + k * tile, tile), tile)
+
+
+def assemble_first(place, near, near_pair, far, far_pair, c_ref, d_ref, stage, sems, tile):
     half, width = far.shape
     here, there = place[2], half - place[2]
     own, pair = place[3], width - place[3]
-    chip_rows, other_rows = (pl.ds(pl.multiple_of(first, half), half) for first in (here, there))
+    n = 2 * half
+    other_rows = pl.ds(pl.multiple_of(there, half), half)
 
     def cols(first):
         return pl.ds(pl.multiple_of(first, width), width)
 
     copies = [
-        (near.at[0], c_ref.at[chip_rows, cols(here + own)]),
-        (near_pair.at[0], c_ref.at[chip_rows, cols(here + pair)]),
         (far, c_ref.at[other_rows, cols(there + own)]),
         (far_pair, c_ref.at[other_rows, cols(there + pair)]),
     ]
     for k in range(2):
-        copies.append((near.at[1 + k], stage.at[pl.ds(k * half, half), cols(own)]))
-        copies.append((near_pair.at[1 + k], stage.at[pl.ds(k * half, half), cols(pair)]))
-    copies = [pltpu.make_async_copy(a, b, sems.at[k]) for k, (a, b) in enumerate(copies)]
-    for copy in copies:
-        copy.start()
-    for copy in copies:
-        copy.wait()
-
-    def part(first, k):
-        return pl.ds(pl.multiple_of(first + k * tile, tile), tile)
+        copies.append((near.at[0, k], stage.at[:, cols(k * half + own)]))
+        copies.append((near_pair.at[0, k], stage.at[:, cols(k * half + pair)]))
+    load_all(copies, sems)
+
+    def near_tile(rows, j):
+        real = stage[rows, pl.ds(j * tile, tile)].astype(F32)
+        imag = stage[rows, pl.ds(half + j * tile, tile)].astype(F32)
+        total, less = (real + imag).astype(BF16), (real - imag).astype(BF16)
+        c_ref[rows, part_of(here, j, tile)] = total
+        d_ref[rows, part_of(here, j, tile)] = less
+        return total, less
 
     @pl.loop(0, half // tile)
     def _(i):
-        for first in (0, half):
-            for j in range(half // tile):
-                d_ref[part(first, j), part(first, i)] = c_ref[part(first, i), part(first, j)].T
         for j in range(half // tile):
-            real = stage[part(0, i), part(0, j)].astype(F32)
-            imag = stage[part(half, i), part(0, j)].astype(F32)
-            total, less = (real + imag).astype(BF16), (real - imag).astype(BF16)
-            c_ref[part(there, i), part(here, j)] = total
-            d_ref[part(there, i), part(here, j)] = less
-            c_ref[part(here, j), part(there, i)] = less.T
-            d_ref[part(here, j), part(there, i)] = total.T
-
-
-def own_step(step, start, width, c_ref, d_ref, flat, turned, tile, base, out):
+            near_tile(part_of(here, i, tile), j)
+            total, less = near_tile(part_of(there, i, tile), j)
+            c_ref[part_of(here, j, tile), part_of(there, i, tile)] = less.T
+            d_ref[part_of(here, j, tile), part_of(there, i, tile)] = total.T
+            turned = c_ref[part_of(there, i, tile), part_of(there, j, tile)].T
+            d_ref[part_of(there, j, tile), part_of(there, i, tile)] = turned
+
+
+def assemble_second(place, near, near_pair, far, far_pair, c_ref, d_ref, stage, sems, tile):
+    depth, width = near[0].shape
+    half = 2 * width
+    chunks = half // depth
+    here, there = place[2], half - place[2]
+    own, pair = place[3], width - place[3]
+
+    def block(rows, cols):
+        return pl.ds(pl.multiple_of(rows, depth), depth), pl.ds(pl.multiple_of(cols, width), width)
+
+    copies = []
+    for pieces, chip, core in ((near, here, own), (near_pair, here, pair), (far, there, own), (far_pair, there, pair)):
+        for k in range(chunks):
+            copies.append((pieces[k], c_ref.at[block(chip + k * depth, chip + core)]))
+            copies.append((pieces[chunks + k], stage.at[block(chip + k * depth, core)]))
+    load_all(copies, sems)
+
+    @pl.loop(0, half // tile)
+    def _(i):
+        for j in range(half // tile):
+            for first in (0, half):
+                d_ref[part_of(first, j, tile), part_of(first, i, tile)] = c_ref[
+                    part_of(first, i, tile), part_of(first, j, tile)
+                ].T
+            low = stage[part_of(0, i, tile), part_of(0, j, tile)]
+            high = stage[part_of(half, j, tile), part_of(0, i, tile)]
+            low_turned, high_turned = low.T.astype(F32), high.T.astype(F32)
+            low, high = low.astype(F32), high.astype(F32)
+            c_ref[part_of(half, i, tile), part_of(0, j, tile)] = (low - high_turned).astype(BF16)
+            d_ref[part_of(half, i, tile), part_of(0, j, tile)] = (low + high_turned).astype(BF16)
+            c_ref[part_of(0, j, tile), part_of(half, i, tile)] = (low_turned + high).astype(BF16)
+            d_ref[part_of(0, j, tile), part_of(half, i, tile)] = (low_turned - high).astype(BF16)
+
+
+def own_step(step, start, width, c_ref, d_ref, flat, turned, tile, base, out, parts):
     n = c_ref.shape[0]
     part = min(tile, width)
 
@@ -189,61 +231,95 @@
             far = pl.ds(j * part, part)
             turned[near, far] = turned_tile(flat[far, near])
 
-    @pl.loop(0, n // step.size)
-    def _(c):
-        own = pl.ds(pl.multiple_of(c * step.size, step.size), step.size)
-        for s in range(width // part):
-            cols = pl.ds(pl.multiple_of(start + s * part, part), part)
-            of = [pl.ds(k * width + s * part, part) for k in range(4)]
-            first = step.ham(step.plus, c, d_ref, c_ref, cols) + step.pull(c, turned, of[2])
-            second = step.ham(step.minus, c, c_ref, d_ref, cols) + step.pull(c, turned, of[3])
-            first = first + turned[own, of[0]].astype(F32)
-            second = second + turned[own, of[1]].astype(F32)
-            real, imag = base(own, cols, pl.ds(s * part, part))
-            out[0, 0, own, pl.ds(s * part, part)] = (real + 0.5 * time_step * (first + second)).astype(BF16)
-            out[0, 1, own, pl.ds(s * part, part)] = (imag + 0.5 * time_step * (first - second)).astype(BF16)
-
-
-def fill(place, pieces, c_ref, d_ref, flat, sems, tile):
-    if len(pieces) == 1:
-        load = pltpu.make_async_copy(pieces[0], c_ref, sems.at[0])
-        load.start()
-        load.wait()
-        turn_whole(c_ref, d_ref, tile)
+    def finish(first, count, pass_on):
+        @pl.loop(0, count)
+        def _(t):
+            c = first // step.size + t
+            own = pl.ds(pl.multiple_of(c * step.size, step.size), step.size)
+            for s in range(width // part):
+                cols = pl.ds(pl.multiple_of(start + s * part, part), part)
+                to = pl.ds(s * part, part)
+                of = [pl.ds(k * width + s * part, part) for k in range(4)]
+                change = step.ham(step.plus, c, d_ref, c_ref, cols) + step.pull(c, turned, of[2])
+                second = step.ham(step.minus, c, c_ref, d_ref, cols) + step.pull(c, turned, of[3])
+                change = change + turned[own, of[0]].astype(F32)
+                second = second + turned[own, of[1]].astype(F32)
+                real, imag = base(own, cols, to)
+                real = real + 0.5 * time_step * (change + second)
+                imag = imag + 0.5 * time_step * (change - second)
+                out[0, 0, own, to] = real.astype(BF16)
+                out[0, 1, own, to] = imag.astype(BF16)
+                if pass_on is not None:
+                    pass_on(pl.ds(pl.multiple_of(t * step.size, step.size), step.size), to, real, imag)
+
+    for first, count, pass_on in parts:
+        finish(first, count, pass_on)
+
+
+def fill_whole(piece, c_ref, d_ref, sems, tile):
+    load_all([(piece, c_ref)], sems)
+    turn_whole(c_ref, d_ref, tile)
+
+
+def inner_kernel(counts, tile, number, rows, place, terminal, plus, minus, jump, *refs):
+    pieces, refs = refs[:number], refs[number:]
+    *outs, c_ref, d_ref, flat, turned, sems = refs
+    out, passed = outs[0], outs[1:]
+    n, width = out.shape[2], out.shape[3]
+    size = plus.shape[1]
+    if number == 1:
+        fill_whole(pieces[0], c_ref, d_ref, sems, tile)
+        parts = [(0, n // size, None)]
     else:
-        assemble(place, *pieces, c_ref, d_ref, flat, sems, tile)
-
-
-def inner_kernel(counts, tile, rows, place, terminal, plus, minus, jump, *refs):
-    *pieces, out, c_ref, d_ref, flat, turned, sems = refs
-    fill(place, pieces, c_ref, d_ref, flat, sems, tile)
-    step = Step(rows, counts, plus.shape[1], plus, minus, jump)
+        assemble_first(place, *pieces, c_ref, d_ref, flat, sems, tile)
+        depth = passed[0].shape[0]
+        half, chunks = 2 * width, 2 * width // depth
+        parts = []
+
+        def send_mixed(target, rows, cols, real, imag):
+            target[rows, cols] = (real + imag).astype(BF16)
+
+        def send_one(target, rows, cols, real, imag):
+            target[rows, cols] = jnp.where(place[2] == 0, real, imag).astype(BF16)
+
+        for k in range(chunks):
+            parts.append((place[2] + k * depth, depth // size, functools.partial(send_mixed, passed[k])))
+        for k in range(chunks):
+            target = passed[chunks + k]
+            parts.append((half - place[2] + k * depth, depth // size, functools.partial(send_one, target)))
+    step = Step(rows, counts, size, plus, minus, jump)
 
     def base(own, _, cols):
         return terminal[0, 0, own, cols].astype(F32), terminal[0, 1, own, cols].astype(F32)
 
-    own_step(step, place[0], out.shape[3], c_ref, d_ref, flat, turned, tile, base, out)
-
-
-def start_kernel(counts, tile, rows, place, terminal, plus, minus, jump, *refs):
-    *pieces, out, c_ref, d_ref, flat, turned, sems = refs
+    own_step(step, place[0], width, c_ref, d_ref, flat, turned, tile, base, out, parts)
+
+
+def start_kernel(counts, tile, number, rows, place, terminal, plus, minus, jump, *refs):
+    pieces, refs = refs[:number], refs[number:]
+    out, c_ref, d_ref, flat, turned, sems = refs
+    size = plus.shape[1]
 
     @pl.when(place[1] == 1)
     def _():
-        keep = pltpu.make_async_copy(terminal, out, sems.at[0])
-        keep.start()
-        keep.wait()
+        load_all([(terminal, out)], sems)
 
     @pl.when(place[1] == 0)
     def _():
-        fill(place, pieces, c_ref, d_ref, flat, sems, tile)
-        step = Step(rows, counts, plus.shape[1], plus, minus, jump)
+        if number == 1:
+            fill_whole(pieces[0], c_ref, d_ref, sems, tile)
+        else:
+            each = number // 4
+            groups = [pieces[k * each : (k + 1) * each] for k in range(4)]
+            assemble_second(place, *groups, c_ref, d_ref, flat, sems, tile)
+        step = Step(rows, counts, size, plus, minus, jump)
 
         def base(own, cols, _):
             first, second = c_ref[own, cols].astype(F32), d_ref[own, cols].astype(F32)
             return 0.5 * (first + second), 0.5 * (first - second)
 
-        own_step(step, place[0], out.shape[3], c_ref, d_ref, flat, turned, tile, base, out)
+        parts = [(0, out.shape[2] // size, None)]
+        own_step(step, place[0], out.shape[3], c_ref, d_ref, flat, turned, tile, base, out, parts)
 
 
 def swapped(block, bit):
@@ -253,7 +329,6 @@
 def on_device(terminal, controls, ham_blocks, ham_cols, jump_blocks, jump_cols):
     n, width = terminal.shape[2], terminal.shape[3]
     tile = 256
-    two_chips = lax.axis_size("row") == 4
     row = lax.axis_index("row")
     here = row // 2 * 2 * width
     controls_next = shifted_down(controls, "tm")
@@ -262,52 +337,57 @@
     amplitudes = jnp.stack([controls[0, 1], controls_next[0, 0]])
     counts, rows, jump_row, plus, minus = operator_tables(ham_blocks, ham_cols, jump_blocks, jump_cols, amplitudes)
 
-    def packed(state):
-        mine = lax.dynamic_slice_in_dim(state[0], here, 2 * width, 1).astype(F32)
-        rest = lax.dynamic_slice_in_dim(state[0], 2 * width - here, 2 * width, 1)
-        return (mine[0] + mine[1]).astype(BF16)[None], rest
-
-    def gathered(mixed, rest):
-        near = jnp.concatenate([mixed, rest], axis=0)
-        far = swapped(mixed[0], 2)
-        return [near, swapped(near, 1), far, swapped(far, 1)]
-
-    def whole(state):
-        return (state[0, 0].astype(F32) + state[0, 1].astype(F32)).astype(BF16)
-
     smem = pl.BlockSpec(memory_space=pltpu.SMEM)
     vmem = pl.BlockSpec(memory_space=pltpu.VMEM)
     anywhere = pl.BlockSpec(memory_space=pl.ANY)
-
-    def step_call(kernel, name, state_spec, k, pieces):
+    whole_out = jax.ShapeDtypeStruct(terminal.shape, BF16)
+
+    def step_call(kernel, name, state_spec, k, pieces, passed):
         return pl.pallas_call(
-            functools.partial(kernel, counts, tile),
-            out_shape=jax.ShapeDtypeStruct(terminal.shape, BF16),
+            functools.partial(kernel, counts, tile, len(pieces)),
+            out_shape=[whole_out] + passed,
             in_specs=[smem, smem, state_spec, vmem, vmem, vmem] + [anywhere] * len(pieces),
-            out_specs=vmem,
+            out_specs=[vmem] * (1 + len(passed)),
             scratch_shapes=[
                 pltpu.VMEM((n, n), BF16),
                 pltpu.VMEM((n, n), BF16),
-                pltpu.VMEM((4 * width, n), BF16),
+                pltpu.VMEM((max(4 * width, n), n), BF16),
                 pltpu.VMEM((n, 4 * width), BF16),
-                pltpu.SemaphoreType.DMA((8,)),
+                pltpu.SemaphoreType.DMA((max(len(pieces), 6),)),
             ],
             compiler_params=pltpu.CompilerParams(vmem_limit_bytes=60 * 2**20),
             cost_estimate=pl.CostEstimate(flops=2 * 10**10, bytes_accessed=16 * 2**20, transcendentals=0),
             name=name,
         )(rows, place, terminal, plus[k], minus[k], jump_row, *pieces)
 
-    if two_chips:
-        pieces = gathered(*packed(terminal))
+    if lax.axis_size("row") == 4:
+        near_pair = swapped(terminal, 1)
+        mine = lax.dynamic_slice_in_dim(terminal[0], here, 2 * width, 1).astype(F32)
+        far = swapped((mine[0] + mine[1]).astype(BF16), 2)
+        far, rows = lax.optimization_barrier((far, rows))
+        chunk = jax.ShapeDtypeStruct((width, width), BF16)
+        new_fpoint, *sent = step_call(
+            inner_kernel, "inner_point", vmem, 0, [terminal, near_pair, far, swapped(far, 1)], [chunk] * 4
+        )
+        near, far = [], []
+        for k, piece in enumerate(sent):
+            if k >= 2:
+                piece, _ = lax.optimization_barrier((piece, near[k - 2]))
+            near.append(shifted_down(piece, "tm"))
+            far.append(swapped(near[k], 2))
+        pieces = near + [swapped(piece, 1) for piece in near] + far + [swapped(piece, 1) for piece in far]
+        (new_cpoint,) = step_call(start_kernel, "left_end", anywhere, 1, pieces, [])
     else:
-        pieces = [lax.all_gather(whole(terminal), "row", axis=1, tiled=True)]
-    new_fpoint = step_call(inner_kernel, "inner_point", vmem, 0, pieces)
-    if two_chips:
-        mixed, rest = packed(new_fpoint)
-        pieces = gathered(shifted_down(mixed, "tm"), shifted_down(rest, "tm"))
-    else:
-        pieces = [lax.all_gather(shifted_down(whole(new_fpoint), "tm"), "row", axis=1, tiled=True)]
-    new_cpoint = step_call(start_kernel, "left_end", anywhere, 1, pieces)
+
+        def gathered(mixed):
+            return [lax.all_gather(mixed, "row", axis=1, tiled=True)]
+
+        def mixture(state):
+            return (state[0, 0].astype(F32) + state[0, 1].astype(F32)).astype(BF16)
+
+        (new_fpoint,) = step_call(inner_kernel, "inner_point", vmem, 0, gathered(mixture(terminal)), [])
+        pieces = gathered(shifted_down(mixture(new_fpoint), "tm"))
+        (new_cpoint,) = step_call(start_kernel, "left_end", anywhere, 1, pieces, [])
     return (new_cpoint, new_fpoint)
 
 

time: 241 us -> 184 us (0.76)
  waiting for transfers between devices: 121 us -> 63.1 us
  other arithmetic: 9 us -> 4.26 us
  Pallas kernels: 90.2 us -> 94.2 us
  starting transfers between devices: 8.73 us -> 12.3 us
  local copies, waits for them, and re-layouts: 11.1 us -> 8.63 us
    ppermute x6 -> x15, waiting for transfers between devices: 50.5 us -> 18.7 us  [swapped(): lax.ppermute(block, 'row', [(i, i ^ bit) for i in range(lax.axis_size('ro...]
    ppermute x3 -> x5, waiting for transfers between devices: 70.3 us -> 44.4 us  [shifted_down(): return lax.ppermute(block, axis, route)]
    pallas_call x2, Pallas kernels: 74.2 us -> 78.1 us  [step_call(): pl.pallas_call(functools.partial(kernel, counts, tile, len(pieces)), out_...]
    dynamic_slice x1 -> x0, other arithmetic: 2.92 us -> none  [packed(): rest = lax.dynamic_slice_in_dim(state[0], 2 * width - here, 2 * width, 1)]
    ppermute x3 -> x5, starting transfers between devices: 3.87 us -> 6.43 us  [shifted_down(): return lax.ppermute(block, axis, route)]
    unnamed x15 -> x42, local copies, waits for them, and re-layouts: 10.4 us -> 8.07 us
    ppermute x6 -> x15, starting transfers between devices: 4.87 us -> 5.84 us  [swapped(): lax.ppermute(block, 'row', [(i, i ^ bit) for i in range(lax.axis_size('ro...]
  transfers between devices with their start and end apart: 9 -> 20, of which waited for: 4 -> 8; matrix products, arithmetic and copies ran while one was open for 5% -> 6% of each run, Pallas kernels for 7% -> 9%
where the time goes in v2:
time: 184 us; the launch traced here: 183 us
  Pallas kernels  94.2 us (51%)
  waiting for transfers between devices  63.1 us (34%)
  starting transfers between devices  12.3 us (7%)
  local copies, waits for them, and re-layouts  8.63 us (5%)
  other arithmetic  4.26 us (2%)
    pallas_call x2, Pallas kernels, step_call(): pl.pallas_call(functools.partial(kernel, counts, tile, len(pieces)), out_...  78.1 us
    ppermute x5, waiting for transfers between devices, shifted_down(): return lax.ppermute(block, axis, route)  44.4 us
    ppermute x15, waiting for transfers between devices, swapped(): lax.ppermute(block, 'row', [(i, i ^ bit) for i in range(lax.axis_size('ro...  18.7 us
    pallas_call x1, Pallas kernels, operator_tables(): pl.pallas_call(table_kernel, out_shape=[jax.ShapeDtypeStruct((2 * layers_...  16 us
    unnamed x42, local copies, waits for them, and re-layouts  8.07 us
    ppermute x5, starting transfers between devices, shifted_down(): return lax.ppermute(block, axis, route)  6.43 us
    ppermute x15, starting transfers between devices, swapped(): lax.ppermute(block, 'row', [(i, i ^ bit) for i in range(lax.axis_size('ro...  5.84 us
  transfers between devices with their start and end apart: 20, of which 8 were waited for; matrix products, arithmetic and copies ran while one was open for 6% of the time, Pallas kernels for 9%

profile of v2, /device:TPU:0, one launch (start us, length us, event | category | flops | bytes accessed | tf_op | source)
XLA Modules:
  0.0 183.3 jit_solution(8813040323403490339)
XLA Ops:
  0.6 0.5 collective-permute-start.2
  1.1 2.2 %dynamic-slice_convert_fusion = f32[1,2,1024,512]{3,2,1,0:T(8,128)S(1)} fusion(bf16[1,2,2048,512]{3,2,1,0:T(8,128)(2,1)} %terminal.3, s32[]{:T(128)S(6)} %select_n.15), kind=kLoop, calls=%fused_computation.2 | loop fusion | flops 1048576 | bytes 6291460 | tf_op jit(solution)/shard_map/convert_element_type | solution.py:365
  3.3 0.0 copy-start.19
  3.3 0.0 copy-start.1
  3.4 0.0 copy-start
  3.4 0.4 fusion.1
  3.7 2.6 %collective-permute-start = (bf16[1024,512]{1,0:T(8,128)(2,1)S(1)}, bf16[1024,512]{1,0:T(8,128)(2,1)}, u32[]{:S(2)}, u32[]{:S(2)}) collective-permute-start(bf16[1024,512]{1,0:T(8,128)(2,1)S(1)} %fusion.1), channel_id=1, source_target_pairs={{0,2},{1,3},{2,0},{3,1},{4,6},{5,7},{6,4},{7,5},{8,10},{9,11},{10,... | collective-permute-start | bytes 3145736 | tf_op jit(solution)/shard_map/ppermute | solution.py:326
  6.3 0.0 copy-done.19
  6.3 1.3 collective-permute-start.1
  7.6 0.6 slice.16
  8.2 0.0 copy-done.1
  8.2 2.4 %copy.9.jump = bf16[64,2,32,32]{3,2,1,0:T(8,128)(2,1)} copy(bf16[64,2,32,32]{0,3,2,1:T(8,128)(2,1)S(1)} %copy-done.1) | data formatting | bytes 524288 | tf_op args[4]
  10.6 3.9 %copy.8.ham = bf16[2,64,2,32,32]{4,3,2,1,0:T(8,128)(2,1)} copy(bf16[2,64,2,32,32]{1,4,3,2,0:T(8,128)(2,1)S(1)} %copy-done) | data formatting | bytes 1048576 | tf_op args[2]
  14.5 0.0 collective-permute-done.1
  14.5 1.2 pad_maximum_fusion.amplitudes
  15.6 16.0 %operator_tables.1 = (s32[9,64]{1,0:T(8,128)}, bf16[64,32,64]{2,1,0:T(8,128)(2,1)}, bf16[64,32,224]{2,1,0:T(8,128)(2,1)}, bf16[64,32,224]{2,1,0:T(8,128)(2,1)}, ...) custom-call(s32[2,64]{1,0:T(2,128)} %ham_cols.1, s32[2,64]{1,0:T(2,128)} %jump_cols.1, ...), custom_call_target="tpu_custom_call" | custom-call | flops 1000000000 | bytes 10485760 | tf_op jit(solution)/shard_map/operator_tables/pallas_call | solution.py:74
  31.7 0.0 collective-permute-done.refs_2_
  31.7 0.2 collective-permute-start.3
  31.9 0.6 pad_add_fusion.place
  32.5 2.1 %collective-permute-done.3.refs_3_ = bf16[1024,512]{1,0:T(8,128)(2,1)S(1)} collective-permute-done((bf16[1024,512]{1,0:T(8,128)(2,1)}, bf16[1024,512]{1,0:T(8,128)(2,1)S(1)}, u32[]{:S(2)}, u32[]{:S(2)}) %collective-permute-start.3) | collective-permute-done | bytes 1048608 | tf_op jit(solution)/shard_map/ppermute | solution.py:326
  34.6 0.0 collective-permute-done.2.refs_1_
  34.6 1.0 copy-done.2
  35.6 40.5 %inner_point.1 = (bf16[1,2,2048,512]{3,2,1,0:T(8,128)(2,1)}, bf16[512,512]{1,0:T(8,128)(2,1)}, bf16[512,512]{1,0:T(8,128)(2,1)}, bf16[512,512]{1,0:T(8,128)(2,1)}, bf16[512,512]{1,0:T(8,128)(2,1)}) custom-call(s32[9,64]{1,0:T(8,128)} %get-tuple-element.18.rows, s32[4]{0:T(128)} %pad_add_fusion.place, bf16[1,2,2048,512]{3,2,1,0:T(8,128)(2,1)} %terminal.3, ...), custom_call_target="tpu_custom_call" | custom-call | flops 20000000000 | bytes 16777216 | tf_op jit(solution)/shard_map/inner_point/pallas_call | solution.py:346
  76.1 1.3 collective-permute-start.4
  77.4 1.3 collective-permute-start.5
  78.7 14.9 %collective-permute-done.4.refs_0_ = bf16[512,512]{1,0:T(8,128)(2,1)S(1)} collective-permute-done((bf16[512,512]{1,0:T(8,128)(2,1)}, bf16[512,512]{1,0:T(8,128)(2,1)S(1)}, u32[]{:S(2)}, u32[]{:S(2)}) %collective-permute-start.4) | collective-permute-done | bytes 524320 | tf_op jit(solution)/shard_map/ppermute | solution.py:17
  93.5 1.3 collective-permute-start.6
  94.8 0.3 collective-permute-start.12
  95.1 9.6 %collective-permute-done.5.refs_1_ = bf16[512,512]{1,0:T(8,128)(2,1)S(1)} collective-permute-done((bf16[512,512]{1,0:T(8,128)(2,1)}, bf16[512,512]{1,0:T(8,128)(2,1)S(1)}, u32[]{:S(2)}, u32[]{:S(2)}) %collective-permute-start.5) | collective-permute-done | bytes 524320 | tf_op jit(solution)/shard_map/ppermute | solution.py:17
  104.8 0.0 collective-permute-start.8
  104.8 1.3 collective-permute-start.7
  106.0 0.3 collective-permute-start.13
  106.3 9.6 %collective-permute-done.6.refs_2_ = bf16[512,512]{1,0:T(8,128)(2,1)S(1)} collective-permute-done((bf16[512,512]{1,0:T(8,128)(2,1)}, bf16[512,512]{1,0:T(8,128)(2,1)S(1)}, u32[]{:S(2)}, u32[]{:S(2)}) %collective-permute-start.6) | collective-permute-done | bytes 524320 | tf_op jit(solution)/shard_map/ppermute | solution.py:17
  116.0 0.0 collective-permute-start.9
  116.0 0.0 collective-permute-done.12.refs_8_
  116.0 0.3 collective-permute-start.14
  116.3 0.0 collective-permute-done.8.refs_4_
  116.3 0.3 collective-permute-start.10
  116.6 10.3 %collective-permute-done.7.refs_3_ = bf16[512,512]{1,0:T(8,128)(2,1)S(1)} collective-permute-done((bf16[512,512]{1,0:T(8,128)(2,1)}, bf16[512,512]{1,0:T(8,128)(2,1)S(1)}, u32[]{:S(2)}, u32[]{:S(2)}) %collective-permute-start.7) | collective-permute-done | bytes 524320 | tf_op jit(solution)/shard_map/ppermute | solution.py:17
  126.9 0.3 collective-permute-start.15
  127.2 0.0 collective-permute-done.13.refs_9_
  127.2 0.0 collective-permute-start.11
  127.2 0.0 collective-permute-done.9.refs_5_
  127.2 0.5 collective-permute-start.16
  127.7 4.4 %collective-permute-done.14.refs_10_ = bf16[512,512]{1,0:T(8,128)(2,1)S(1)} collective-permute-done((bf16[512,512]{1,0:T(8,128)(2,1)S(1)}, bf16[512,512]{1,0:T(8,128)(2,1)S(1)}, u32[]{:S(2)}, u32[]{:S(2)}) %collective-permute-start.14) | collective-permute-done | bytes 524320 | tf_op jit(solution)/shard_map/ppermute | solution.py:326
  132.1 0.0 collective-permute-start.17
  132.1 0.0 collective-permute-done.10.refs_6_
  132.1 0.0 copy-start.12
  132.1 0.5 collective-permute-start.18
  132.6 10.3 %collective-permute-done.15.refs_11_ = bf16[512,512]{1,0:T(8,128)(2,1)S(1)} collective-permute-done((bf16[512,512]{1,0:T(8,128)(2,1)S(1)}, bf16[512,512]{1,0:T(8,128)(2,1)S(1)}, u32[]{:S(2)}, u32[]{:S(2)}) %collective-permute-start.15) | collective-permute-done | bytes 524320 | tf_op jit(solution)/shard_map/ppermute | solution.py:326
  142.9 0.0 collective-permute-start.19
  142.9 0.0 collective-permute-done.16.refs_12_
  142.9 0.0 collective-permute-done.11.refs_7_
  143.0 0.0 copy-start.14
  143.0 0.0 collective-permute-done.17.refs_13_
  143.0 0.0 collective-permute-done.18.refs_14_
  143.0 1.8 collective-permute-done.19.refs_15_
  144.8 0.0 copy-done.12
  144.8 0.0 copy-done.14
  144.9 0.0 copy-done.16
  144.9 0.0 copy-done.17
  144.9 0.7 copy-done.18
  145.6 0.0 copy-done.5
  145.7 37.7 %left_end.1 = bf16[1,2,2048,512]{3,2,1,0:T(8,128)(2,1)} custom-call(s32[9,64]{1,0:T(8,128)} %get-tuple-element.18.rows, s32[4]{0:T(128)} %pad_add_fusion.place, bf16[1,2,2048,512]{3,2,1,0:T(8,128)(2,1)} %terminal.3, bf16[64,32,224]{2,1,0:T(8,128)(2,1)} %get-tuple-element.19.plus, bf16[64,32,224]{2,1,0:T(8,128)(2,1)} %get-tuple-element.20.minus, ...), custom_call_target="tpu_custom_call" | custom-call | flops 20000000000 | bytes 16777216 | tf_op jit(solution)/shard_map/left_end/pallas_call | solution.py:346
  (26 shorter events, 0.0 us)
Async XLA Ops:
  0.6 34.0 %collective-permute-start.2 = (bf16[1,2,2048,512]{3,2,1,0:T(8,128)(2,1)}, bf16[1,2,2048,512]{3,2,1,0:T(8,128)(2,1)}, u32[]{:S(2)}, u32[]{:S(2)}) collective-permute-start(bf16[1,2,2048,512]{3,2,1,0:T(8,128)(2,1)} %terminal.3), channel_id=1, source_target_pairs={{0,1},{1,0},{2,3},{3,2},{4,5},{5,4},{6,7},{7,6},{8,9},{9,8},{10,11... | collective-permute-start | bytes 12582920 | tf_op jit(solution)/shard_map/ppermute | solution.py:326
  3.3 3.0 %copy-start.19 = (f32[1,2]{1,0:T(1,128)S(1)}, f32[1,2]{1,0:T(1,128)}, u32[]{:S(2)}) copy-start(f32[1,2]{1,0:T(1,128)} %param.7) | copy-start | bytes 28
  3.3 4.8 %copy-start.1 = (bf16[64,2,32,32]{0,3,2,1:T(8,128)(2,1)S(1)}, bf16[64,2,32,32]{0,3,2,1:T(8,128)(2,1)}, u32[]{:S(2)}) copy-start(bf16[64,2,32,32]{0,3,2,1:T(8,128)(2,1)} %param.10) | copy-start | bytes 786436
  3.4 7.2 %copy-start = (bf16[2,64,2,32,32]{1,4,3,2,0:T(8,128)(2,1)S(1)}, bf16[2,64,2,32,32]{1,4,3,2,0:T(8,128)(2,1)}, u32[]{:S(2)}) copy-start(bf16[2,64,2,32,32]{1,4,3,2,0:T(8,128)(2,1)} %param.8) | copy-start | bytes 1572868
  3.7 28.0 %collective-permute-start = (bf16[1024,512]{1,0:T(8,128)(2,1)S(1)}, bf16[1024,512]{1,0:T(8,128)(2,1)}, u32[]{:S(2)}, u32[]{:S(2)}) collective-permute-start(bf16[1024,512]{1,0:T(8,128)(2,1)S(1)} %fusion.1), channel_id=1, source_target_pairs={{0,2},{1,3},{2,0},{3,1},{4,6},{5,7},{6,4},{7,5},{8,10},{9,11},{10,... | collective-permute-start | bytes 3145736 | tf_op jit(solution)/shard_map/ppermute | solution.py:326
  6.3 8.1 %collective-permute-start.1 = (f32[1,2]{1,0:T(1,128)S(1)}, f32[1,2]{1,0:T(1,128)S(1)}, u32[]{:S(2)}, u32[]{:S(2)}) collective-permute-start(f32[1,2]{1,0:T(1,128)S(1)} %copy-done.19), channel_id=1, source_target_pairs={{4,0},{8,4},{12,8},{5,1},{9,5},{13,9},{6,2},{10,6},{14,10},{7,3},{... | collective-permute-start | bytes 32 | tf_op jit(solution)/shard_map/ppermute | solution.py:17
  31.7 2.9 %collective-permute-start.3 = (bf16[1024,512]{1,0:T(8,128)(2,1)}, bf16[1024,512]{1,0:T(8,128)(2,1)S(1)}, u32[]{:S(2)}, u32[]{:S(2)}) collective-permute-start(bf16[1024,512]{1,0:T(8,128)(2,1)} %collective-permute-done.refs_2_), channel_id=1, source_target_pairs={{0,1},{1,0},{2,3},{3,2},{4,5},{5,4},{6,7},{7,6},{8,9},{9,8},{10,11... | collective-permute-start | bytes 3145736 | tf_op jit(solution)/shard_map/ppermute | solution.py:326
  34.6 1.0 copy-start.2
  76.1 17.5 %collective-permute-start.4 = (bf16[512,512]{1,0:T(8,128)(2,1)}, bf16[512,512]{1,0:T(8,128)(2,1)S(1)}, u32[]{:S(2)}, u32[]{:S(2)}) collective-permute-start(bf16[512,512]{1,0:T(8,128)(2,1)} %get-tuple-element.25), channel_id=1, source_target_pairs={{4,0},{8,4},{12,8},{5,1},{9,5},{13,9},{6,2},{10,6},{14,10},{7,3},{... | collective-permute-start | bytes 1572872 | tf_op jit(solution)/shard_map/ppermute | solution.py:17
  77.4 27.4 %collective-permute-start.5 = (bf16[512,512]{1,0:T(8,128)(2,1)}, bf16[512,512]{1,0:T(8,128)(2,1)S(1)}, u32[]{:S(2)}, u32[]{:S(2)}) collective-permute-start(bf16[512,512]{1,0:T(8,128)(2,1)} %get-tuple-element.26), channel_id=1, source_target_pairs={{4,0},{8,4},{12,8},{5,1},{9,5},{13,9},{6,2},{10,6},{14,10},{7,3},{... | collective-permute-start | bytes 1572872 | tf_op jit(solution)/shard_map/ppermute | solution.py:17
  93.5 52.1 %copy-start.3 = (bf16[512,512]{1,0:T(8,128)(2,1)}, bf16[512,512]{1,0:T(8,128)(2,1)S(1)}, u32[]{:S(2)}) copy-start(bf16[512,512]{1,0:T(8,128)(2,1)S(1)} %collective-permute-done.4.refs_0_) | copy-start | bytes 1572868
  93.5 22.5 %collective-permute-start.6 = (bf16[512,512]{1,0:T(8,128)(2,1)}, bf16[512,512]{1,0:T(8,128)(2,1)S(1)}, u32[]{:S(2)}, u32[]{:S(2)}) collective-permute-start(bf16[512,512]{1,0:T(8,128)(2,1)} %get-tuple-element.28), channel_id=1, source_target_pairs={{4,0},{8,4},{12,8},{5,1},{9,5},{13,9},{6,2},{10,6},{14,10},{7,3},{... | collective-permute-start | bytes 1572872 | tf_op jit(solution)/shard_map/ppermute | solution.py:17
  94.8 21.2 %collective-permute-start.12 = (bf16[512,512]{1,0:T(8,128)(2,1)S(1)}, bf16[512,512]{1,0:T(8,128)(2,1)S(1)}, u32[]{:S(2)}, u32[]{:S(2)}) collective-permute-start(bf16[512,512]{1,0:T(8,128)(2,1)S(1)} %collective-permute-done.4.refs_0_), channel_id=1, source_target_pairs={{0,2},{1,3},{2,0},{3,1},{4,6},{5,7},{6,4},{7,5},{8,10},{9,11},{10,... | collective-permute-start | bytes 1572872 | tf_op jit(solution)/shard_map/ppermute | solution.py:326
  104.8 40.9 %copy-start.4 = (bf16[512,512]{1,0:T(8,128)(2,1)}, bf16[512,512]{1,0:T(8,128)(2,1)S(1)}, u32[]{:S(2)}) copy-start(bf16[512,512]{1,0:T(8,128)(2,1)S(1)} %collective-permute-done.5.refs_1_) | copy-start | bytes 1572868
  104.8 11.6 %collective-permute-start.8 = (bf16[512,512]{1,0:T(8,128)(2,1)S(1)}, bf16[512,512]{1,0:T(8,128)(2,1)S(1)}, u32[]{:S(2)}, u32[]{:S(2)}) collective-permute-start(bf16[512,512]{1,0:T(8,128)(2,1)S(1)} %collective-permute-done.4.refs_0_), channel_id=1, source_target_pairs={{0,1},{1,0},{2,3},{3,2},{4,5},{5,4},{6,7},{7,6},{8,9},{9,8},{10,11... | collective-permute-start | bytes 1572872 | tf_op jit(solution)/shard_map/ppermute | solution.py:326
  104.8 22.1 %collective-permute-start.7 = (bf16[512,512]{1,0:T(8,128)(2,1)}, bf16[512,512]{1,0:T(8,128)(2,1)S(1)}, u32[]{:S(2)}, u32[]{:S(2)}) collective-permute-start(bf16[512,512]{1,0:T(8,128)(2,1)} %get-tuple-element.30), channel_id=1, source_target_pairs={{4,0},{8,4},{12,8},{5,1},{9,5},{13,9},{6,2},{10,6},{14,10},{7,3},{... | collective-permute-start | bytes 1572872 | tf_op jit(solution)/shard_map/ppermute | solution.py:17
  106.0 21.1 %collective-permute-start.13 = (bf16[512,512]{1,0:T(8,128)(2,1)S(1)}, bf16[512,512]{1,0:T(8,128)(2,1)S(1)}, u32[]{:S(2)}, u32[]{:S(2)}) collective-permute-start(bf16[512,512]{1,0:T(8,128)(2,1)S(1)} %collective-permute-done.5.refs_1_), channel_id=1, source_target_pairs={{0,2},{1,3},{2,0},{3,1},{4,6},{5,7},{6,4},{7,5},{8,10},{9,11},{10,... | collective-permute-start | bytes 1572872 | tf_op jit(solution)/shard_map/ppermute | solution.py:326
  116.0 29.6 %copy-start.5 = (bf16[512,512]{1,0:T(8,128)(2,1)}, bf16[512,512]{1,0:T(8,128)(2,1)S(1)}, u32[]{:S(2)}) copy-start(bf16[512,512]{1,0:T(8,128)(2,1)S(1)} %collective-permute-done.6.refs_2_) | copy-start | bytes 1572868
  116.0 11.2 %collective-permute-start.9 = (bf16[512,512]{1,0:T(8,128)(2,1)S(1)}, bf16[512,512]{1,0:T(8,128)(2,1)S(1)}, u32[]{:S(2)}, u32[]{:S(2)}) collective-permute-start(bf16[512,512]{1,0:T(8,128)(2,1)S(1)} %collective-permute-done.5.refs_1_), channel_id=1, source_target_pairs={{0,1},{1,0},{2,3},{3,2},{4,5},{5,4},{6,7},{7,6},{8,9},{9,8},{10,11... | collective-permute-start | bytes 1572872 | tf_op jit(solution)/shard_map/ppermute | solution.py:326
  116.0 29.6 %copy-start.6 = (bf16[512,512]{1,0:T(8,128)(2,1)}, bf16[512,512]{1,0:T(8,128)(2,1)S(1)}, u32[]{:S(2)}) copy-start(bf16[512,512]{1,0:T(8,128)(2,1)S(1)} %collective-permute-done.12.refs_8_) | copy-start | bytes 1572868
  116.0 16.1 %collective-permute-start.14 = (bf16[512,512]{1,0:T(8,128)(2,1)S(1)}, bf16[512,512]{1,0:T(8,128)(2,1)S(1)}, u32[]{:S(2)}, u32[]{:S(2)}) collective-permute-start(bf16[512,512]{1,0:T(8,128)(2,1)S(1)} %collective-permute-done.6.refs_2_), channel_id=1, source_target_pairs={{0,2},{1,3},{2,0},{3,1},{4,6},{5,7},{6,4},{7,5},{8,10},{9,11},{10,... | collective-permute-start | bytes 1572872 | tf_op jit(solution)/shard_map/ppermute | solution.py:326
  116.3 29.3 %copy-start.7 = (bf16[512,512]{1,0:T(8,128)(2,1)}, bf16[512,512]{1,0:T(8,128)(2,1)S(1)}, u32[]{:S(2)}) copy-start(bf16[512,512]{1,0:T(8,128)(2,1)S(1)} %collective-permute-done.8.refs_4_) | copy-start | bytes 1572868
  116.3 15.8 %collective-permute-start.10 = (bf16[512,512]{1,0:T(8,128)(2,1)S(1)}, bf16[512,512]{1,0:T(8,128)(2,1)S(1)}, u32[]{:S(2)}, u32[]{:S(2)}) collective-permute-start(bf16[512,512]{1,0:T(8,128)(2,1)S(1)} %collective-permute-done.6.refs_2_), channel_id=1, source_target_pairs={{0,1},{1,0},{2,3},{3,2},{4,5},{5,4},{6,7},{7,6},{8,9},{9,8},{10,11... | collective-permute-start | bytes 1572872 | tf_op jit(solution)/shard_map/ppermute | solution.py:326
  126.9 18.8 %copy-start.8 = (bf16[512,512]{1,0:T(8,128)(2,1)}, bf16[512,512]{1,0:T(8,128)(2,1)S(1)}, u32[]{:S(2)}) copy-start(bf16[512,512]{1,0:T(8,128)(2,1)S(1)} %collective-permute-done.7.refs_3_) | copy-start | bytes 1572868
  126.9 16.0 %collective-permute-start.15 = (bf16[512,512]{1,0:T(8,128)(2,1)S(1)}, bf16[512,512]{1,0:T(8,128)(2,1)S(1)}, u32[]{:S(2)}, u32[]{:S(2)}) collective-permute-start(bf16[512,512]{1,0:T(8,128)(2,1)S(1)} %collective-permute-done.7.refs_3_), channel_id=1, source_target_pairs={{0,2},{1,3},{2,0},{3,1},{4,6},{5,7},{6,4},{7,5},{8,10},{9,11},{10,... | collective-permute-start | bytes 1572872 | tf_op jit(solution)/shard_map/ppermute | solution.py:326
  127.2 18.5 %copy-start.9 = (bf16[512,512]{1,0:T(8,128)(2,1)}, bf16[512,512]{1,0:T(8,128)(2,1)S(1)}, u32[]{:S(2)}) copy-start(bf16[512,512]{1,0:T(8,128)(2,1)S(1)} %collective-permute-done.13.refs_9_) | copy-start | bytes 1572868
  127.2 15.8 %collective-permute-start.11 = (bf16[512,512]{1,0:T(8,128)(2,1)S(1)}, bf16[512,512]{1,0:T(8,128)(2,1)S(1)}, u32[]{:S(2)}, u32[]{:S(2)}) collective-permute-start(bf16[512,512]{1,0:T(8,128)(2,1)S(1)} %collective-permute-done.7.refs_3_), channel_id=1, source_target_pairs={{0,1},{1,0},{2,3},{3,2},{4,5},{5,4},{6,7},{7,6},{8,9},{9,8},{10,11... | collective-permute-start | bytes 1572872 | tf_op jit(solution)/shard_map/ppermute | solution.py:326
  127.2 15.8 %copy-start.10 = (bf16[512,512]{1,0:T(8,128)(2,1)}, bf16[512,512]{1,0:T(8,128)(2,1)S(1)}, u32[]{:S(2)}) copy-start(bf16[512,512]{1,0:T(8,128)(2,1)S(1)} %collective-permute-done.9.refs_5_) | copy-start | bytes 1572868
  127.2 15.7 %collective-permute-start.16 = (bf16[512,512]{1,0:T(8,128)(2,1)S(1)}, bf16[512,512]{1,0:T(8,128)(2,1)S(1)}, u32[]{:S(2)}, u32[]{:S(2)}) collective-permute-start(bf16[512,512]{1,0:T(8,128)(2,1)S(1)} %collective-permute-done.12.refs_8_), channel_id=1, source_target_pairs={{0,1},{1,0},{2,3},{3,2},{4,5},{5,4},{6,7},{7,6},{8,9},{9,8},{10,11... | collective-permute-start | bytes 1572872 | tf_op jit(solution)/shard_map/ppermute | solution.py:326
  132.1 10.9 %copy-start.11 = (bf16[512,512]{1,0:T(8,128)(2,1)}, bf16[512,512]{1,0:T(8,128)(2,1)S(1)}, u32[]{:S(2)}) copy-start(bf16[512,512]{1,0:T(8,128)(2,1)S(1)} %collective-permute-done.14.refs_10_) | copy-start | bytes 1572868
  132.1 10.9 %collective-permute-start.17 = (bf16[512,512]{1,0:T(8,128)(2,1)S(1)}, bf16[512,512]{1,0:T(8,128)(2,1)S(1)}, u32[]{:S(2)}, u32[]{:S(2)}) collective-permute-start(bf16[512,512]{1,0:T(8,128)(2,1)S(1)} %collective-permute-done.13.refs_9_), channel_id=1, source_target_pairs={{0,1},{1,0},{2,3},{3,2},{4,5},{5,4},{6,7},{7,6},{8,9},{9,8},{10,11... | collective-permute-start | bytes 1572872 | tf_op jit(solution)/shard_map/ppermute | solution.py:326
  132.1 12.8 %copy-start.12 = (bf16[512,512]{1,0:T(8,128)(2,1)}, bf16[512,512]{1,0:T(8,128)(2,1)S(1)}, u32[]{:S(2)}) copy-start(bf16[512,512]{1,0:T(8,128)(2,1)S(1)} %collective-permute-done.10.refs_6_) | copy-start | bytes 1572868
  132.1 10.9 %collective-permute-start.18 = (bf16[512,512]{1,0:T(8,128)(2,1)S(1)}, bf16[512,512]{1,0:T(8,128)(2,1)S(1)}, u32[]{:S(2)}, u32[]{:S(2)}) collective-permute-start(bf16[512,512]{1,0:T(8,128)(2,1)S(1)} %collective-permute-done.14.refs_10_), channel_id=1, source_target_pairs={{0,1},{1,0},{2,3},{3,2},{4,5},{5,4},{6,7},{7,6},{8,9},{9,8},{10,11... | collective-permute-start | bytes 1572872 | tf_op jit(solution)/shard_map/ppermute | solution.py:326
  142.9 1.9 %copy-start.13 = (bf16[512,512]{1,0:T(8,128)(2,1)}, bf16[512,512]{1,0:T(8,128)(2,1)S(1)}, u32[]{:S(2)}) copy-start(bf16[512,512]{1,0:T(8,128)(2,1)S(1)} %collective-permute-done.15.refs_11_) | copy-start | bytes 1572868
  142.9 1.9 %collective-permute-start.19 = (bf16[512,512]{1,0:T(8,128)(2,1)S(1)}, bf16[512,512]{1,0:T(8,128)(2,1)S(1)}, u32[]{:S(2)}, u32[]{:S(2)}) collective-permute-start(bf16[512,512]{1,0:T(8,128)(2,1)S(1)} %collective-permute-done.15.refs_11_), channel_id=1, source_target_pairs={{0,1},{1,0},{2,3},{3,2},{4,5},{5,4},{6,7},{7,6},{8,9},{9,8},{10,11... | collective-permute-start | bytes 1572872 | tf_op jit(solution)/shard_map/ppermute | solution.py:326
  142.9 1.9 %copy-start.15 = (bf16[512,512]{1,0:T(8,128)(2,1)}, bf16[512,512]{1,0:T(8,128)(2,1)S(1)}, u32[]{:S(2)}) copy-start(bf16[512,512]{1,0:T(8,128)(2,1)S(1)} %collective-permute-done.16.refs_12_) | copy-start | bytes 1572868
  143.0 1.9 %copy-start.14 = (bf16[512,512]{1,0:T(8,128)(2,1)}, bf16[512,512]{1,0:T(8,128)(2,1)S(1)}, u32[]{:S(2)}) copy-start(bf16[512,512]{1,0:T(8,128)(2,1)S(1)} %collective-permute-done.11.refs_7_) | copy-start | bytes 1572868
  143.0 1.9 %copy-start.16 = (bf16[512,512]{1,0:T(8,128)(2,1)}, bf16[512,512]{1,0:T(8,128)(2,1)S(1)}, u32[]{:S(2)}) copy-start(bf16[512,512]{1,0:T(8,128)(2,1)S(1)} %collective-permute-done.17.refs_13_) | copy-start | bytes 1572868
  143.0 1.9 %copy-start.17 = (bf16[512,512]{1,0:T(8,128)(2,1)}, bf16[512,512]{1,0:T(8,128)(2,1)S(1)}, u32[]{:S(2)}) copy-start(bf16[512,512]{1,0:T(8,128)(2,1)S(1)} %collective-permute-done.18.refs_14_) | copy-start | bytes 1572868
  144.8 0.8 copy-start.18

commit v3 on v2

--- a/solution.py
+++ b/solution.py
@@ -134,68 +134,66 @@
     return pl.ds(pl.multiple_of(first + k * tile, tile), tile)
 
 
-def assemble_first(place, near, near_pair, far, far_pair, c_ref, d_ref, stage, sems, tile):
+def assemble_first(place, near, near_pair, far, far_pair, c_ref, d_ref, stage, other, sems, tile):
     half, width = far.shape
     here, there = place[2], half - place[2]
     own, pair = place[3], width - place[3]
-    n = 2 * half
-    other_rows = pl.ds(pl.multiple_of(there, half), half)
 
     def cols(first):
         return pl.ds(pl.multiple_of(first, width), width)
 
     copies = [
-        (far, c_ref.at[other_rows, cols(there + own)]),
-        (far_pair, c_ref.at[other_rows, cols(there + pair)]),
+        (far, other.at[pl.ds(0, half), cols(own)]),
+        (far_pair, other.at[pl.ds(0, half), cols(pair)]),
     ]
     for k in range(2):
         copies.append((near.at[0, k], stage.at[:, cols(k * half + own)]))
         copies.append((near_pair.at[0, k], stage.at[:, cols(k * half + pair)]))
     load_all(copies, sems)
 
-    def near_tile(rows, j):
+    def mixed(rows, j):
         real = stage[rows, pl.ds(j * tile, tile)].astype(F32)
         imag = stage[rows, pl.ds(half + j * tile, tile)].astype(F32)
-        total, less = (real + imag).astype(BF16), (real - imag).astype(BF16)
-        c_ref[rows, part_of(here, j, tile)] = total
-        d_ref[rows, part_of(here, j, tile)] = less
-        return total, less
+        return (real + imag).astype(BF16), (real - imag).astype(BF16)
 
     @pl.loop(0, half // tile)
     def _(i):
+        here_i, there_i = part_of(here, i, tile), part_of(there, i, tile)
         for j in range(half // tile):
-            near_tile(part_of(here, i, tile), j)
-            total, less = near_tile(part_of(there, i, tile), j)
-            c_ref[part_of(here, j, tile), part_of(there, i, tile)] = less.T
-            d_ref[part_of(here, j, tile), part_of(there, i, tile)] = total.T
-            turned = c_ref[part_of(there, i, tile), part_of(there, j, tile)].T
-            d_ref[part_of(there, j, tile), part_of(there, i, tile)] = turned
-
-
-def assemble_second(place, near, near_pair, far, far_pair, c_ref, d_ref, stage, sems, tile):
-    depth, width = near[0].shape
+            here_j, there_j = part_of(here, j, tile), part_of(there, j, tile)
+            total, less = mixed(there_i, j)
+            c_ref[there_i, here_j] = total
+            d_ref[there_i, here_j] = less
+            c_ref[here_j, there_i] = less.T
+            d_ref[here_j, there_i] = total.T
+            block = other[part_of(0, i, tile), pl.ds(j * tile, tile)]
+            c_ref[there_i, there_j] = block
+            d_ref[there_j, there_i] = block.T
+            total, less = mixed(here_i, j)
+            c_ref[here_i, here_j] = total
+            d_ref[here_i, here_j] = less
+
+
+def assemble_second(place, spans, near, near_pair, far, far_pair, c_ref, d_ref, stage, other, sems, tile):
+    width = near[0].shape[1]
     half = 2 * width
-    chunks = half // depth
     here, there = place[2], half - place[2]
     own, pair = place[3], width - place[3]
-
-    def block(rows, cols):
-        return pl.ds(pl.multiple_of(rows, depth), depth), pl.ds(pl.multiple_of(cols, width), width)
-
     copies = []
     for pieces, chip, core in ((near, here, own), (near_pair, here, pair), (far, there, own), (far_pair, there, pair)):
-        for k in range(chunks):
-            copies.append((pieces[k], c_ref.at[block(chip + k * depth, chip + core)]))
-            copies.append((pieces[chunks + k], stage.at[block(chip + k * depth, core)]))
+        for piece, (first, depth) in zip(pieces, spans):
+            target = other if first < half else stage
+            rows = pl.ds(pl.multiple_of(chip + first % half, depth), depth)
+            copies.append((piece, target.at[rows, pl.ds(pl.multiple_of(core, width), width)]))
     load_all(copies, sems)
 
     @pl.loop(0, half // tile)
     def _(i):
         for j in range(half // tile):
             for first in (0, half):
-                d_ref[part_of(first, j, tile), part_of(first, i, tile)] = c_ref[
-                    part_of(first, i, tile), part_of(first, j, tile)
-                ].T
+                block = other[part_of(first, i, tile), pl.ds(j * tile, tile)]
+                c_ref[part_of(first, i, tile), part_of(first, j, tile)] = block
+                d_ref[part_of(first, j, tile), part_of(first, i, tile)] = block.T
             low = stage[part_of(0, i, tile), part_of(0, j, tile)]
             high = stage[part_of(half, j, tile), part_of(0, i, tile)]
             low_turned, high_turned = low.T.astype(F32), high.T.astype(F32)
@@ -206,33 +204,29 @@
             d_ref[part_of(0, j, tile), part_of(half, i, tile)] = (low_turned - high).astype(BF16)
 
 
-def own_step(step, start, width, c_ref, d_ref, flat, turned, tile, base, out, parts):
+def own_step(step, start, width, c_ref, d_ref, turned, tile, base, out, parts):
     n = c_ref.shape[0]
     part = min(tile, width)
-
-    @pl.loop(0, width // step.size)
-    def _(t):
-        c = start // step.size + t
-        for s in range(n // tile):
-            cols = pl.ds(s * tile, tile)
-            products = (
-                step.ham(step.minus, c, c_ref, d_ref, cols),
-                step.ham(step.plus, c, d_ref, c_ref, cols),
-                step.pull(c, d_ref, cols),
-                step.pull(c, c_ref, cols),
-            )
+    products = (
+        lambda c, cols: step.ham(step.minus, c, c_ref, d_ref, cols),
+        lambda c, cols: step.ham(step.plus, c, d_ref, c_ref, cols),
+        lambda c, cols: step.pull(c, d_ref, cols),
+        lambda c, cols: step.pull(c, c_ref, cols),
+    )
+
+    @pl.loop(0, width // part)
+    def _(g):
+        first = start // step.size + g * (part // step.size)
+
+        @pl.loop(0, n // tile)
+        def _(s):
+            cols = part_of(0, s, tile)
             for k, product in enumerate(products):
-                flat[pl.ds(pl.multiple_of(k * width + t * step.size, step.size), step.size), cols] = product.astype(BF16)
-
-    @pl.loop(0, n // part)
-    def _(i):
-        near = pl.ds(pl.multiple_of(i * part, part), part)
-        for j in range(4 * width // part):
-            far = pl.ds(j * part, part)
-            turned[near, far] = turned_tile(flat[far, near])
+                rows = [product(first + u, cols).astype(BF16) for u in range(part // step.size)]
+                turned[cols, part_of(k * width, g, part)] = jnp.concatenate(rows, axis=0).T
 
     def finish(first, count, pass_on):
-        @pl.loop(0, count)
+        @pl.loop(0, count, unroll=4)
         def _(t):
             c = first // step.size + t
             own = pl.ds(pl.multiple_of(c * step.size, step.size), step.size)
@@ -261,43 +255,40 @@
     turn_whole(c_ref, d_ref, tile)
 
 
-def inner_kernel(counts, tile, number, rows, place, terminal, plus, minus, jump, *refs):
+def inner_kernel(counts, tile, spans, number, rows, place, terminal, plus, minus, jump, *refs):
     pieces, refs = refs[:number], refs[number:]
-    *outs, c_ref, d_ref, flat, turned, sems = refs
+    *outs, c_ref, d_ref, stage, turned, sems = refs
     out, passed = outs[0], outs[1:]
     n, width = out.shape[2], out.shape[3]
     size = plus.shape[1]
+    half = 2 * width
     if number == 1:
         fill_whole(pieces[0], c_ref, d_ref, sems, tile)
         parts = [(0, n // size, None)]
     else:
-        assemble_first(place, *pieces, c_ref, d_ref, flat, sems, tile)
-        depth = passed[0].shape[0]
-        half, chunks = 2 * width, 2 * width // depth
-        parts = []
-
-        def send_mixed(target, rows, cols, real, imag):
-            target[rows, cols] = (real + imag).astype(BF16)
-
-        def send_one(target, rows, cols, real, imag):
-            target[rows, cols] = jnp.where(place[2] == 0, real, imag).astype(BF16)
-
-        for k in range(chunks):
-            parts.append((place[2] + k * depth, depth // size, functools.partial(send_mixed, passed[k])))
-        for k in range(chunks):
-            target = passed[chunks + k]
-            parts.append((half - place[2] + k * depth, depth // size, functools.partial(send_one, target)))
+        assemble_first(place, *pieces, c_ref, d_ref, stage, turned, sems, tile)
+
+        def send_mixed(rows, cols, real, imag):
+            stage[rows, cols] = (real + imag).astype(BF16)
+
+        def send_one(rows, cols, real, imag):
+            below = pl.ds(pl.multiple_of(half + rows.start, size), size)
+            stage[below, cols] = jnp.where(place[2] == 0, real, imag).astype(BF16)
+
+        parts = [(place[2], half // size, send_mixed), (half - place[2], half // size, send_one)]
     step = Step(rows, counts, size, plus, minus, jump)
 
     def base(own, _, cols):
         return terminal[0, 0, own, cols].astype(F32), terminal[0, 1, own, cols].astype(F32)
 
-    own_step(step, place[0], width, c_ref, d_ref, flat, turned, tile, base, out, parts)
-
-
-def start_kernel(counts, tile, number, rows, place, terminal, plus, minus, jump, *refs):
+    own_step(step, place[0], width, c_ref, d_ref, turned, tile, base, out, parts)
+    if passed:
+        load_all([(stage.at[pl.ds(*span), pl.ds(0, width)], to) for span, to in zip(spans, passed)], sems)
+
+
+def start_kernel(counts, tile, spans, number, rows, place, terminal, plus, minus, jump, *refs):
     pieces, refs = refs[:number], refs[number:]
-    out, c_ref, d_ref, flat, turned, sems = refs
+    out, c_ref, d_ref, stage, turned, sems = refs
     size = plus.shape[1]
 
     @pl.when(place[1] == 1)
@@ -309,9 +300,9 @@
         if number == 1:
             fill_whole(pieces[0], c_ref, d_ref, sems, tile)
         else:
-            each = number // 4
+            each = len(spans)
             groups = [pieces[k * each : (k + 1) * each] for k in range(4)]
-            assemble_second(place, *groups, c_ref, d_ref, flat, sems, tile)
+            assemble_second(place, spans, *groups, c_ref, d_ref, stage, turned, sems, tile)
         step = Step(rows, counts, size, plus, minus, jump)
 
         def base(own, cols, _):
@@ -319,7 +310,7 @@
             return 0.5 * (first + second), 0.5 * (first - second)
 
         parts = [(0, out.shape[2] // size, None)]
-        own_step(step, place[0], out.shape[3], c_ref, d_ref, flat, turned, tile, base, out, parts)
+        own_step(step, place[0], out.shape[3], c_ref, d_ref, turned, tile, base, out, parts)
 
 
 def swapped(block, bit):
@@ -341,17 +332,21 @@
     vmem = pl.BlockSpec(memory_space=pltpu.VMEM)
     anywhere = pl.BlockSpec(memory_space=pl.ANY)
     whole_out = jax.ShapeDtypeStruct(terminal.shape, BF16)
+    spans, reached = [], 0
+    for depth in (width // 2, width // 2, width, width, width // 2, width // 2):
+        spans.append((reached, depth))
+        reached += depth
 
     def step_call(kernel, name, state_spec, k, pieces, passed):
         return pl.pallas_call(
-            functools.partial(kernel, counts, tile, len(pieces)),
+            functools.partial(kernel, counts, tile, spans, len(pieces)),
             out_shape=[whole_out] + passed,
             in_specs=[smem, smem, state_spec, vmem, vmem, vmem] + [anywhere] * len(pieces),
-            out_specs=[vmem] * (1 + len(passed)),
+            out_specs=[vmem] + [anywhere] * len(passed),
             scratch_shapes=[
                 pltpu.VMEM((n, n), BF16),
                 pltpu.VMEM((n, n), BF16),
-                pltpu.VMEM((max(4 * width, n), n), BF16),
+                pltpu.VMEM((n, n), BF16),
                 pltpu.VMEM((n, 4 * width), BF16),
                 pltpu.SemaphoreType.DMA((max(len(pieces), 6),)),
             ],
@@ -365,9 +360,9 @@
         mine = lax.dynamic_slice_in_dim(terminal[0], here, 2 * width, 1).astype(F32)
         far = swapped((mine[0] + mine[1]).astype(BF16), 2)
         far, rows = lax.optimization_barrier((far, rows))
-        chunk = jax.ShapeDtypeStruct((width, width), BF16)
+        chunks = [jax.ShapeDtypeStruct((depth, width), BF16) for _, depth in spans]
         new_fpoint, *sent = step_call(
-            inner_kernel, "inner_point", vmem, 0, [terminal, near_pair, far, swapped(far, 1)], [chunk] * 4
+            inner_kernel, "inner_point", vmem, 0, [terminal, near_pair, far, swapped(far, 1)], chunks
         )
         near, far = [], []
         for k, piece in enumerate(sent):

time: 184 us -> 172 us (0.935)
  Pallas kernels: 94.2 us -> 80.3 us
  starting transfers between devices: 12.3 us -> 19.1 us
  waiting for transfers between devices: 63.1 us -> 57.2 us
    pallas_call x2, Pallas kernels: 78.1 us -> 64.2 us  [step_call(): pl.pallas_call(functools.partial(kernel, counts, tile, spans, len(pieces)...]
    ppermute x5 -> x7, waiting for transfers between devices: 44.4 us -> 33.3 us  [shifted_down(): return lax.ppermute(block, axis, route)]
    ppermute x15 -> x21, waiting for transfers between devices: 18.7 us -> 23.9 us  [swapped(): lax.ppermute(block, 'row', [(i, i ^ bit) for i in range(lax.axis_size('ro...]
    ppermute x15 -> x21, starting transfers between devices: 5.84 us -> 10.1 us  [swapped(): lax.ppermute(block, 'row', [(i, i ^ bit) for i in range(lax.axis_size('ro...]
    ppermute x5 -> x7, starting transfers between devices: 6.43 us -> 8.99 us  [shifted_down(): return lax.ppermute(block, axis, route)]
    unnamed x42 -> x56, local copies, waits for them, and re-layouts: 8.07 us -> 8.84 us
  transfers between devices with their start and end apart: 20 -> 28, of which waited for: 8 -> 12; matrix products, arithmetic and copies ran while one was open for 6% -> 7% of each run, Pallas kernels for 9% -> 9%
where the time goes in v3:
time: 172 us; the launch traced here: 171 us
  Pallas kernels  80.3 us (47%)
  waiting for transfers between devices  57.2 us (33%)
  starting transfers between devices  19.1 us (11%)
  local copies, waits for them, and re-layouts  9.48 us (6%)
  other arithmetic  4.44 us (3%)
    pallas_call x2, Pallas kernels, step_call(): pl.pallas_call(functools.partial(kernel, counts, tile, spans, len(pieces)...  64.2 us
    ppermute x7, waiting for transfers between devices, shifted_down(): return lax.ppermute(block, axis, route)  33.3 us
    ppermute x21, waiting for transfers between devices, swapped(): lax.ppermute(block, 'row', [(i, i ^ bit) for i in range(lax.axis_size('ro...  23.9 us
    pallas_call x1, Pallas kernels, operator_tables(): pl.pallas_call(table_kernel, out_shape=[jax.ShapeDtypeStruct((2 * layers_...  16.1 us
    ppermute x21, starting transfers between devices, swapped(): lax.ppermute(block, 'row', [(i, i ^ bit) for i in range(lax.axis_size('ro...  10.1 us
    ppermute x7, starting transfers between devices, shifted_down(): return lax.ppermute(block, axis, route)  8.99 us
    unnamed x56, local copies, waits for them, and re-layouts  8.84 us
  transfers between devices with their start and end apart: 28, of which 12 were waited for; matrix products, arithmetic and copies ran while one was open for 7% of the time, Pallas kernels for 9%

profile of v3, /device:TPU:0, one launch (start us, length us, event | category | flops | bytes accessed | tf_op | source)
XLA Modules:
  0.0 171.4 jit_solution(11264049256652876137)
XLA Ops:
  0.6 0.5 collective-permute-start.2
  1.1 2.2 %dynamic-slice_convert_fusion = f32[1,2,1024,512]{3,2,1,0:T(8,128)S(1)} fusion(bf16[1,2,2048,512]{3,2,1,0:T(8,128)(2,1)} %terminal.3, s32[]{:T(128)S(6)} %select_n.15), kind=kLoop, calls=%fused_computation.2 | loop fusion | flops 1048576 | bytes 6291460 | tf_op jit(solution)/shard_map/convert_element_type | solution.py:360
  3.3 0.0 copy-start.26
  3.3 0.0 copy-start.1
  3.4 0.0 copy-start
  3.4 0.4 fusion.1
  3.7 2.6 %collective-permute-start = (bf16[1024,512]{1,0:T(8,128)(2,1)S(1)}, bf16[1024,512]{1,0:T(8,128)(2,1)}, u32[]{:S(2)}, u32[]{:S(2)}) collective-permute-start(bf16[1024,512]{1,0:T(8,128)(2,1)S(1)} %fusion.1), channel_id=1, source_target_pairs={{0,2},{1,3},{2,0},{3,1},{4,6},{5,7},{6,4},{7,5},{8,10},{9,11},{10,... | collective-permute-start | bytes 3145736 | tf_op jit(solution)/shard_map/ppermute | solution.py:317
  6.3 1.3 collective-permute-start.1
  7.6 0.6 slice.16
  8.3 2.4 %copy.9.jump = bf16[64,2,32,32]{3,2,1,0:T(8,128)(2,1)} copy(bf16[64,2,32,32]{0,3,2,1:T(8,128)(2,1)S(1)} %copy-done.1) | data formatting | bytes 524288 | tf_op args[4]
  10.7 3.9 %copy.8.ham = bf16[2,64,2,32,32]{4,3,2,1,0:T(8,128)(2,1)} copy(bf16[2,64,2,32,32]{1,4,3,2,0:T(8,128)(2,1)S(1)} %copy-done) | data formatting | bytes 1048576 | tf_op args[2]
  14.6 0.0 collective-permute-done.1
  14.6 1.3 pad_maximum_fusion.amplitudes
  15.9 16.1 %operator_tables.1 = (s32[9,64]{1,0:T(8,128)}, bf16[64,32,64]{2,1,0:T(8,128)(2,1)}, bf16[64,32,224]{2,1,0:T(8,128)(2,1)}, bf16[64,32,224]{2,1,0:T(8,128)(2,1)}, ...) custom-call(s32[2,64]{1,0:T(2,128)} %ham_cols.1, s32[2,64]{1,0:T(2,128)} %jump_cols.1, ...), custom_call_target="tpu_custom_call" | custom-call | flops 1000000000 | bytes 10485760 | tf_op jit(solution)/shard_map/operator_tables/pallas_call | solution.py:74
  32.0 0.0 collective-permute-done.refs_2_
  32.0 0.2 collective-permute-start.3
  32.2 0.6 pad_add_fusion.place
  32.8 2.1 %collective-permute-done.3.refs_3_ = bf16[1024,512]{1,0:T(8,128)(2,1)S(1)} collective-permute-done((bf16[1024,512]{1,0:T(8,128)(2,1)}, bf16[1024,512]{1,0:T(8,128)(2,1)S(1)}, u32[]{:S(2)}, u32[]{:S(2)}) %collective-permute-start.3) | collective-permute-done | bytes 1048608 | tf_op jit(solution)/shard_map/ppermute | solution.py:317
  34.9 0.0 collective-permute-done.2.refs_1_
  34.9 1.0 copy-done.2
  35.9 33.8 %inner_point.1 = (bf16[1,2,2048,512]{3,2,1,0:T(8,128)(2,1)}, bf16[256,512]{1,0:T(8,128)(2,1)}, bf16[256,512]{1,0:T(8,128)(2,1)}, bf16[512,512]{1,0:T(8,128)(2,1)...) custom-call(s32[9,64]{1,0:T(8,128)} %get-tuple-element.22.rows, ...), custom_call_target="tpu_custom_call" | custom-call | flops 20000000000 | bytes 16777216 | tf_op jit(solution)/shard_map/inner_point/pallas_call | solution.py:341
  69.7 1.3 collective-permute-start.5
  71.0 1.3 collective-permute-start.4
  72.3 9.2 %collective-permute-done.5.refs_1_ = bf16[256,512]{1,0:T(8,128)(2,1)S(1)} collective-permute-done((bf16[256,512]{1,0:T(8,128)(2,1)}, bf16[256,512]{1,0:T(8,128)(2,1)S(1)}, u32[]{:S(2)}, u32[]{:S(2)}) %collective-permute-start.5) | collective-permute-done | bytes 262176 | tf_op jit(solution)/shard_map/ppermute | solution.py:17
  81.5 1.3 collective-permute-start.7
  82.8 4.3 %collective-permute-done.4.refs_0_ = bf16[256,512]{1,0:T(8,128)(2,1)S(1)} collective-permute-done((bf16[256,512]{1,0:T(8,128)(2,1)}, bf16[256,512]{1,0:T(8,128)(2,1)S(1)}, u32[]{:S(2)}, u32[]{:S(2)}) %collective-permute-start.4) | collective-permute-done | bytes 262176 | tf_op jit(solution)/shard_map/ppermute | solution.py:17
  87.1 0.2 collective-permute-start.16
  87.3 1.3 collective-permute-start.6
  88.6 1.9 %collective-permute-start.17 = (bf16[256,512]{1,0:T(8,128)(2,1)S(1)}, bf16[256,512]{1,0:T(8,128)(2,1)S(1)}, u32[]{:S(2)}, u32[]{:S(2)}) collective-permute-start(bf16[256,512]{1,0:T(8,128)(2,1)S(1)} %collective-permute-done.5.refs_1_), channel_id=1, source_target_pairs={{0,2},{1,3},{2,0},{3,1},{4,6},{5,7},{6,4},{7,5},{8,10},{9,11},{10,... | collective-permute-start | bytes 786440 | tf_op jit(solution)/shard_map/ppermute | solution.py:317
  90.5 0.0 collective-permute-start.10
  90.5 5.9 %collective-permute-done.16.refs_12_ = bf16[256,512]{1,0:T(8,128)(2,1)S(1)} collective-permute-done((bf16[256,512]{1,0:T(8,128)(2,1)S(1)}, bf16[256,512]{1,0:T(8,128)(2,1)S(1)}, u32[]{:S(2)}, u32[]{:S(2)}) %collective-permute-start.16) | collective-permute-done | bytes 262176 | tf_op jit(solution)/shard_map/ppermute | solution.py:317
  96.4 0.0 collective-permute-start.11
  96.4 3.7 %collective-permute-done.17.refs_13_ = bf16[256,512]{1,0:T(8,128)(2,1)S(1)} collective-permute-done((bf16[256,512]{1,0:T(8,128)(2,1)S(1)}, bf16[256,512]{1,0:T(8,128)(2,1)S(1)}, u32[]{:S(2)}, u32[]{:S(2)}) %collective-permute-start.17) | collective-permute-done | bytes 262176 | tf_op jit(solution)/shard_map/ppermute | solution.py:317
  100.1 0.0 collective-permute-start.22
  100.1 0.0 collective-permute-done.7.refs_3_
  100.1 0.5 collective-permute-start.23
  100.6 0.0 collective-permute-done.10.refs_6_
  100.6 1.3 collective-permute-start.9
  101.9 0.0 collective-permute-done.11.refs_7_
  101.9 0.3 collective-permute-start.19
  102.3 7.5 %collective-permute-done.6.refs_2_ = bf16[512,512]{1,0:T(8,128)(2,1)S(1)} collective-permute-done((bf16[512,512]{1,0:T(8,128)(2,1)}, bf16[512,512]{1,0:T(8,128)(2,1)S(1)}, u32[]{:S(2)}, u32[]{:S(2)}) %collective-permute-start.6) | collective-permute-done | bytes 524320 | tf_op jit(solution)/shard_map/ppermute | solution.py:17
  109.7 0.0 collective-permute-start.13
  109.8 0.2 collective-permute-start.18
  110.0 0.5 copy-done.16
  110.5 0.5 collective-permute-start.12
  111.0 3.7 %collective-permute-done.9.refs_5_ = bf16[256,512]{1,0:T(8,128)(2,1)S(1)} collective-permute-done((bf16[256,512]{1,0:T(8,128)(2,1)}, bf16[256,512]{1,0:T(8,128)(2,1)S(1)}, u32[]{:S(2)}, u32[]{:S(2)}) %collective-permute-start.9) | collective-permute-done | bytes 262176 | tf_op jit(solution)/shard_map/ppermute | solution.py:17
  114.7 1.3 collective-permute-start.8
  116.0 8.5 %collective-permute-done.8.refs_4_ = bf16[256,512]{1,0:T(8,128)(2,1)S(1)} collective-permute-done((bf16[256,512]{1,0:T(8,128)(2,1)}, bf16[256,512]{1,0:T(8,128)(2,1)S(1)}, u32[]{:S(2)}, u32[]{:S(2)}) %collective-permute-start.8) | collective-permute-done | bytes 262176 | tf_op jit(solution)/shard_map/ppermute | solution.py:17
  124.5 0.3 collective-permute-start.21
  124.8 0.0 collective-permute-done.19.refs_15_
  124.8 0.0 collective-permute-done.13.refs_9_
  124.8 1.8 %collective-permute-start.20 = (bf16[256,512]{1,0:T(8,128)(2,1)S(1)}, bf16[256,512]{1,0:T(8,128)(2,1)S(1)}, u32[]{:S(2)}, u32[]{:S(2)}) collective-permute-start(bf16[256,512]{1,0:T(8,128)(2,1)S(1)} %collective-permute-done.8.refs_4_), channel_id=1, source_target_pairs={{0,2},{1,3},{2,0},{3,1},{4,6},{5,7},{6,4},{7,5},{8,10},{9,11},{10,... | collective-permute-start | bytes 786440 | tf_op jit(solution)/shard_map/ppermute | solution.py:317
  126.6 1.4 collective-permute-done.18.refs_14_
  128.0 0.5 collective-permute-start.24
  128.5 5.2 %collective-permute-done.21.refs_17_ = bf16[256,512]{1,0:T(8,128)(2,1)S(1)} collective-permute-done((bf16[256,512]{1,0:T(8,128)(2,1)S(1)}, bf16[256,512]{1,0:T(8,128)(2,1)S(1)}, u32[]{:S(2)}, u32[]{:S(2)}) %collective-permute-start.21) | collective-permute-done | bytes 262176 | tf_op jit(solution)/shard_map/ppermute | solution.py:317
  133.8 0.0 collective-permute-done.15.refs_11_
  133.8 0.5 collective-permute-start.27
  134.3 4.1 %collective-permute-done.20.refs_16_ = bf16[256,512]{1,0:T(8,128)(2,1)S(1)} collective-permute-done((bf16[256,512]{1,0:T(8,128)(2,1)S(1)}, bf16[256,512]{1,0:T(8,128)(2,1)S(1)}, u32[]{:S(2)}, u32[]{:S(2)}) %collective-permute-start.20) | collective-permute-done | bytes 262176 | tf_op jit(solution)/shard_map/ppermute | solution.py:317
  138.4 0.0 collective-permute-done.27.refs_23_
  138.4 1.5 collective-permute-done.26.refs_22_
  139.9 0.8 copy-done.10
  140.8 0.0 copy-done.25
  140.9 0.1 copy-done.9
  141.0 30.4 %left_end.1 = bf16[1,2,2048,512]{3,2,1,0:T(8,128)(2,1)} custom-call(s32[9,64]{1,0:T(8,128)} %get-tuple-element.22.rows, s32[4]{0:T(128)} %pad_add_fusion.place, bf16[1,2,2048,512]{3,2,1,0:T(8,128)(2,1)} %terminal.3, bf16[64,32,224]{2,1,0:T(8,128)(2,1)} %get-tuple-element.23.plus, bf16[64,32,224]{2,1,0:T(8,128)(2,1)} %get-tuple-element.24.minus, ...), custom_call_target="tpu_custom_call" | custom-call | flops 20000000000 | bytes 16777216 | tf_op jit(solution)/shard_map/left_end/pallas_call | solution.py:341
  (56 shorter events, 0.1 us)
Async XLA Ops:
  0.6 34.3 %collective-permute-start.2 = (bf16[1,2,2048,512]{3,2,1,0:T(8,128)(2,1)}, bf16[1,2,2048,512]{3,2,1,0:T(8,128)(2,1)}, u32[]{:S(2)}, u32[]{:S(2)}) collective-permute-start(bf16[1,2,2048,512]{3,2,1,0:T(8,128)(2,1)} %terminal.3), channel_id=1, source_target_pairs={{0,1},{1,0},{2,3},{3,2},{4,5},{5,4},{6,7},{7,6},{8,9},{9,8},{10,11... | collective-permute-start | bytes 12582920 | tf_op jit(solution)/shard_map/ppermute | solution.py:317
  3.3 3.0 %copy-start.26 = (f32[1,2]{1,0:T(1,128)S(1)}, f32[1,2]{1,0:T(1,128)}, u32[]{:S(2)}) copy-start(f32[1,2]{1,0:T(1,128)} %param.7) | copy-start | bytes 28
  3.3 4.9 %copy-start.1 = (bf16[64,2,32,32]{0,3,2,1:T(8,128)(2,1)S(1)}, bf16[64,2,32,32]{0,3,2,1:T(8,128)(2,1)}, u32[]{:S(2)}) copy-start(bf16[64,2,32,32]{0,3,2,1:T(8,128)(2,1)} %param.10) | copy-start | bytes 786436
  3.4 7.3 %copy-start = (bf16[2,64,2,32,32]{1,4,3,2,0:T(8,128)(2,1)S(1)}, bf16[2,64,2,32,32]{1,4,3,2,0:T(8,128)(2,1)}, u32[]{:S(2)}) copy-start(bf16[2,64,2,32,32]{1,4,3,2,0:T(8,128)(2,1)} %param.8) | copy-start | bytes 1572868
  3.7 28.2 %collective-permute-start = (bf16[1024,512]{1,0:T(8,128)(2,1)S(1)}, bf16[1024,512]{1,0:T(8,128)(2,1)}, u32[]{:S(2)}, u32[]{:S(2)}) collective-permute-start(bf16[1024,512]{1,0:T(8,128)(2,1)S(1)} %fusion.1), channel_id=1, source_target_pairs={{0,2},{1,3},{2,0},{3,1},{4,6},{5,7},{6,4},{7,5},{8,10},{9,11},{10,... | collective-permute-start | bytes 3145736 | tf_op jit(solution)/shard_map/ppermute | solution.py:317
  6.3 8.2 %collective-permute-start.1 = (f32[1,2]{1,0:T(1,128)S(1)}, f32[1,2]{1,0:T(1,128)S(1)}, u32[]{:S(2)}, u32[]{:S(2)}) collective-permute-start(f32[1,2]{1,0:T(1,128)S(1)} %copy-done.26), channel_id=1, source_target_pairs={{4,0},{8,4},{12,8},{5,1},{9,5},{13,9},{6,2},{10,6},{14,10},{7,3},{... | collective-permute-start | bytes 32 | tf_op jit(solution)/shard_map/ppermute | solution.py:17
  32.0 2.9 %collective-permute-start.3 = (bf16[1024,512]{1,0:T(8,128)(2,1)}, bf16[1024,512]{1,0:T(8,128)(2,1)S(1)}, u32[]{:S(2)}, u32[]{:S(2)}) collective-permute-start(bf16[1024,512]{1,0:T(8,128)(2,1)} %collective-permute-done.refs_2_), channel_id=1, source_target_pairs={{0,1},{1,0},{2,3},{3,2},{4,5},{5,4},{6,7},{7,6},{8,9},{9,8},{10,11... | collective-permute-start | bytes 3145736 | tf_op jit(solution)/shard_map/ppermute | solution.py:317
  34.9 1.0 copy-start.2
  69.7 11.8 %collective-permute-start.5 = (bf16[256,512]{1,0:T(8,128)(2,1)}, bf16[256,512]{1,0:T(8,128)(2,1)S(1)}, u32[]{:S(2)}, u32[]{:S(2)}) collective-permute-start(bf16[256,512]{1,0:T(8,128)(2,1)} %get-tuple-element.30), channel_id=1, source_target_pairs={{4,0},{8,4},{12,8},{5,1},{9,5},{13,9},{6,2},{10,6},{14,10},{7,3},{... | collective-permute-start | bytes 786440 | tf_op jit(solution)/shard_map/ppermute | solution.py:17
  71.0 16.2 %collective-permute-start.4 = (bf16[256,512]{1,0:T(8,128)(2,1)}, bf16[256,512]{1,0:T(8,128)(2,1)S(1)}, u32[]{:S(2)}, u32[]{:S(2)}) collective-permute-start(bf16[256,512]{1,0:T(8,128)(2,1)} %get-tuple-element.29), channel_id=1, source_target_pairs={{4,0},{8,4},{12,8},{5,1},{9,5},{13,9},{6,2},{10,6},{14,10},{7,3},{... | collective-permute-start | bytes 786440 | tf_op jit(solution)/shard_map/ppermute | solution.py:17
  81.5 59.3 %copy-start.11 = (bf16[256,512]{1,0:T(8,128)(2,1)}, bf16[256,512]{1,0:T(8,128)(2,1)S(1)}, u32[]{:S(2)}) copy-start(bf16[256,512]{1,0:T(8,128)(2,1)S(1)} %collective-permute-done.5.refs_1_) | copy-start | bytes 786436
  81.5 18.6 %collective-permute-start.7 = (bf16[512,512]{1,0:T(8,128)(2,1)}, bf16[512,512]{1,0:T(8,128)(2,1)S(1)}, u32[]{:S(2)}, u32[]{:S(2)}) collective-permute-start(bf16[512,512]{1,0:T(8,128)(2,1)} %get-tuple-element.34), channel_id=1, source_target_pairs={{4,0},{8,4},{12,8},{5,1},{9,5},{13,9},{6,2},{10,6},{14,10},{7,3},{... | collective-permute-start | bytes 1572872 | tf_op jit(solution)/shard_map/ppermute | solution.py:17
  87.1 14.8 %copy-start.12 = (bf16[256,512]{1,0:T(8,128)(2,1)}, bf16[256,512]{1,0:T(8,128)(2,1)S(1)}, u32[]{:S(2)}) copy-start(bf16[256,512]{1,0:T(8,128)(2,1)S(1)} %collective-permute-done.4.refs_0_) | copy-start | bytes 786436
  87.1 9.2 %collective-permute-start.16 = (bf16[256,512]{1,0:T(8,128)(2,1)S(1)}, bf16[256,512]{1,0:T(8,128)(2,1)S(1)}, u32[]{:S(2)}, u32[]{:S(2)}) collective-permute-start(bf16[256,512]{1,0:T(8,128)(2,1)S(1)} %collective-permute-done.4.refs_0_), channel_id=1, source_target_pairs={{0,2},{1,3},{2,0},{3,1},{4,6},{5,7},{6,4},{7,5},{8,10},{9,11},{10,... | collective-permute-start | bytes 786440 | tf_op jit(solution)/shard_map/ppermute | solution.py:317
  87.3 22.5 %collective-permute-start.6 = (bf16[512,512]{1,0:T(8,128)(2,1)}, bf16[512,512]{1,0:T(8,128)(2,1)S(1)}, u32[]{:S(2)}, u32[]{:S(2)}) collective-permute-start(bf16[512,512]{1,0:T(8,128)(2,1)} %get-tuple-element.32), channel_id=1, source_target_pairs={{4,0},{8,4},{12,8},{5,1},{9,5},{13,9},{6,2},{10,6},{14,10},{7,3},{... | collective-permute-start | bytes 1572872 | tf_op jit(solution)/shard_map/ppermute | solution.py:17
  88.6 11.5 %collective-permute-start.17 = (bf16[256,512]{1,0:T(8,128)(2,1)S(1)}, bf16[256,512]{1,0:T(8,128)(2,1)S(1)}, u32[]{:S(2)}, u32[]{:S(2)}) collective-permute-start(bf16[256,512]{1,0:T(8,128)(2,1)S(1)} %collective-permute-done.5.refs_1_), channel_id=1, source_target_pairs={{0,2},{1,3},{2,0},{3,1},{4,6},{5,7},{6,4},{7,5},{8,10},{9,11},{10,... | collective-permute-start | bytes 786440 | tf_op jit(solution)/shard_map/ppermute | solution.py:317
  90.5 10.1 %collective-permute-start.10 = (bf16[256,512]{1,0:T(8,128)(2,1)S(1)}, bf16[256,512]{1,0:T(8,128)(2,1)S(1)}, u32[]{:S(2)}, u32[]{:S(2)}) collective-permute-start(bf16[256,512]{1,0:T(8,128)(2,1)S(1)} %collective-permute-done.4.refs_0_), channel_id=1, source_target_pairs={{0,1},{1,0},{2,3},{3,2},{4,5},{5,4},{6,7},{7,6},{8,9},{9,8},{10,11... | collective-permute-start | bytes 786440 | tf_op jit(solution)/shard_map/ppermute | solution.py:317
  96.4 13.4 %copy-start.13 = (bf16[256,512]{1,0:T(8,128)(2,1)}, bf16[256,512]{1,0:T(8,128)(2,1)S(1)}, u32[]{:S(2)}) copy-start(bf16[256,512]{1,0:T(8,128)(2,1)S(1)} %collective-permute-done.16.refs_12_) | copy-start | bytes 786436
  96.4 5.5 %collective-permute-start.11 = (bf16[256,512]{1,0:T(8,128)(2,1)S(1)}, bf16[256,512]{1,0:T(8,128)(2,1)}, u32[]{:S(2)}, u32[]{:S(2)}) collective-permute-start(bf16[256,512]{1,0:T(8,128)(2,1)S(1)} %collective-permute-done.5.refs_1_), channel_id=1, source_target_pairs={{0,1},{1,0},{2,3},{3,2},{4,5},{5,4},{6,7},{7,6},{8,9},{9,8},{10,11... | collective-permute-start | bytes 786440 | tf_op jit(solution)/shard_map/ppermute | solution.py:317
  100.1 9.9 %copy-start.14 = (bf16[256,512]{1,0:T(8,128)(2,1)}, bf16[256,512]{1,0:T(8,128)(2,1)S(1)}, u32[]{:S(2)}) copy-start(bf16[256,512]{1,0:T(8,128)(2,1)S(1)} %collective-permute-done.17.refs_13_) | copy-start | bytes 786436
  100.1 9.7 %collective-permute-start.22 = (bf16[256,512]{1,0:T(8,128)(2,1)S(1)}, bf16[256,512]{1,0:T(8,128)(2,1)S(1)}, u32[]{:S(2)}, u32[]{:S(2)}) collective-permute-start(bf16[256,512]{1,0:T(8,128)(2,1)S(1)} %collective-permute-done.16.refs_12_), channel_id=1, source_target_pairs={{0,1},{1,0},{2,3},{3,2},{4,5},{5,4},{6,7},{7,6},{8,9},{9,8},{10,11... | collective-permute-start | bytes 786440 | tf_op jit(solution)/shard_map/ppermute | solution.py:317
  100.1 40.7 %copy-start.3 = (bf16[512,512]{1,0:T(8,128)(2,1)}, bf16[512,512]{1,0:T(8,128)(2,1)S(1)}, u32[]{:S(2)}) copy-start(bf16[512,512]{1,0:T(8,128)(2,1)S(1)} %collective-permute-done.7.refs_3_) | copy-start | bytes 1572868
  100.1 10.4 %collective-permute-start.23 = (bf16[256,512]{1,0:T(8,128)(2,1)S(1)}, bf16[256,512]{1,0:T(8,128)(2,1)S(1)}, u32[]{:S(2)}, u32[]{:S(2)}) collective-permute-start(bf16[256,512]{1,0:T(8,128)(2,1)S(1)} %collective-permute-done.17.refs_13_), channel_id=1, source_target_pairs={{0,1},{1,0},{2,3},{3,2},{4,5},{5,4},{6,7},{7,6},{8,9},{9,8},{10,11... | collective-permute-start | bytes 786440 | tf_op jit(solution)/shard_map/ppermute | solution.py:317
  100.6 9.1 %copy-start.15 = (bf16[256,512]{1,0:T(8,128)(2,1)}, bf16[256,512]{1,0:T(8,128)(2,1)S(1)}, u32[]{:S(2)}) copy-start(bf16[256,512]{1,0:T(8,128)(2,1)S(1)} %collective-permute-done.10.refs_6_) | copy-start | bytes 786436
  100.6 14.1 %collective-permute-start.9 = (bf16[256,512]{1,0:T(8,128)(2,1)}, bf16[256,512]{1,0:T(8,128)(2,1)S(1)}, u32[]{:S(2)}, u32[]{:S(2)}) collective-permute-start(bf16[256,512]{1,0:T(8,128)(2,1)} %get-tuple-element.38), channel_id=1, source_target_pairs={{4,0},{8,4},{12,8},{5,1},{9,5},{13,9},{6,2},{10,6},{14,10},{7,3},{... | collective-permute-start | bytes 786440 | tf_op jit(solution)/shard_map/ppermute | solution.py:17
  101.9 22.9 %collective-permute-start.19 = (bf16[512,512]{1,0:T(8,128)(2,1)S(1)}, bf16[512,512]{1,0:T(8,128)(2,1)S(1)}, u32[]{:S(2)}, u32[]{:S(2)}) collective-permute-start(bf16[512,512]{1,0:T(8,128)(2,1)S(1)} %collective-permute-done.7.refs_3_), channel_id=1, source_target_pairs={{0,2},{1,3},{2,0},{3,1},{4,6},{5,7},{6,4},{7,5},{8,10},{9,11},{10,... | collective-permute-start | bytes 1572872 | tf_op jit(solution)/shard_map/ppermute | solution.py:317
  109.7 31.1 %copy-start.4 = (bf16[512,512]{1,0:T(8,128)(2,1)}, bf16[512,512]{1,0:T(8,128)(2,1)S(1)}, u32[]{:S(2)}) copy-start(bf16[512,512]{1,0:T(8,128)(2,1)S(1)} %collective-permute-done.6.refs_2_) | copy-start | bytes 1572868
  109.7 15.1 %collective-permute-start.13 = (bf16[512,512]{1,0:T(8,128)(2,1)S(1)}, bf16[512,512]{1,0:T(8,128)(2,1)S(1)}, u32[]{:S(2)}, u32[]{:S(2)}) collective-permute-start(bf16[512,512]{1,0:T(8,128)(2,1)S(1)} %collective-permute-done.7.refs_3_), channel_id=1, source_target_pairs={{0,1},{1,0},{2,3},{3,2},{4,5},{5,4},{6,7},{7,6},{8,9},{9,8},{10,11... | collective-permute-start | bytes 1572872 | tf_op jit(solution)/shard_map/ppermute | solution.py:317
  109.8 0.8 copy-start.16
  109.8 18.2 %collective-permute-start.18 = (bf16[512,512]{1,0:T(8,128)(2,1)S(1)}, bf16[512,512]{1,0:T(8,128)(2,1)S(1)}, u32[]{:S(2)}, u32[]{:S(2)}) collective-permute-start(bf16[512,512]{1,0:T(8,128)(2,1)S(1)} %collective-permute-done.6.refs_2_), channel_id=1, source_target_pairs={{0,2},{1,3},{2,0},{3,1},{4,6},{5,7},{6,4},{7,5},{8,10},{9,11},{10,... | collective-permute-start | bytes 1572872 | tf_op jit(solution)/shard_map/ppermute | solution.py:317
  110.5 16.1 %copy-start.17 = (bf16[256,512]{1,0:T(8,128)(2,1)}, bf16[256,512]{1,0:T(8,128)(2,1)S(1)}, u32[]{:S(2)}) copy-start(bf16[256,512]{1,0:T(8,128)(2,1)S(1)} %collective-permute-done.23.refs_19_) | copy-start | bytes 786436
  110.5 17.5 %collective-permute-start.12 = (bf16[512,512]{1,0:T(8,128)(2,1)S(1)}, bf16[512,512]{1,0:T(8,128)(2,1)S(1)}, u32[]{:S(2)}, u32[]{:S(2)}) collective-permute-start(bf16[512,512]{1,0:T(8,128)(2,1)S(1)} %collective-permute-done.6.refs_2_), channel_id=1, source_target_pairs={{0,1},{1,0},{2,3},{3,2},{4,5},{5,4},{6,7},{7,6},{8,9},{9,8},{10,11... | collective-permute-start | bytes 1572872 | tf_op jit(solution)/shard_map/ppermute | solution.py:317
  114.7 26.0 %copy-start.18 = (bf16[256,512]{1,0:T(8,128)(2,1)}, bf16[256,512]{1,0:T(8,128)(2,1)S(1)}, u32[]{:S(2)}) copy-start(bf16[256,512]{1,0:T(8,128)(2,1)S(1)} %collective-permute-done.9.refs_5_) | copy-start | bytes 786436
  114.7 9.8 %collective-permute-start.8 = (bf16[256,512]{1,0:T(8,128)(2,1)}, bf16[256,512]{1,0:T(8,128)(2,1)S(1)}, u32[]{:S(2)}, u32[]{:S(2)}) collective-permute-start(bf16[256,512]{1,0:T(8,128)(2,1)} %get-tuple-element.36), channel_id=1, source_target_pairs={{4,0},{8,4},{12,8},{5,1},{9,5},{13,9},{6,2},{10,6},{14,10},{7,3},{... | collective-permute-start | bytes 786440 | tf_op jit(solution)/shard_map/ppermute | solution.py:17
  124.5 16.3 %copy-start.19 = (bf16[256,512]{1,0:T(8,128)(2,1)}, bf16[256,512]{1,0:T(8,128)(2,1)S(1)}, u32[]{:S(2)}) copy-start(bf16[256,512]{1,0:T(8,128)(2,1)S(1)} %collective-permute-done.8.refs_4_) | copy-start | bytes 786436
  124.5 9.2 %collective-permute-start.21 = (bf16[256,512]{1,0:T(8,128)(2,1)S(1)}, bf16[256,512]{1,0:T(8,128)(2,1)S(1)}, u32[]{:S(2)}, u32[]{:S(2)}) collective-permute-start(bf16[256,512]{1,0:T(8,128)(2,1)S(1)} %collective-permute-done.9.refs_5_), channel_id=1, source_target_pairs={{0,2},{1,3},{2,0},{3,1},{4,6},{5,7},{6,4},{7,5},{8,10},{9,11},{10,... | collective-permute-start | bytes 786440 | tf_op jit(solution)/shard_map/ppermute | solution.py:317
  124.8 16.0 %copy-start.5 = (bf16[512,512]{1,0:T(8,128)(2,1)}, bf16[512,512]{1,0:T(8,128)(2,1)S(1)}, u32[]{:S(2)}) copy-start(bf16[512,512]{1,0:T(8,128)(2,1)S(1)} %collective-permute-done.19.refs_15_) | copy-start | bytes 1572868
  124.8 9.0 %collective-permute-start.15 = (bf16[256,512]{1,0:T(8,128)(2,1)S(1)}, bf16[256,512]{1,0:T(8,128)(2,1)S(1)}, u32[]{:S(2)}, u32[]{:S(2)}) collective-permute-start(bf16[256,512]{1,0:T(8,128)(2,1)S(1)} %collective-permute-done.9.refs_5_), channel_id=1, source_target_pairs={{0,1},{1,0},{2,3},{3,2},{4,5},{5,4},{6,7},{7,6},{8,9},{9,8},{10,11... | collective-permute-start | bytes 786440 | tf_op jit(solution)/shard_map/ppermute | solution.py:317
  124.8 16.0 %copy-start.6 = (bf16[512,512]{1,0:T(8,128)(2,1)}, bf16[512,512]{1,0:T(8,128)(2,1)S(1)}, u32[]{:S(2)}) copy-start(bf16[512,512]{1,0:T(8,128)(2,1)S(1)} %collective-permute-done.13.refs_9_) | copy-start | bytes 1572868
  124.8 13.5 %collective-permute-start.20 = (bf16[256,512]{1,0:T(8,128)(2,1)S(1)}, bf16[256,512]{1,0:T(8,128)(2,1)S(1)}, u32[]{:S(2)}, u32[]{:S(2)}) collective-permute-start(bf16[256,512]{1,0:T(8,128)(2,1)S(1)} %collective-permute-done.8.refs_4_), channel_id=1, source_target_pairs={{0,2},{1,3},{2,0},{3,1},{4,6},{5,7},{6,4},{7,5},{8,10},{9,11},{10,... | collective-permute-start | bytes 786440 | tf_op jit(solution)/shard_map/ppermute | solution.py:317
  128.0 12.9 %copy-start.7 = (bf16[512,512]{1,0:T(8,128)(2,1)}, bf16[512,512]{1,0:T(8,128)(2,1)S(1)}, u32[]{:S(2)}) copy-start(bf16[512,512]{1,0:T(8,128)(2,1)S(1)} %collective-permute-done.18.refs_14_) | copy-start | bytes 1572868
  128.0 11.9 %collective-permute-start.25 = (bf16[512,512]{1,0:T(8,128)(2,1)S(1)}, bf16[512,512]{1,0:T(8,128)(2,1)S(1)}, u32[]{:S(2)}, u32[]{:S(2)}) collective-permute-start(bf16[512,512]{1,0:T(8,128)(2,1)S(1)} %collective-permute-done.19.refs_15_), channel_id=1, source_target_pairs={{0,1},{1,0},{2,3},{3,2},{4,5},{5,4},{6,7},{7,6},{8,9},{9,8},{10,11... | collective-permute-start | bytes 1572872 | tf_op jit(solution)/shard_map/ppermute | solution.py:317
  128.0 12.9 %copy-start.8 = (bf16[512,512]{1,0:T(8,128)(2,1)}, bf16[512,512]{1,0:T(8,128)(2,1)S(1)}, u32[]{:S(2)}) copy-start(bf16[512,512]{1,0:T(8,128)(2,1)S(1)} %collective-permute-done.12.refs_8_) | copy-start | bytes 1572868
  128.0 11.9 %collective-permute-start.24 = (bf16[512,512]{1,0:T(8,128)(2,1)S(1)}, bf16[512,512]{1,0:T(8,128)(2,1)S(1)}, u32[]{:S(2)}, u32[]{:S(2)}) collective-permute-start(bf16[512,512]{1,0:T(8,128)(2,1)S(1)} %collective-permute-done.18.refs_14_), channel_id=1, source_target_pairs={{0,1},{1,0},{2,3},{3,2},{4,5},{5,4},{6,7},{7,6},{8,9},{9,8},{10,11... | collective-permute-start | bytes 1572872 | tf_op jit(solution)/shard_map/ppermute | solution.py:317
  133.8 7.0 %copy-start.20 = (bf16[256,512]{1,0:T(8,128)(2,1)}, bf16[256,512]{1,0:T(8,128)(2,1)S(1)}, u32[]{:S(2)}) copy-start(bf16[256,512]{1,0:T(8,128)(2,1)S(1)} %collective-permute-done.21.refs_17_) | copy-start | bytes 786436
  133.8 4.6 %collective-permute-start.14 = (bf16[256,512]{1,0:T(8,128)(2,1)S(1)}, bf16[256,512]{1,0:T(8,128)(2,1)S(1)}, u32[]{:S(2)}, u32[]{:S(2)}) collective-permute-start(bf16[256,512]{1,0:T(8,128)(2,1)S(1)} %collective-permute-done.8.refs_4_), channel_id=1, source_target_pairs={{0,1},{1,0},{2,3},{3,2},{4,5},{5,4},{6,7},{7,6},{8,9},{9,8},{10,11... | collective-permute-start | bytes 786440 | tf_op jit(solution)/shard_map/ppermute | solution.py:317
  133.8 7.0 %copy-start.21 = (bf16[256,512]{1,0:T(8,128)(2,1)}, bf16[256,512]{1,0:T(8,128)(2,1)S(1)}, u32[]{:S(2)}) copy-start(bf16[256,512]{1,0:T(8,128)(2,1)S(1)} %collective-permute-done.15.refs_11_) | copy-start | bytes 786436
  133.8 4.6 %collective-permute-start.27 = (bf16[256,512]{1,0:T(8,128)(2,1)S(1)}, bf16[256,512]{1,0:T(8,128)(2,1)S(1)}, u32[]{:S(2)}, u32[]{:S(2)}) collective-permute-start(bf16[256,512]{1,0:T(8,128)(2,1)S(1)} %collective-permute-done.21.refs_17_), channel_id=1, source_target_pairs={{0,1},{1,0},{2,3},{3,2},{4,5},{5,4},{6,7},{7,6},{8,9},{9,8},{10,11... | collective-permute-start | bytes 786440 | tf_op jit(solution)/shard_map/ppermute | solution.py:317
  138.4 2.4 %copy-start.22 = (bf16[256,512]{1,0:T(8,128)(2,1)}, bf16[256,512]{1,0:T(8,128)(2,1)S(1)}, u32[]{:S(2)}) copy-start(bf16[256,512]{1,0:T(8,128)(2,1)S(1)} %collective-permute-done.20.refs_16_) | copy-start | bytes 786436
  138.4 1.5 collective-permute-start.26
  138.4 2.4 %copy-start.23 = (bf16[256,512]{1,0:T(8,128)(2,1)}, bf16[256,512]{1,0:T(8,128)(2,1)S(1)}, u32[]{:S(2)}) copy-start(bf16[256,512]{1,0:T(8,128)(2,1)S(1)} %collective-permute-done.14.refs_10_) | copy-start | bytes 786436
  138.4 2.4 %copy-start.24 = (bf16[256,512]{1,0:T(8,128)(2,1)}, bf16[256,512]{1,0:T(8,128)(2,1)S(1)}, u32[]{:S(2)}) copy-start(bf16[256,512]{1,0:T(8,128)(2,1)S(1)} %collective-permute-done.27.refs_23_) | copy-start | bytes 786436
  139.9 0.9 copy-start.25
  139.9 1.1 copy-start.9
  139.9 0.8 copy-start.10

commit v4 on v3

v4 whole, which is shorter than its diff:
```python
import functools

import jax
import jax.numpy as jnp
from jax import lax
from jax.experimental import pallas as pl
from jax.experimental.pallas import tpu as pltpu
from jax.sharding import PartitionSpec as P

time_step = 0.2
F32 = jnp.float32
BF16 = jnp.bfloat16


def shifted_down(block, axis):
    route = [(i, i - 1) for i in range(1, lax.axis_size(axis))]
    return lax.ppermute(block, axis, route)


def table_kernel(ham_cols, jump_cols, amplitudes, ham, jump, rows, jump_row, *tables):
    layers_h, count = ham_cols.shape
    layers_j = jump_cols.shape[0]
    size = ham.shape[-1]
    crossed = [(k, other) for k in range(layers_j) for other in range(layers_j) if k != other]
    first_k = 2 * layers_h
    first_j = first_k + 1 + len(crossed)

    @pl.loop(0, count)
    def _(b):
        for k in range(layers_h):
            rows[k, b] = ham_cols[k, b] * size
            rows[layers_h + k, ham_cols[k, b]] = b * size
        for k in range(layers_j):
            rows[first_j + k, jump_cols[k, b]] = b * size

    @pl.loop(0, count, unroll=2)
    def _(c):
        came_h = [rows[layers_h + k, c] // size for k in range(layers_h)]
        came_j = [rows[first_j + k, c] // size for k in range(layers_j)]
        rows[first_k, c] = c * size
        for at, (k, other) in enumerate(crossed):
            rows[first_k + 1 + at, c] = jump_cols[other, came_j[k]] * size

        def ham_row(term):
            parts = [ham[term, c, k].astype(F32) for k in range(layers_h)]
            parts += [ham[term, came_h[k], k].astype(F32).T for k in range(layers_h)]
            return jnp.concatenate(parts, axis=1)

        turned = [jump[came_j[k], k].astype(F32).T.astype(BF16) for k in range(layers_j)]
        jump_row[c] = jnp.concatenate(turned, axis=1)
        square = sum(
            jnp.dot(turned[k], jump[came_j[k], k], preferred_element_type=F32) for k in range(layers_j)
        )
        blocks = [square] + [
            jnp.dot(turned[k], jump[came_j[k], other], preferred_element_type=F32) for k, other in crossed
        ]
        decay = -0.5 * jnp.concatenate(blocks, axis=1)
        drift, steer = ham_row(0), ham_row(1)
        for at in range(len(tables) // 2):
            coeffs = drift + amplitudes[at] * steer
            tables[2 * at][c] = jnp.concatenate([coeffs, decay], axis=1).astype(BF16)
            tables[2 * at + 1][c] = jnp.concatenate([-coeffs, decay], axis=1).astype(BF16)


def operator_tables(ham_blocks, ham_cols, jump_blocks, jump_cols, amplitudes):
    layers_h, count = ham_cols.shape
    layers_j = jump_cols.shape[0]
    size = ham_blocks.shape[-1]
    layers_k = 1 + layers_j * (layers_j - 1)
    smem = pl.BlockSpec(memory_space=pltpu.SMEM)
    vmem = pl.BlockSpec(memory_space=pltpu.VMEM)
    table = jax.ShapeDtypeStruct((count, size, (2 * layers_h + layers_k) * size), BF16)
    number = amplitudes.shape[0]
    rows, jump_row, *tables = pl.pallas_call(
        table_kernel,
        out_shape=[
            jax.ShapeDtypeStruct((2 * layers_h + layers_k + layers_j, count), jnp.int32),
            jax.ShapeDtypeStruct((count, size, layers_j * size), BF16),
        ] + [table] * (2 * number),
        in_specs=[smem, smem, smem, vmem, vmem],
        out_specs=[smem, vmem] + [vmem] * (2 * number),
        compiler_params=pltpu.CompilerParams(vmem_limit_bytes=60 * 2**20),
        cost_estimate=pl.CostEstimate(flops=1, bytes_accessed=1, transcendentals=0),
        name="operator_tables",
    )(ham_cols, jump_cols, amplitudes, ham_blocks, jump_blocks)
    return (2 * layers_h, layers_k, layers_j), rows, jump_row, tables[0::2], tables[1::2]


class Step:
    def __init__(self, rows, counts, size, plus, minus, jump):
        self.rows, self.counts, self.size = rows, counts, size
        self.plus, self.minus, self.jump = plus, minus, jump

    def take(self, ref, kind, c, cols):
        first = sum(self.counts[:kind])
        return [
            ref[pl.ds(pl.multiple_of(self.rows[first + k, c], self.size), self.size), cols]
            for k in range(self.counts[kind])
        ]

    def ham(self, table, c, ham_ref, decay_ref, cols):
        met = jnp.concatenate(self.take(ham_ref, 0, c, cols) + self.take(decay_ref, 1, c, cols), axis=0)
        return jnp.dot(table[c], met, preferred_element_type=F32)

    def pull(self, c, ref, cols):
        met = jnp.concatenate(self.take(ref, 2, c, cols), axis=0)
        return jnp.dot(self.jump[c], met, preferred_element_type=F32)


def turn_whole(source, target, tile):
    n = source.shape[0] // tile

    @pl.loop(0, n)
    def _(i):
        near = pl.ds(pl.multiple_of(i * tile, tile), tile)
        for j in range(n):
            far = pl.ds(j * tile, tile)
            target[far, near] = source[near, far].T


def load_all(copies, sems):
    copies = [pltpu.make_async_copy(source, target, sems.at[k]) for k, (source, target) in enumerate(copies)]
    for copy in copies:
        copy.start()
    for copy in copies:
        copy.wait()


def part_of(first, k, tile):
    return pl.ds(pl.multiple_of(first + k * tile, tile), tile)


def assemble_first(place, near, near_pair, far, far_pair, c_ref, d_ref, stage, other, sems, tile):
    half, width = far.shape
    here, there = place[2], half - place[2]
    own, pair = place[3], width - place[3]

    def cols(first):
        return pl.ds(pl.multiple_of(first, width), width)

    copies = [
        (far, other.at[pl.ds(0, half), cols(own)]),
        (far_pair, other.at[pl.ds(0, half), cols(pair)]),
    ]
    for k in range(2):
        copies.append((near.at[0, k], stage.at[:, cols(k * half + own)]))
        copies.append((near_pair.at[0, k], stage.at[:, cols(k * half + pair)]))
    load_all(copies, sems)

    def mixed(rows, j):
        real = stage[rows, pl.ds(j * tile, tile)].astype(F32)
        imag = stage[rows, pl.ds(half + j * tile, tile)].astype(F32)
        return (real + imag).astype(BF16), (real - imag).astype(BF16)

    @pl.loop(0, half // tile)
    def _(i):
        here_i, there_i = part_of(here, i, tile), part_of(there, i, tile)
        for j in range(half // tile):
            here_j, there_j = part_of(here, j, tile), part_of(there, j, tile)
            total, less = mixed(there_i, j)
            c_ref[there_i, here_j] = total
            d_ref[there_i, here_j] = less
            c_ref[here_j, there_i] = less.T
            d_ref[here_j, there_i] = total.T
            block = other[part_of(0, i, tile), pl.ds(j * tile, tile)]
            c_ref[there_i, there_j] = block
            d_ref[there_j, there_i] = block.T
            total, less = mixed(here_i, j)
            c_ref[here_i, here_j] = total
            d_ref[here_i, here_j] = less


def assemble_next(place, near, near_pair, far, far_pair, c_ref, d_ref, stage, other, sems, tile):
    half, width = far.shape
    here, there = place[2], half - place[2]
    copies = []
    for pieces, last, core in ((near, far, place[3]), (near_pair, far_pair, width - place[3])):
        for k, piece in enumerate((*pieces, last)):
            target = other if k in (0, 3) else stage
            to = pl.ds(pl.multiple_of((0, 0, half, half)[k] + core, width), width)
            copies.append((piece, target.at[pl.ds(0, half), to]))
    load_all(copies, sems)

    @pl.loop(0, half // tile)
    def _(i):
        rows = part_of(0, i, tile)
        here_i, there_i = part_of(here, i, tile), part_of(there, i, tile)
        for j in range(half // tile):
            here_j, there_j = part_of(here, j, tile), part_of(there, j, tile)
            real = stage[rows, pl.ds(j * tile, tile)].astype(F32)
            imag = stage[rows, pl.ds(half + j * tile, tile)].astype(F32)
            total, less = (real + imag).astype(BF16), (real - imag).astype(BF16)
            c_ref[there_i, here_j] = total
            d_ref[there_i, here_j] = less
            c_ref[here_j, there_i] = less.T
            d_ref[here_j, there_i] = total.T
            block = other[rows, pl.ds(j * tile, tile)]
            c_ref[here_i, here_j] = block
            d_ref[here_j, here_i] = block.T
            block = other[rows, pl.ds(half + j * tile, tile)]
            c_ref[there_i, there_j] = block
            d_ref[there_j, there_i] = block.T


def whole_step(step, c_ref, d_ref, r_ref, x_ref, c_new, d_new, tile):
    n = c_ref.shape[0]
    count = tile // step.size
    products = (
        (r_ref, lambda c, cols: step.ham(step.minus, c, c_ref, d_ref, cols)),
        (x_ref, lambda c, cols: step.pull(c, d_ref, cols)),
    )

    @pl.loop(0, n // tile)
    def _(g):
        @pl.loop(0, n // tile, unroll=2)
        def _(s):
            cols = part_of(0, s, tile)
            for target, product in products:
                rows = [product(g * count + u, cols).astype(BF16) for u in range(count)]
                target[cols, part_of(0, g, tile)] = jnp.concatenate(rows, axis=0).T

    @pl.loop(0, n // tile)
    def _(g):
        @pl.loop(0, n // tile, unroll=2)
        def _(s):
            cols = part_of(0, s, tile)
            made = []
            for u in range(count):
                c = g * count + u
                own = pl.ds(pl.multiple_of(c * step.size, step.size), step.size)
                change = step.ham(step.plus, c, d_ref, c_ref, cols) + step.pull(c, x_ref, cols)
                change = change + r_ref[own, cols].astype(F32)
                made.append((c_ref[own, cols].astype(F32) + time_step * change).astype(BF16))
                c_new[own, cols] = made[u]
            d_new[cols, part_of(0, g, tile)] = jnp.concatenate(made, axis=0).T


def own_step(step, start, width, c_ref, d_ref, turned, tile, base, out):
    n = c_ref.shape[0]
    part = min(tile, width)
    products = (
        lambda c, cols: step.ham(step.minus, c, c_ref, d_ref, cols),
        lambda c, cols: step.ham(step.plus, c, d_ref, c_ref, cols),
        lambda c, cols: step.pull(c, d_ref, cols),
        lambda c, cols: step.pull(c, c_ref, cols),
    )

    @pl.loop(0, width // part)
    def _(g):
        first = start // step.size + g * (part // step.size)

        @pl.loop(0, n // tile)
        def _(s):
            cols = part_of(0, s, tile)
            for k, product in enumerate(products):
                rows = [product(first + u, cols).astype(BF16) for u in range(part // step.size)]
                turned[cols, part_of(k * width, g, part)] = jnp.concatenate(rows, axis=0).T

    @pl.loop(0, n // step.size, unroll=4)
    def _(c):
        own = pl.ds(pl.multiple_of(c * step.size, step.size), step.size)
        for s in range(width // part):
            cols = pl.ds(pl.multiple_of(start + s * part, part), part)
            to = pl.ds(s * part, part)
            of = [pl.ds(k * width + s * part, part) for k in range(4)]
            change = step.ham(step.plus, c, d_ref, c_ref, cols) + step.pull(c, turned, of[2])
            second = step.ham(step.minus, c, c_ref, d_ref, cols) + step.pull(c, turned, of[3])
            change = change + turned[own, of[0]].astype(F32)
            second = second + turned[own, of[1]].astype(F32)
            real, imag = base(own, cols, to)
            out[0, 0, own, to] = (real + 0.5 * time_step * (change + second)).astype(BF16)
            out[0, 1, own, to] = (imag + 0.5 * time_step * (change - second)).astype(BF16)


def fill_whole(piece, c_ref, d_ref, sems, tile):
    load_all([(piece, c_ref)], sems)
    turn_whole(c_ref, d_ref, tile)


def inner_kernel(counts, tile, number, rows, place, terminal, plus, minus, jump, *refs):
    pieces, refs = refs[:number], refs[number:]
    out, c_ref, d_ref, stage, turned, sems = refs
    if number == 1:
        fill_whole(pieces[0], c_ref, d_ref, sems, tile)
    else:
        assemble_first(place, *pieces, c_ref, d_ref, stage, turned, sems, tile)
    step = Step(rows, counts, plus.shape[1], plus, minus, jump)

    def base(own, _, cols):
        return terminal[0, 0, own, cols].astype(F32), terminal[0, 1, own, cols].astype(F32)

    own_step(step, place[0], out.shape[3], c_ref, d_ref, turned, tile, base, out)


def start_kernel(counts, tile, number, rows, place, terminal, plus, minus, jump, plus_two, minus_two, *refs):
    pieces, refs = refs[:number], refs[number:]
    out, c_ref, d_ref, r_ref, x_ref, c_new, d_new, sems = refs
    size = plus.shape[1]

    @pl.when(place[1] == 1)
    def _():
        load_all([(terminal, out)], sems)

    @pl.when(place[1] == 0)
    def _():
        if number == 1:
            fill_whole(pieces[0], c_ref, d_ref, sems, tile)
        else:
            near, near_pair = pieces[0:3], pieces[3:6]
            assemble_next(place, near, near_pair, *pieces[6:], c_ref, d_ref, r_ref, x_ref, sems, tile)
        whole_step(Step(rows, counts, size, plus, minus, jump), c_ref, d_ref, r_ref, x_ref, c_new, d_new, tile)

        def base(own, cols, _):
            first, second = c_new[own, cols].astype(F32), d_new[own, cols].astype(F32)
            return 0.5 * (first + second), 0.5 * (first - second)

        step = Step(rows, counts, size, plus_two, minus_two, jump)
        own_step(step, place[0], out.shape[3], c_new, d_new, r_ref, tile, base, out)


def swapped(block, bit):
    return lax.ppermute(block, "row", [(i, i ^ bit) for i in range(lax.axis_size("row"))])


def on_device(terminal, controls, ham_blocks, ham_cols, jump_blocks, jump_cols):
    n, width = terminal.shape[2], terminal.shape[3]
    tile = 256
    row = lax.axis_index("row")
    here = row // 2 * 2 * width
    controls_next = shifted_down(controls, "tm")
    is_last = lax.axis_index("tm") == lax.axis_size("tm") - 1
    place = jnp.stack([row * width, is_last.astype(jnp.int32), here, row % 2 * width]).astype(jnp.int32)
    amplitudes = jnp.stack([controls[0, 1], controls_next[0, 1], controls_next[0, 0]])
    counts, rows, jump_row, plus, minus = operator_tables(ham_blocks, ham_cols, jump_blocks, jump_cols, amplitudes)

    smem = pl.BlockSpec(memory_space=pltpu.SMEM)
    vmem = pl.BlockSpec(memory_space=pltpu.VMEM)
    anywhere = pl.BlockSpec(memory_space=pl.ANY)
    square = pltpu.VMEM((n, n), BF16)

    def step_call(kernel, name, state_spec, squares, tables, pieces):
        return pl.pallas_call(
            functools.partial(kernel, counts, tile, len(pieces)),
            out_shape=jax.ShapeDtypeStruct(terminal.shape, BF16),
            in_specs=[smem, smem, state_spec] + [vmem] * len(tables) + [anywhere] * len(pieces),
            out_specs=vmem,
            scratch_shapes=[square] * squares + [pltpu.SemaphoreType.DMA((max(len(pieces), 6),))],
            compiler_params=pltpu.CompilerParams(vmem_limit_bytes=60 * 2**20),
            cost_estimate=pl.CostEstimate(flops=1, bytes_accessed=1, transcendentals=0),
            name=name,
        )(rows, place, terminal, *tables, *pieces)

    first = [plus[0], minus[0], jump_row]
    second = [plus[1], minus[1], jump_row, plus[2], minus[2]]
    if lax.axis_size("row") == 4:
        near_pair = swapped(terminal, 1)
        mine = lax.dynamic_slice_in_dim(terminal[0], here, 2 * width, 1).astype(F32)
        mixed = (mine[0] + mine[1]).astype(BF16)
        apart = lax.dynamic_slice_in_dim(terminal[0], 2 * width - here, 2 * width, 1)
        far = swapped(mixed, 2)
        mixed, real, imag, _ = lax.optimization_barrier((mixed, apart[0], apart[1], controls_next))
        near = [shifted_down(piece, "tm") for piece in (mixed, real, imag)]
        far, rows, near[0] = lax.optimization_barrier((far, rows, near[0]))
        far_next = swapped(near[0], 2)
        new_fpoint = step_call(inner_kernel, "inner_point", vmem, 4, first, [terminal, near_pair, far, swapped(far, 1)])
        pair = [swapped(near[0], 1)]
        near[1], near[2], far_next, new_fpoint = lax.optimization_barrier((near[1], near[2], far_next, new_fpoint))
        pair += [swapped(piece, 1) for piece in near[1:]]
        pieces = near + pair + [far_next, swapped(far_next, 1)]
    else:
        mixed = (terminal[0, 0].astype(F32) + terminal[0, 1].astype(F32)).astype(BF16)

        def gathered(piece):
            return [lax.all_gather(piece, "row", axis=1, tiled=True)]

        new_fpoint = step_call(inner_kernel, "inner_point", vmem, 4, first, gathered(mixed))
        pieces = gathered(shifted_down(mixed, "tm"))
    new_cpoint = step_call(start_kernel, "left_end", anywhere, 6, second, pieces)
    return (new_cpoint, new_fpoint)


def solution(mesh):
    in_specs = (P(("grp", "tm"), None, None, "row"), P(("grp", "tm"), None), P(), P(), P(), P())
    out_specs = (P(("grp", "tm"), None, None, "row"), P(("grp", "tm"), None, None, "row"))
    return jax.shard_map(
        on_device, mesh=mesh, in_specs=in_specs, out_specs=out_specs, check_vma=False
    )
```

time: 172 us -> 171 us (level)
  Pallas kernels: 80.3 us -> 120 us
  waiting for transfers between devices: 57.2 us -> 21.2 us
  starting transfers between devices: 19.1 us -> 9.36 us
  local copies, waits for them, and re-layouts: 9.48 us -> 12.5 us
  other arithmetic: 4.44 us -> 6.68 us
    pallas_call x2, Pallas kernels: 64.2 us -> 103 us  [step_call(): pl.pallas_call(functools.partial(kernel, counts, tile, len(pieces)), out_...]
    ppermute x21 -> x8, waiting for transfers between devices: 23.9 us -> 5.49 us  [swapped(): lax.ppermute(block, 'row', [(i, i ^ bit) for i in range(lax.axis_size('ro...]
    ppermute x7 -> x4, waiting for transfers between devices: 33.3 us -> 15.7 us  [shifted_down(): return lax.ppermute(block, axis, route)]
    ppermute x21 -> x8, starting transfers between devices: 10.1 us -> 4.22 us  [swapped(): lax.ppermute(block, 'row', [(i, i ^ bit) for i in range(lax.axis_size('ro...]
    ppermute x7 -> x4, starting transfers between devices: 8.99 us -> 5.13 us  [shifted_down(): return lax.ppermute(block, axis, route)]
    squeeze x0 -> x1, local copies, waits for them, and re-layouts: none -> 2.99 us  [on_device(): apart[1]]
    unnamed x56 -> x16, local copies, waits for them, and re-layouts: 8.84 us -> 8.27 us
  transfers between devices with their start and end apart: 28 -> 12, of which waited for: 12 -> 4; matrix products, arithmetic and copies ran while one was open for 7% -> 11% of each run, Pallas kernels for 9% -> 29%
where the time goes in v4:
time: 171 us
  Pallas kernels  120 us (70%)
  waiting for transfers between devices  21.2 us (12%)
  local copies, waits for them, and re-layouts  12.5 us (7%)
  starting transfers between devices  9.36 us (5%)
  other arithmetic  6.68 us (4%)
    pallas_call x2, Pallas kernels, step_call(): pl.pallas_call(functools.partial(kernel, counts, tile, len(pieces)), out_...  103 us
    pallas_call x1, Pallas kernels, operator_tables(): pl.pallas_call(table_kernel, out_shape=[jax.ShapeDtypeStruct((2 * layers_...  16.8 us
    ppermute x4, waiting for transfers between devices, shifted_down(): return lax.ppermute(block, axis, route)  15.7 us
    unnamed x16, local copies, waits for them, and re-layouts  8.27 us
    ppermute x8, waiting for transfers between devices, swapped(): lax.ppermute(block, 'row', [(i, i ^ bit) for i in range(lax.axis_size('ro...  5.49 us
    ppermute x4, starting transfers between devices, shifted_down(): return lax.ppermute(block, axis, route)  5.13 us
    ppermute x8, starting transfers between devices, swapped(): lax.ppermute(block, 'row', [(i, i ^ bit) for i in range(lax.axis_size('ro...  4.22 us
  transfers between devices with their start and end apart: 12, of which 4 were waited for; matrix products, arithmetic and copies ran while one was open for 11% of the time, Pallas kernels for 29%

profile of v4, /device:TPU:0, one launch (start us, length us, event | category | flops | bytes accessed | tf_op | source)
XLA Modules:
  0.0 170.8 jit_solution(905118890869919136)
XLA Ops:
  0.6 0.5 collective-permute-start.6
  1.1 1.3 collective-permute-start.1
  2.5 2.2 %dynamic-slice_convert_fusion = f32[1,2,1024,512]{3,2,1,0:T(8,128)S(1)} fusion(bf16[1,2,2048,512]{3,2,1,0:T(8,128)(2,1)} %terminal.3, s32[]{:T(128)S(6)} %select_n.18), kind=kLoop, calls=%fused_computation.2 | loop fusion | flops 1048576 | bytes 6291460 | tf_op jit(solution)/shard_map/convert_element_type | solution.py:357
  4.6 0.0 copy-start.6
  4.7 0.0 copy-start
  4.7 1.4 fusion.1
  6.1 2.5 %collective-permute-start = (bf16[1024,512]{1,0:T(8,128)(2,1)}, bf16[1024,512]{1,0:T(8,128)(2,1)S(1)}, u32[]{:S(2)}, u32[]{:S(2)}) collective-permute-start(bf16[1024,512]{1,0:T(8,128)(2,1)} %fusion.1), channel_id=1, source_target_pairs={{0,2},{1,3},{2,0},{3,1},{4,6},{5,7},{6,4},{7,5},{8,10},{9,11},{10,... | collective-permute-start | bytes 3145736 | tf_op jit(solution)/shard_map/ppermute | solution.py:322
  8.6 3.0 %dynamic-slice_bitcast_fusion = (bf16[1024,512]{1,0:T(8,128)(2,1)}, bf16[1024,512]{1,0:T(8,128)(2,1)}) fusion(bf16[1,2,2048,512]{3,2,1,0:T(8,128)(2,1)} %terminal.3, s32[]{:T(128)S(6)} %add.24, s32[]{:T(128)S(6)} %select_n.19), kind=kLoop, calls=%fused_computation.4 | loop fusion | bytes 4194312 | tf_op jit(solution)/shard_map/squeeze | solution.py:361
  11.6 0.0 collective-permute-done.1
  11.6 1.3 collective-permute-start.2
  12.9 0.0 copy-done.6
  12.9 0.6 slice.27
  13.5 0.0 copy-done
  13.5 3.9 %copy.8.ham = bf16[2,64,2,32,32]{4,3,2,1,0:T(8,128)(2,1)} copy(bf16[2,64,2,32,32]{1,4,3,2,0:T(8,128)(2,1)S(1)} %copy-done) | data formatting | bytes 1048576 | tf_op args[2]
  17.4 0.0 copy-start.3
  17.4 3.5 %copy.9.jump = bf16[64,2,32,32]{3,2,1,0:T(8,128)(2,1)} copy(bf16[64,2,32,32]{0,3,2,1:T(8,128)(2,1)} %param.10) | data formatting | bytes 524288 | tf_op args[4]
  20.9 0.6 fusion.2
  21.5 2.5 %pad_maximum_fusion.amplitudes = f32[3]{0:T(128)} fusion(f32[1]{0:T(128)} %bitcast.3, f32[1]{0:T(128)} %bitcast.2, f32[1]{0:T(128)} %bitcast.1), kind=kLoop, calls=%fused_computation.6 | loop fusion | flops 6 | bytes 24 | tf_op jit(solution)/shard_map/stack | solution.py:333
  24.0 16.8 %operator_tables.1 = (s32[9,64]{1,0:T(8,128)}, bf16[64,32,64]{2,1,0:T(8,128)(2,1)}, bf16[64,32,224]{2,1,0:T(8,128)(2,1)}, bf16[64,32,224]{2,1,0:T(8,128)(2,1)}, ...) custom-call(s32[2,64]{1,0:T(2,128)} %ham_cols.1, ...), custom_call_target="tpu_custom_call" | custom-call | flops 1 | bytes 1 | tf_op jit(solution)/shard_map/operator_tables/pallas_call | solution.py:74
  40.8 0.0 collective-permute-done.refs_2_
  40.8 0.0 copy-start.2
  40.8 0.0 collective-permute-done.2.refs_0_
  40.8 0.0 copy-start.1
  40.8 0.3 collective-permute-start.7
  41.1 1.3 collective-permute-start.3
  42.4 0.0 copy-done.3
  42.4 1.3 collective-permute-start.4
  43.7 0.3 collective-permute-start.5
  44.0 0.6 pad_add_fusion.place
  44.6 0.0 collective-permute-done.7.refs_3_
  44.6 0.1 collective-permute-start.8
  44.7 0.0 collective-permute-done.6.refs_1_
  44.7 0.0 copy-done.2
  44.7 32.2 %inner_point.1 = bf16[1,2,2048,512]{3,2,1,0:T(8,128)(2,1)} custom-call(s32[9,64]{1,0:T(8,128)} %get-tuple-element.22.rows, s32[4]{0:T(128)} %pad_add_fusion.place, bf16[1,2,2048,512]{3,2,1,0:T(8,128)(2,1)} %terminal.3, bf16[64,32,224]{2,1,0:T(8,128)(2,1)} %get-tuple-element.31.plus, bf16[64,32,224]{2,1,0:T(8,128)(2,1)} %get-tuple-element.32.minus, ...), custom_call_target="tpu_custom_call" | custom-call | flops 1 | bytes 1 | tf_op jit(solution)/shard_map/inner_point/pallas_call | solution.py:342
  76.9 0.0 copy-done.1
  77.0 0.0 collective-permute-done.3.refs_1_
  77.0 15.7 %collective-permute-done.4.refs_2_ = bf16[1024,512]{1,0:T(8,128)(2,1)} collective-permute-done((bf16[1024,512]{1,0:T(8,128)(2,1)S(1)}, bf16[1024,512]{1,0:T(8,128)(2,1)}, u32[]{:S(2)}, u32[]{:S(2)}) %collective-permute-start.4) | collective-permute-done | bytes 1048608 | tf_op jit(solution)/shard_map/ppermute | solution.py:17
  92.7 0.0 collective-permute-done.5.refs_6_
  92.7 0.0 collective-permute-start.10
  92.7 0.5 collective-permute-start.11
  93.2 0.0 collective-permute-start.9
  93.2 0.0 collective-permute-done.8.refs_3_
  93.2 2.4 %collective-permute-done.10.refs_5_ = bf16[1024,512]{1,0:T(8,128)(2,1)S(1)} collective-permute-done((bf16[1024,512]{1,0:T(8,128)(2,1)}, bf16[1024,512]{1,0:T(8,128)(2,1)S(1)}, u32[]{:S(2)}, u32[]{:S(2)}) %collective-permute-start.10) | collective-permute-done | bytes 1048608 | tf_op jit(solution)/shard_map/ppermute | solution.py:322
  95.6 0.0 copy-start.4
  95.6 3.0 %collective-permute-done.11.refs_7_ = bf16[1024,512]{1,0:T(8,128)(2,1)S(1)} collective-permute-done((bf16[1024,512]{1,0:T(8,128)(2,1)}, bf16[1024,512]{1,0:T(8,128)(2,1)S(1)}, u32[]{:S(2)}, u32[]{:S(2)}) %collective-permute-start.11) | collective-permute-done | bytes 1048608 | tf_op jit(solution)/shard_map/ppermute | solution.py:322
  98.6 0.0 copy-start.5
  98.6 0.1 collective-permute-done.9.refs_4_
  98.7 0.0 copy-done.4
  98.7 0.9 copy-done.5
  99.5 71.3 %left_end.1 = bf16[1,2,2048,512]{3,2,1,0:T(8,128)(2,1)} custom-call(s32[9,64]{1,0:T(8,128)} %get-tuple-element.22.rows, s32[4]{0:T(128)} %pad_add_fusion.place, bf16[1,2,2048,512]{3,2,1,0:T(8,128)(2,1)} %terminal.3, bf16[64,32,224]{2,1,0:T(8,128)(2,1)} %get-tuple-element.23.plus, bf16[64,32,224]{2,1,0:T(8,128)(2,1)} %get-tuple-element.24.minus, ...), custom_call_target="tpu_custom_call" | custom-call | flops 1 | bytes 1 | tf_op jit(solution)/shard_map/left_end/pallas_call | solution.py:342
Async XLA Ops:
  0.6 44.1 %collective-permute-start.6 = (bf16[1,2,2048,512]{3,2,1,0:T(8,128)(2,1)}, bf16[1,2,2048,512]{3,2,1,0:T(8,128)(2,1)}, u32[]{:S(2)}, u32[]{:S(2)}) collective-permute-start(bf16[1,2,2048,512]{3,2,1,0:T(8,128)(2,1)} %terminal.3), channel_id=1, source_target_pairs={{0,1},{1,0},{2,3},{3,2},{4,5},{5,4},{6,7},{7,6},{8,9},{9,8},{10,11... | collective-permute-start | bytes 12582920 | tf_op jit(solution)/shard_map/ppermute | solution.py:322
  1.1 10.4 %collective-permute-start.1 = (f32[1,2]{1,0:T(1,128)}, f32[1,2]{1,0:T(1,128)S(1)}, u32[]{:S(2)}, u32[]{:S(2)}) collective-permute-start(f32[1,2]{1,0:T(1,128)} %param.7), channel_id=1, source_target_pairs={{4,0},{8,4},{12,8},{5,1},{9,5},{13,9},{6,2},{10,6},{14,10},{7,3},{... | collective-permute-start | bytes 32 | tf_op jit(solution)/shard_map/ppermute | solution.py:17
  4.6 8.2 %copy-start.6 = (f32[1,2]{1,0:T(1,128)S(1)}, f32[1,2]{1,0:T(1,128)}, u32[]{:S(2)}) copy-start(f32[1,2]{1,0:T(1,128)} %param.7) | copy-start | bytes 28
  4.7 8.9 %copy-start = (bf16[2,64,2,32,32]{1,4,3,2,0:T(8,128)(2,1)S(1)}, bf16[2,64,2,32,32]{1,4,3,2,0:T(8,128)(2,1)}, u32[]{:S(2)}) copy-start(bf16[2,64,2,32,32]{1,4,3,2,0:T(8,128)(2,1)} %param.8) | copy-start | bytes 1572868
  6.1 34.7 %collective-permute-start = (bf16[1024,512]{1,0:T(8,128)(2,1)}, bf16[1024,512]{1,0:T(8,128)(2,1)S(1)}, u32[]{:S(2)}, u32[]{:S(2)}) collective-permute-start(bf16[1024,512]{1,0:T(8,128)(2,1)} %fusion.1), channel_id=1, source_target_pairs={{0,2},{1,3},{2,0},{3,1},{4,6},{5,7},{6,4},{7,5},{8,10},{9,11},{10,... | collective-permute-start | bytes 3145736 | tf_op jit(solution)/shard_map/ppermute | solution.py:322
  11.6 29.3 %collective-permute-start.2 = (bf16[1024,512]{1,0:T(8,128)(2,1)}, bf16[1024,512]{1,0:T(8,128)(2,1)S(1)}, u32[]{:S(2)}, u32[]{:S(2)}) collective-permute-start(bf16[1024,512]{1,0:T(8,128)(2,1)} %fusion.1), channel_id=1, source_target_pairs={{4,0},{8,4},{12,8},{5,1},{9,5},{13,9},{6,2},{10,6},{14,10},{7,3},{... | collective-permute-start | bytes 3145736 | tf_op jit(solution)/shard_map/ppermute | solution.py:17
  17.4 25.0 %copy-start.3 = (bf16[1024,512]{1,0:T(8,128)(2,1)S(1)}, bf16[1024,512]{1,0:T(8,128)(2,1)}, u32[]{:S(2)}) copy-start(bf16[1024,512]{1,0:T(8,128)(2,1)} %get-tuple-element.30) | copy-start | bytes 3145732
  40.8 3.9 %copy-start.2 = (bf16[1024,512]{1,0:T(8,128)(2,1)}, bf16[1024,512]{1,0:T(8,128)(2,1)S(1)}, u32[]{:S(2)}) copy-start(bf16[1024,512]{1,0:T(8,128)(2,1)S(1)} %collective-permute-done.refs_2_) | copy-start | bytes 3145732
  40.8 36.1 %copy-start.1 = (bf16[1024,512]{1,0:T(8,128)(2,1)}, bf16[1024,512]{1,0:T(8,128)(2,1)S(1)}, u32[]{:S(2)}) copy-start(bf16[1024,512]{1,0:T(8,128)(2,1)S(1)} %collective-permute-done.2.refs_0_) | copy-start | bytes 3145732
  40.8 3.8 %collective-permute-start.7 = (bf16[1024,512]{1,0:T(8,128)(2,1)S(1)}, bf16[1024,512]{1,0:T(8,128)(2,1)}, u32[]{:S(2)}, u32[]{:S(2)}) collective-permute-start(bf16[1024,512]{1,0:T(8,128)(2,1)S(1)} %collective-permute-done.refs_2_), channel_id=1, source_target_pairs={{0,1},{1,0},{2,3},{3,2},{4,5},{5,4},{6,7},{7,6},{8,9},{9,8},{10,11... | collective-permute-start | bytes 3145736 | tf_op jit(solution)/shard_map/ppermute | solution.py:322
  41.1 35.9 %collective-permute-start.3 = (bf16[1024,512]{1,0:T(8,128)(2,1)}, bf16[1024,512]{1,0:T(8,128)(2,1)}, u32[]{:S(2)}, u32[]{:S(2)}) collective-permute-start(bf16[1024,512]{1,0:T(8,128)(2,1)} %get-tuple-element.29), channel_id=1, source_target_pairs={{4,0},{8,4},{12,8},{5,1},{9,5},{13,9},{6,2},{10,6},{14,10},{7,3},{... | collective-permute-start | bytes 3145736 | tf_op jit(solution)/shard_map/ppermute | solution.py:17
  42.4 50.3 %collective-permute-start.4 = (bf16[1024,512]{1,0:T(8,128)(2,1)S(1)}, bf16[1024,512]{1,0:T(8,128)(2,1)}, u32[]{:S(2)}, u32[]{:S(2)}) collective-permute-start(bf16[1024,512]{1,0:T(8,128)(2,1)S(1)} %copy-done.3), channel_id=1, source_target_pairs={{4,0},{8,4},{12,8},{5,1},{9,5},{13,9},{6,2},{10,6},{14,10},{7,3},{... | collective-permute-start | bytes 3145736 | tf_op jit(solution)/shard_map/ppermute | solution.py:17
  43.7 49.0 %collective-permute-start.5 = (bf16[1024,512]{1,0:T(8,128)(2,1)S(1)}, bf16[1024,512]{1,0:T(8,128)(2,1)}, u32[]{:S(2)}, u32[]{:S(2)}) collective-permute-start(bf16[1024,512]{1,0:T(8,128)(2,1)S(1)} %collective-permute-done.2.refs_0_), channel_id=1, source_target_pairs={{0,2},{1,3},{2,0},{3,1},{4,6},{5,7},{6,4},{7,5},{8,10},{9,11},{10,... | collective-permute-start | bytes 3145736 | tf_op jit(solution)/shard_map/ppermute | solution.py:322
  44.6 48.6 %collective-permute-start.8 = (bf16[1024,512]{1,0:T(8,128)(2,1)S(1)}, bf16[1024,512]{1,0:T(8,128)(2,1)}, u32[]{:S(2)}, u32[]{:S(2)}) collective-permute-start(bf16[1024,512]{1,0:T(8,128)(2,1)S(1)} %collective-permute-done.2.refs_0_), channel_id=1, source_target_pairs={{0,1},{1,0},{2,3},{3,2},{4,5},{5,4},{6,7},{7,6},{8,9},{9,8},{10,11... | collective-permute-start | bytes 3145736 | tf_op jit(solution)/shard_map/ppermute | solution.py:322
  92.7 2.9 %collective-permute-start.10 = (bf16[1024,512]{1,0:T(8,128)(2,1)}, bf16[1024,512]{1,0:T(8,128)(2,1)S(1)}, u32[]{:S(2)}, u32[]{:S(2)}) collective-permute-start(bf16[1024,512]{1,0:T(8,128)(2,1)} %collective-permute-done.4.refs_2_), channel_id=1, source_target_pairs={{0,1},{1,0},{2,3},{3,2},{4,5},{5,4},{6,7},{7,6},{8,9},{9,8},{10,11... | collective-permute-start | bytes 3145736 | tf_op jit(solution)/shard_map/ppermute | solution.py:322
  92.7 5.9 %collective-permute-start.11 = (bf16[1024,512]{1,0:T(8,128)(2,1)}, bf16[1024,512]{1,0:T(8,128)(2,1)S(1)}, u32[]{:S(2)}, u32[]{:S(2)}) collective-permute-start(bf16[1024,512]{1,0:T(8,128)(2,1)} %collective-permute-done.5.refs_6_), channel_id=1, source_target_pairs={{0,1},{1,0},{2,3},{3,2},{4,5},{5,4},{6,7},{7,6},{8,9},{9,8},{10,11... | collective-permute-start | bytes 3145736 | tf_op jit(solution)/shard_map/ppermute | solution.py:322
  93.2 5.5 %collective-permute-start.9 = (bf16[1024,512]{1,0:T(8,128)(2,1)}, bf16[1024,512]{1,0:T(8,128)(2,1)}, u32[]{:S(2)}, u32[]{:S(2)}) collective-permute-start(bf16[1024,512]{1,0:T(8,128)(2,1)} %collective-permute-done.3.refs_1_), channel_id=1, source_target_pairs={{0,1},{1,0},{2,3},{3,2},{4,5},{5,4},{6,7},{7,6},{8,9},{9,8},{10,11... | collective-permute-start | bytes 3145736 | tf_op jit(solution)/shard_map/ppermute | solution.py:322
  95.6 3.1 %copy-start.4 = (bf16[1024,512]{1,0:T(8,128)(2,1)}, bf16[1024,512]{1,0:T(8,128)(2,1)S(1)}, u32[]{:S(2)}) copy-start(bf16[1024,512]{1,0:T(8,128)(2,1)S(1)} %collective-permute-done.10.refs_5_) | copy-start | bytes 3145732
  98.6 1.0 copy-start.5

commit v5 on v4

--- a/solution.py
+++ b/solution.py
@@ -17,7 +17,7 @@
     return lax.ppermute(block, axis, route)
 
 
-def table_kernel(ham_cols, jump_cols, amplitudes, ham, jump, rows, jump_row, *tables):
+def table_kernel(which, ham_cols, jump_cols, controls, controls_next, ham, jump, rows, jump_row, *tables):
     layers_h, count = ham_cols.shape
     layers_j = jump_cols.shape[0]
     size = ham.shape[-1]
@@ -33,7 +33,7 @@
         for k in range(layers_j):
             rows[first_j + k, jump_cols[k, b]] = b * size
 
-    @pl.loop(0, count, unroll=2)
+    @pl.loop(0, count, unroll=8)
     def _(c):
         came_h = [rows[layers_h + k, c] // size for k in range(layers_h)]
         came_j = [rows[first_j + k, c] // size for k in range(layers_j)]
@@ -56,13 +56,14 @@
         ]
         decay = -0.5 * jnp.concatenate(blocks, axis=1)
         drift, steer = ham_row(0), ham_row(1)
-        for at in range(len(tables) // 2):
-            coeffs = drift + amplitudes[at] * steer
+        for at, (later, fine) in enumerate(which):
+            amplitude = (controls, controls_next)[later][0, fine]
+            coeffs = drift + amplitude * steer
             tables[2 * at][c] = jnp.concatenate([coeffs, decay], axis=1).astype(BF16)
             tables[2 * at + 1][c] = jnp.concatenate([-coeffs, decay], axis=1).astype(BF16)
 
 
-def operator_tables(ham_blocks, ham_cols, jump_blocks, jump_cols, amplitudes):
+def operator_tables(which, ham_blocks, ham_cols, jump_blocks, jump_cols, controls, controls_next):
     layers_h, count = ham_cols.shape
     layers_j = jump_cols.shape[0]
     size = ham_blocks.shape[-1]
@@ -70,19 +71,19 @@
     smem = pl.BlockSpec(memory_space=pltpu.SMEM)
     vmem = pl.BlockSpec(memory_space=pltpu.VMEM)
     table = jax.ShapeDtypeStruct((count, size, (2 * layers_h + layers_k) * size), BF16)
-    number = amplitudes.shape[0]
+    number = len(which)
     rows, jump_row, *tables = pl.pallas_call(
-        table_kernel,
+        functools.partial(table_kernel, which),
         out_shape=[
             jax.ShapeDtypeStruct((2 * layers_h + layers_k + layers_j, count), jnp.int32),
             jax.ShapeDtypeStruct((count, size, layers_j * size), BF16),
         ] + [table] * (2 * number),
-        in_specs=[smem, smem, smem, vmem, vmem],
+        in_specs=[smem, smem, smem, smem, vmem, vmem],
         out_specs=[smem, vmem] + [vmem] * (2 * number),
         compiler_params=pltpu.CompilerParams(vmem_limit_bytes=60 * 2**20),
         cost_estimate=pl.CostEstimate(flops=1, bytes_accessed=1, transcendentals=0),
         name="operator_tables",
-    )(ham_cols, jump_cols, amplitudes, ham_blocks, jump_blocks)
+    )(ham_cols, jump_cols, controls, controls_next, ham_blocks, jump_blocks)
     return (2 * layers_h, layers_k, layers_j), rows, jump_row, tables[0::2], tables[1::2]
 
 
@@ -170,15 +171,16 @@
             d_ref[here_i, here_j] = less
 
 
-def assemble_next(place, near, near_pair, far, far_pair, c_ref, d_ref, stage, other, sems, tile):
-    half, width = far.shape
+def assemble_next(place, pieces, c_ref, d_ref, stage, other, sems, tile):
+    half, width = pieces[0].shape
     here, there = place[2], half - place[2]
     copies = []
-    for pieces, last, core in ((near, far, place[3]), (near_pair, far_pair, width - place[3])):
-        for k, piece in enumerate((*pieces, last)):
-            target = other if k in (0, 3) else stage
-            to = pl.ds(pl.multiple_of((0, 0, half, half)[k] + core, width), width)
-            copies.append((piece, target.at[pl.ds(0, half), to]))
+    for (near, apart, far), core in ((pieces[:3], place[3]), (pieces[3:], width - place[3])):
+        low = pl.ds(pl.multiple_of(core, width), width)
+        high = pl.ds(pl.multiple_of(half + core, width), width)
+        rows = pl.ds(0, half)
+        copies += [(near, other.at[rows, low]), (far, other.at[rows, high])]
+        copies += [(apart.at[0], stage.at[rows, low]), (apart.at[1], stage.at[rows, high])]
     load_all(copies, sems)
 
     @pl.loop(0, half // tile)
@@ -306,8 +308,7 @@
         if number == 1:
             fill_whole(pieces[0], c_ref, d_ref, sems, tile)
         else:
-            near, near_pair = pieces[0:3], pieces[3:6]
-            assemble_next(place, near, near_pair, *pieces[6:], c_ref, d_ref, r_ref, x_ref, sems, tile)
+            assemble_next(place, pieces, c_ref, d_ref, r_ref, x_ref, sems, tile)
         whole_step(Step(rows, counts, size, plus, minus, jump), c_ref, d_ref, r_ref, x_ref, c_new, d_new, tile)
 
         def base(own, cols, _):
@@ -330,8 +331,9 @@
     controls_next = shifted_down(controls, "tm")
     is_last = lax.axis_index("tm") == lax.axis_size("tm") - 1
     place = jnp.stack([row * width, is_last.astype(jnp.int32), here, row % 2 * width]).astype(jnp.int32)
-    amplitudes = jnp.stack([controls[0, 1], controls_next[0, 1], controls_next[0, 0]])
-    counts, rows, jump_row, plus, minus = operator_tables(ham_blocks, ham_cols, jump_blocks, jump_cols, amplitudes)
+    operators = (ham_blocks, ham_cols, jump_blocks, jump_cols)
+    which = ((0, 1), (1, 1), (1, 0))
+    counts, rows, jump_row, plus, minus = operator_tables(which, *operators, controls, controls_next)
 
     smem = pl.BlockSpec(memory_space=pltpu.SMEM)
     vmem = pl.BlockSpec(memory_space=pltpu.VMEM)
@@ -344,7 +346,7 @@
             out_shape=jax.ShapeDtypeStruct(terminal.shape, BF16),
             in_specs=[smem, smem, state_spec] + [vmem] * len(tables) + [anywhere] * len(pieces),
             out_specs=vmem,
-            scratch_shapes=[square] * squares + [pltpu.SemaphoreType.DMA((max(len(pieces), 6),))],
+            scratch_shapes=[square] * squares + [pltpu.SemaphoreType.DMA((8,))],
             compiler_params=pltpu.CompilerParams(vmem_limit_bytes=60 * 2**20),
             cost_estimate=pl.CostEstimate(flops=1, bytes_accessed=1, transcendentals=0),
             name=name,
@@ -354,19 +356,19 @@
     second = [plus[1], minus[1], jump_row, plus[2], minus[2]]
     if lax.axis_size("row") == 4:
         near_pair = swapped(terminal, 1)
-        mine = lax.dynamic_slice_in_dim(terminal[0], here, 2 * width, 1).astype(F32)
+        size = (1, 1, 2 * width, width)
+        mine = [lax.dynamic_slice(terminal, (0, k, here, 0), size)[0, 0].astype(F32) for k in range(2)]
         mixed = (mine[0] + mine[1]).astype(BF16)
-        apart = lax.dynamic_slice_in_dim(terminal[0], 2 * width - here, 2 * width, 1)
+        apart = lax.dynamic_slice(terminal, (0, 0, 2 * width - here, 0), (1, 2, 2 * width, width))[0]
         far = swapped(mixed, 2)
-        mixed, real, imag, _ = lax.optimization_barrier((mixed, apart[0], apart[1], controls_next))
-        near = [shifted_down(piece, "tm") for piece in (mixed, real, imag)]
-        far, rows, near[0] = lax.optimization_barrier((far, rows, near[0]))
-        far_next = swapped(near[0], 2)
+        mixed, apart, _ = lax.optimization_barrier((mixed, apart, controls_next))
+        mixed, apart = shifted_down(mixed, "tm"), shifted_down(apart, "tm")
+        far, rows, mixed = lax.optimization_barrier((far, rows, mixed))
+        far_next = swapped(mixed, 2)
         new_fpoint = step_call(inner_kernel, "inner_point", vmem, 4, first, [terminal, near_pair, far, swapped(far, 1)])
-        pair = [swapped(near[0], 1)]
-        near[1], near[2], far_next, new_fpoint = lax.optimization_barrier((near[1], near[2], far_next, new_fpoint))
-        pair += [swapped(piece, 1) for piece in near[1:]]
-        pieces = near + pair + [far_next, swapped(far_next, 1)]
+        mixed_pair = swapped(mixed, 1)
+        apart, far_next, new_fpoint = lax.optimization_barrier((apart, far_next, new_fpoint))
+        pieces = [mixed, apart, far_next, mixed_pair, swapped(apart, 1), swapped(far_next, 1)]
     else:
         mixed = (terminal[0, 0].astype(F32) + terminal[0, 1].astype(F32)).astype(BF16)
 

time: 171 us -> 164 us (0.959)
  Pallas kernels: 120 us -> 114 us
  waiting for transfers between devices: 21.2 us -> 26.5 us
  other arithmetic: 6.68 us -> 3.51 us
  starting transfers between devices: 9.36 us -> 7.46 us
    pallas_call x1, Pallas kernels: 16.8 us -> 10.2 us  [operator_tables(): pl.pallas_call(functools.partial(table_kernel, which), out_shape=[jax.Sha...]
    ppermute x8 -> x7, waiting for transfers between devices: 5.49 us -> 9.78 us  [swapped(): lax.ppermute(block, 'row', [(i, i ^ bit) for i in range(lax.axis_size('ro...]
    another operation x1 -> x0, other arithmetic: 2.52 us -> none  [on_device(): jnp.stack([controls[0, 1], controls_next[0, 1], controls_next[0, 0]])]
    convert_element_type x1 -> x0, other arithmetic: 2.18 us -> none  [on_device(): mine = lax.dynamic_slice_in_dim(terminal[0], here, 2 * width, 1).astype(F32)]
    ppermute x4 -> x3, starting transfers between devices: 5.13 us -> 3.85 us  [shifted_down(): return lax.ppermute(block, axis, route)]
    ppermute x4 -> x3, waiting for transfers between devices: 15.7 us -> 16.7 us  [shifted_down(): return lax.ppermute(block, axis, route)]
    ppermute x8 -> x7, starting transfers between devices: 4.22 us -> 3.61 us  [swapped(): lax.ppermute(block, 'row', [(i, i ^ bit) for i in range(lax.axis_size('ro...]
  transfers between devices with their start and end apart: 12 -> 10, of which waited for: 4 -> 6; matrix products, arithmetic and copies ran while one was open for 11% -> 8% of each run, Pallas kernels for 29% -> 26%
where the time goes in v5:
time: 164 us
  Pallas kernels  114 us (70%)
  waiting for transfers between devices  26.5 us (16%)
  local copies, waits for them, and re-layouts  12.3 us (8%)
  starting transfers between devices  7.46 us (5%)
  other arithmetic  3.51 us (2%)
    pallas_call x2, Pallas kernels, step_call(): pl.pallas_call(functools.partial(kernel, counts, tile, len(pieces)), out_...  104 us
    ppermute x3, waiting for transfers between devices, shifted_down(): return lax.ppermute(block, axis, route)  16.7 us
    pallas_call x1, Pallas kernels, operator_tables(): pl.pallas_call(functools.partial(table_kernel, which), out_shape=[jax.Sha...  10.2 us
    ppermute x7, waiting for transfers between devices, swapped(): lax.ppermute(block, 'row', [(i, i ^ bit) for i in range(lax.axis_size('ro...  9.78 us
    unnamed x16, local copies, waits for them, and re-layouts  9.14 us
    ppermute x3, starting transfers between devices, shifted_down(): return lax.ppermute(block, axis, route)  3.85 us
    ppermute x7, starting transfers between devices, swapped(): lax.ppermute(block, 'row', [(i, i ^ bit) for i in range(lax.axis_size('ro...  3.61 us
  transfers between devices with their start and end apart: 10, of which 6 were waited for; matrix products, arithmetic and copies ran while one was open for 8% of the time, Pallas kernels for 26%

profile of v5, /device:TPU:0, one launch (start us, length us, event | category | flops | bytes accessed | tf_op | source)
XLA Modules:
  0.0 164.2 jit_solution(11209871312392949273)
XLA Ops:
  0.6 0.5 collective-permute-start.5
  1.1 1.3 collective-permute-start.1
  2.5 2.9 %fusion = bf16[1024,512]{1,0:T(8,128)(2,1)} fusion(bf16[1,2,2048,512]{3,2,1,0:T(8,128)(2,1)} %terminal.3, s32[]{:T(128)S(6)} %select_n.19), kind=kLoop, calls=%fused_computation.2 | loop fusion | flops 2097152 | bytes 3145732 | tf_op jit(solution)/shard_map/convert_element_type | solution.py:361
  5.3 2.5 %collective-permute-start = (bf16[1024,512]{1,0:T(8,128)(2,1)}, bf16[1024,512]{1,0:T(8,128)(2,1)}, u32[]{:S(2)}, u32[]{:S(2)}) collective-permute-start(bf16[1024,512]{1,0:T(8,128)(2,1)} %fusion), channel_id=1, source_target_pairs={{0,2},{1,3},{2,0},{3,1},{4,6},{5,7},{6,4},{7,5},{8,10},{9,11},{10,... | collective-permute-start | bytes 3145736 | tf_op jit(solution)/shard_map/ppermute | solution.py:323
  7.8 0.0 copy-start.2
  7.8 3.1 %dynamic-slice_bitcast_fusion = bf16[2,1024,512]{2,1,0:T(8,128)(2,1)} fusion(bf16[1,2,2048,512]{3,2,1,0:T(8,128)(2,1)} %terminal.3, s32[]{:T(128)S(6)} %select_n.20), kind=kLoop, calls=%fused_computation | loop fusion | bytes 4194308 | tf_op jit(solution)/shard_map/squeeze | solution.py:362
  11.0 0.0 collective-permute-done.1.controls_next
  11.0 0.0 copy-start.6
  11.0 1.3 collective-permute-start.2
  12.3 1.3 collective-permute-start.3
  13.6 0.0 copy-done.2
  13.6 3.9 %copy.8.ham = bf16[2,64,2,32,32]{4,3,2,1,0:T(8,128)(2,1)} copy(bf16[2,64,2,32,32]{1,4,3,2,0:T(8,128)(2,1)S(1)} %copy-done.2) | data formatting | bytes 1048576 | tf_op args[2]
  17.5 3.4 %copy.9.jump = bf16[64,2,32,32]{3,2,1,0:T(8,128)(2,1)} copy(bf16[64,2,32,32]{0,3,2,1:T(8,128)(2,1)} %param.10) | data formatting | bytes 524288 | tf_op args[4]
  20.9 0.0 copy-done.6
  20.9 10.2 %operator_tables.1 = (s32[9,64]{1,0:T(8,128)}, bf16[64,32,64]{2,1,0:T(8,128)(2,1)}, bf16[64,32,224]{2,1,0:T(8,128)(2,1)}, bf16[64,32,224]{2,1,0:T(8,128)(2,1)}, ...) custom-call(s32[2,64]{1,0:T(2,128)} %ham_cols.1, ...), custom_call_target="tpu_custom_call" | custom-call | flops 1 | bytes 1 | tf_op jit(solution)/shard_map/operator_tables/pallas_call | solution.py:75
  31.1 0.8 collective-permute-done.refs_2_
  32.0 7.9 %collective-permute-done.2.refs_0_ = bf16[1024,512]{1,0:T(8,128)(2,1)} collective-permute-done((bf16[1024,512]{1,0:T(8,128)(2,1)}, bf16[1024,512]{1,0:T(8,128)(2,1)}, u32[]{:S(2)}, u32[]{:S(2)}) %collective-permute-start.2) | collective-permute-done | bytes 1048608 | tf_op jit(solution)/shard_map/ppermute | solution.py:17
  39.8 0.0 collective-permute-start.6
  39.8 0.1 collective-permute-start.4
  39.9 0.6 pad_add_fusion.place
  40.5 2.3 %collective-permute-done.6.refs_3_ = bf16[1024,512]{1,0:T(8,128)(2,1)} collective-permute-done((bf16[1024,512]{1,0:T(8,128)(2,1)}, bf16[1024,512]{1,0:T(8,128)(2,1)}, u32[]{:S(2)}, u32[]{:S(2)}) %collective-permute-start.6) | collective-permute-done | bytes 1048608 | tf_op jit(solution)/shard_map/ppermute | solution.py:323
  42.8 0.0 collective-permute-done.5.refs_1_
  42.8 32.2 %inner_point.1 = bf16[1,2,2048,512]{3,2,1,0:T(8,128)(2,1)} custom-call(s32[9,64]{1,0:T(8,128)} %get-tuple-element.20.rows, s32[4]{0:T(128)} %pad_add_fusion.place, bf16[1,2,2048,512]{3,2,1,0:T(8,128)(2,1)} %terminal.3, bf16[64,32,224]{2,1,0:T(8,128)(2,1)} %get-tuple-element.28.plus, bf16[64,32,224]{2,1,0:T(8,128)(2,1)} %get-tuple-element.29.minus, ...), custom_call_target="tpu_custom_call" | custom-call | flops 1 | bytes 1 | tf_op jit(solution)/shard_map/inner_point/pallas_call | solution.py:344
  75.1 0.0 collective-permute-done.4.refs_2_
  75.1 0.0 copy-start.3
  75.1 8.8 %collective-permute-done.3.refs_1_ = bf16[2,1024,512]{2,1,0:T(8,128)(2,1)S(1)} collective-permute-done((bf16[2,1024,512]{2,1,0:T(8,128)(2,1)}, bf16[2,1024,512]{2,1,0:T(8,128)(2,1)S(1)}, u32[]{:S(2)}, u32[]{:S(2)}) %collective-permute-start.3) | collective-permute-done | bytes 2097184 | tf_op jit(solution)/shard_map/ppermute | solution.py:17
  83.9 0.0 copy-start
  83.9 0.0 collective-permute-start.8
  83.9 0.5 collective-permute-start.7
  84.4 0.0 collective-permute-start.9
  84.4 6.5 %collective-permute-done.7.refs_3_ = bf16[1024,512]{1,0:T(8,128)(2,1)S(1)} collective-permute-done((bf16[1024,512]{1,0:T(8,128)(2,1)}, bf16[1024,512]{1,0:T(8,128)(2,1)S(1)}, u32[]{:S(2)}, u32[]{:S(2)}) %collective-permute-start.7) | collective-permute-done | bytes 1048608 | tf_op jit(solution)/shard_map/ppermute | solution.py:323
  90.9 0.0 copy-start.4
  90.9 0.2 collective-permute-done.9.refs_5_
  91.1 0.0 copy-start.5
  91.1 0.0 collective-permute-done.8.refs_4_
  91.1 0.0 copy-start.1
  91.1 1.4 copy-done.1
  92.5 0.0 copy-done.4
  92.6 0.3 copy-done.5
  92.9 0.0 copy-done.3
  92.9 0.0 copy-done
  92.9 71.3 %left_end.1 = bf16[1,2,2048,512]{3,2,1,0:T(8,128)(2,1)} custom-call(s32[9,64]{1,0:T(8,128)} %get-tuple-element.20.rows, s32[4]{0:T(128)} %pad_add_fusion.place, bf16[1,2,2048,512]{3,2,1,0:T(8,128)(2,1)} %terminal.3, bf16[64,32,224]{2,1,0:T(8,128)(2,1)} %get-tuple-element.21.plus, bf16[64,32,224]{2,1,0:T(8,128)(2,1)} %get-tuple-element.22.minus, ...), custom_call_target="tpu_custom_call" | custom-call | flops 1 | bytes 1 | tf_op jit(solution)/shard_map/left_end/pallas_call | solution.py:344
Async XLA Ops:
  0.6 42.2 %collective-permute-start.5 = (bf16[1,2,2048,512]{3,2,1,0:T(8,128)(2,1)}, bf16[1,2,2048,512]{3,2,1,0:T(8,128)(2,1)}, u32[]{:S(2)}, u32[]{:S(2)}) collective-permute-start(bf16[1,2,2048,512]{3,2,1,0:T(8,128)(2,1)} %terminal.3), channel_id=1, source_target_pairs={{0,1},{1,0},{2,3},{3,2},{4,5},{5,4},{6,7},{7,6},{8,9},{9,8},{10,11... | collective-permute-start | bytes 12582920 | tf_op jit(solution)/shard_map/ppermute | solution.py:323
  1.1 9.8 %collective-permute-start.1 = (f32[1,2]{1,0:T(1,128)}, f32[1,2]{1,0:T(1,128)S(1)}, u32[]{:S(2)}, u32[]{:S(2)}) collective-permute-start(f32[1,2]{1,0:T(1,128)} %controls.1), channel_id=1, source_target_pairs={{4,0},{8,4},{12,8},{5,1},{9,5},{13,9},{6,2},{10,6},{14,10},{7,3},{... | collective-permute-start | bytes 32 | tf_op jit(solution)/shard_map/ppermute | solution.py:17
  5.3 26.6 %collective-permute-start = (bf16[1024,512]{1,0:T(8,128)(2,1)}, bf16[1024,512]{1,0:T(8,128)(2,1)}, u32[]{:S(2)}, u32[]{:S(2)}) collective-permute-start(bf16[1024,512]{1,0:T(8,128)(2,1)} %fusion), channel_id=1, source_target_pairs={{0,2},{1,3},{2,0},{3,1},{4,6},{5,7},{6,4},{7,5},{8,10},{9,11},{10,... | collective-permute-start | bytes 3145736 | tf_op jit(solution)/shard_map/ppermute | solution.py:323
  7.8 5.7 %copy-start.2 = (bf16[2,64,2,32,32]{1,4,3,2,0:T(8,128)(2,1)S(1)}, bf16[2,64,2,32,32]{1,4,3,2,0:T(8,128)(2,1)}, u32[]{:S(2)}) copy-start(bf16[2,64,2,32,32]{1,4,3,2,0:T(8,128)(2,1)} %param.8) | copy-start | bytes 1572868
  11.0 9.9 %copy-start.6 = (f32[1,2]{1,0:T(1,128)}, f32[1,2]{1,0:T(1,128)S(1)}, u32[]{:S(2)}) copy-start(f32[1,2]{1,0:T(1,128)S(1)} %collective-permute-done.1.controls_next) | copy-start | bytes 28
  11.0 28.8 %collective-permute-start.2 = (bf16[1024,512]{1,0:T(8,128)(2,1)}, bf16[1024,512]{1,0:T(8,128)(2,1)}, u32[]{:S(2)}, u32[]{:S(2)}) collective-permute-start(bf16[1024,512]{1,0:T(8,128)(2,1)} %fusion), channel_id=1, source_target_pairs={{4,0},{8,4},{12,8},{5,1},{9,5},{13,9},{6,2},{10,6},{14,10},{7,3},{... | collective-permute-start | bytes 3145736 | tf_op jit(solution)/shard_map/ppermute | solution.py:17
  12.3 71.6 %collective-permute-start.3 = (bf16[2,1024,512]{2,1,0:T(8,128)(2,1)}, bf16[2,1024,512]{2,1,0:T(8,128)(2,1)S(1)}, u32[]{:S(2)}, u32[]{:S(2)}) collective-permute-start(bf16[2,1024,512]{2,1,0:T(8,128)(2,1)} %dynamic-slice_bitcast_fusion), channel_id=1, source_target_pairs={{4,0},{8,4},{12,8},{5,1},{9,5},{13,9},{6,2},{10,6},{14,10},{7,3},{... | collective-permute-start | bytes 6291464 | tf_op jit(solution)/shard_map/ppermute | solution.py:17
  39.8 3.0 %collective-permute-start.6 = (bf16[1024,512]{1,0:T(8,128)(2,1)}, bf16[1024,512]{1,0:T(8,128)(2,1)}, u32[]{:S(2)}, u32[]{:S(2)}) collective-permute-start(bf16[1024,512]{1,0:T(8,128)(2,1)} %collective-permute-done.refs_2_), channel_id=1, source_target_pairs={{0,1},{1,0},{2,3},{3,2},{4,5},{5,4},{6,7},{7,6},{8,9},{9,8},{10,11... | collective-permute-start | bytes 3145736 | tf_op jit(solution)/shard_map/ppermute | solution.py:323
  39.8 35.2 %collective-permute-start.4 = (bf16[1024,512]{1,0:T(8,128)(2,1)}, bf16[1024,512]{1,0:T(8,128)(2,1)S(1)}, u32[]{:S(2)}, u32[]{:S(2)}) collective-permute-start(bf16[1024,512]{1,0:T(8,128)(2,1)} %collective-permute-done.2.refs_0_), channel_id=1, source_target_pairs={{0,2},{1,3},{2,0},{3,1},{4,6},{5,7},{6,4},{7,5},{8,10},{9,11},{10,... | collective-permute-start | bytes 3145736 | tf_op jit(solution)/shard_map/ppermute | solution.py:323
  75.1 17.8 %copy-start.3 = (bf16[1024,512]{1,0:T(8,128)(2,1)}, bf16[1024,512]{1,0:T(8,128)(2,1)S(1)}, u32[]{:S(2)}) copy-start(bf16[1024,512]{1,0:T(8,128)(2,1)S(1)} %collective-permute-done.4.refs_2_) | copy-start | bytes 3145732
  83.9 9.0 %copy-start = (bf16[2,1024,512]{2,1,0:T(8,128)(2,1)}, bf16[2,1024,512]{2,1,0:T(8,128)(2,1)S(1)}, u32[]{:S(2)}) copy-start(bf16[2,1024,512]{2,1,0:T(8,128)(2,1)S(1)} %collective-permute-done.3.refs_1_) | copy-start | bytes 6291460
  83.9 7.2 %collective-permute-start.8 = (bf16[2,1024,512]{2,1,0:T(8,128)(2,1)S(1)}, bf16[2,1024,512]{2,1,0:T(8,128)(2,1)S(1)}, u32[]{:S(2)}, u32[]{:S(2)}) collective-permute-start(bf16[2,1024,512]{2,1,0:T(8,128)(2,1)S(1)} %collective-permute-done.3.refs_1_), channel_id=1, source_target_pairs={{0,1},{1,0},{2,3},{3,2},{4,5},{5,4},{6,7},{7,6},{8,9},{9,8},{10,11... | collective-permute-start | bytes 6291464 | tf_op jit(solution)/shard_map/ppermute | solution.py:323
  83.9 7.0 %collective-permute-start.7 = (bf16[1024,512]{1,0:T(8,128)(2,1)}, bf16[1024,512]{1,0:T(8,128)(2,1)S(1)}, u32[]{:S(2)}, u32[]{:S(2)}) collective-permute-start(bf16[1024,512]{1,0:T(8,128)(2,1)} %collective-permute-done.2.refs_0_), channel_id=1, source_target_pairs={{0,1},{1,0},{2,3},{3,2},{4,5},{5,4},{6,7},{7,6},{8,9},{9,8},{10,11... | collective-permute-start | bytes 3145736 | tf_op jit(solution)/shard_map/ppermute | solution.py:323
  84.4 6.6 %collective-permute-start.9 = (bf16[1024,512]{1,0:T(8,128)(2,1)S(1)}, bf16[1024,512]{1,0:T(8,128)(2,1)S(1)}, u32[]{:S(2)}, u32[]{:S(2)}) collective-permute-start(bf16[1024,512]{1,0:T(8,128)(2,1)S(1)} %collective-permute-done.4.refs_2_), channel_id=1, source_target_pairs={{0,1},{1,0},{2,3},{3,2},{4,5},{5,4},{6,7},{7,6},{8,9},{9,8},{10,11... | collective-permute-start | bytes 3145736 | tf_op jit(solution)/shard_map/ppermute | solution.py:323
  90.9 1.7 %copy-start.4 = (bf16[1024,512]{1,0:T(8,128)(2,1)}, bf16[1024,512]{1,0:T(8,128)(2,1)S(1)}, u32[]{:S(2)}) copy-start(bf16[1024,512]{1,0:T(8,128)(2,1)S(1)} %collective-permute-done.7.refs_3_) | copy-start | bytes 3145732
  91.1 1.8 %copy-start.5 = (bf16[1024,512]{1,0:T(8,128)(2,1)}, bf16[1024,512]{1,0:T(8,128)(2,1)S(1)}, u32[]{:S(2)}) copy-start(bf16[1024,512]{1,0:T(8,128)(2,1)S(1)} %collective-permute-done.9.refs_5_) | copy-start | bytes 3145732
  91.1 1.5 copy-start.1

commit v6 on v5

--- a/solution.py
+++ b/solution.py
@@ -17,11 +17,16 @@
     return lax.ppermute(block, axis, route)
 
 
+def group_of(layers_j, size):
+    return max(256 // (layers_j * size), 1)
+
+
 def table_kernel(which, ham_cols, jump_cols, controls, controls_next, ham, jump, rows, jump_row, *tables):
     layers_h, count = ham_cols.shape
     layers_j = jump_cols.shape[0]
     size = ham.shape[-1]
     crossed = [(k, other) for k in range(layers_j) for other in range(layers_j) if k != other]
+    group = jump_row.shape[1] // size
     first_k = 2 * layers_h
     first_j = first_k + 1 + len(crossed)
 
@@ -47,7 +52,9 @@
             return jnp.concatenate(parts, axis=1)
 
         turned = [jump[came_j[k], k].astype(F32).T.astype(BF16) for k in range(layers_j)]
-        jump_row[c] = jnp.concatenate(turned, axis=1)
+        jump_row[c // group, pl.ds(c % group * size, size), :] = jnp.concatenate(
+            [jnp.where(c % group == v, piece, jnp.zeros_like(piece)) for v in range(group) for piece in turned], axis=1
+        )
         square = sum(
             jnp.dot(turned[k], jump[came_j[k], k], preferred_element_type=F32) for k in range(layers_j)
         )
@@ -72,11 +79,12 @@
     vmem = pl.BlockSpec(memory_space=pltpu.VMEM)
     table = jax.ShapeDtypeStruct((count, size, (2 * layers_h + layers_k) * size), BF16)
     number = len(which)
+    group = group_of(layers_j, size)
     rows, jump_row, *tables = pl.pallas_call(
         functools.partial(table_kernel, which),
         out_shape=[
             jax.ShapeDtypeStruct((2 * layers_h + layers_k + layers_j, count), jnp.int32),
-            jax.ShapeDtypeStruct((count, size, layers_j * size), BF16),
+            jax.ShapeDtypeStruct((count // group, group * size, group * layers_j * size), BF16),
         ] + [table] * (2 * number),
         in_specs=[smem, smem, smem, smem, vmem, vmem],
         out_specs=[smem, vmem] + [vmem] * (2 * number),
@@ -91,6 +99,7 @@
     def __init__(self, rows, counts, size, plus, minus, jump):
         self.rows, self.counts, self.size = rows, counts, size
         self.plus, self.minus, self.jump = plus, minus, jump
+        self.group = jump.shape[1] // size
 
     def take(self, ref, kind, c, cols):
         first = sum(self.counts[:kind])
@@ -103,9 +112,14 @@
         met = jnp.concatenate(self.take(ham_ref, 0, c, cols) + self.take(decay_ref, 1, c, cols), axis=0)
         return jnp.dot(table[c], met, preferred_element_type=F32)
 
-    def pull(self, c, ref, cols):
-        met = jnp.concatenate(self.take(ref, 2, c, cols), axis=0)
-        return jnp.dot(self.jump[c], met, preferred_element_type=F32)
+    def pull(self, q, ref, cols):
+        met = jnp.concatenate(sum((self.take(ref, 2, q * self.group + v, cols) for v in range(self.group)), []), axis=0)
+        return jnp.dot(self.jump[q], met, preferred_element_type=F32)
+
+    def flat(self, kind, table, q, cols, *refs):
+        if kind == "pull":
+            return [self.pull(q, *refs, cols)]
+        return [self.ham(table, q * self.group + v, *refs, cols) for v in range(self.group)]
 
 
 def turn_whole(source, target, tile):
@@ -204,22 +218,25 @@
             d_ref[there_j, there_i] = block.T
 
 
+def put_turned(step, target, cols, to, first, count, kind, table, *refs):
+    rows = sum((step.flat(kind, table, first + v, cols, *refs) for v in range(count)), [])
+    target[cols, to] = jnp.concatenate([piece.astype(BF16) for piece in rows], axis=0).T
+
+
 def whole_step(step, c_ref, d_ref, r_ref, x_ref, c_new, d_new, tile):
     n = c_ref.shape[0]
-    count = tile // step.size
-    products = (
-        (r_ref, lambda c, cols: step.ham(step.minus, c, c_ref, d_ref, cols)),
-        (x_ref, lambda c, cols: step.pull(c, d_ref, cols)),
-    )
+    size = step.size
+    count = tile // (step.group * size)
 
     @pl.loop(0, n // tile)
     def _(g):
+        to = part_of(0, g, tile)
+
         @pl.loop(0, n // tile, unroll=2)
         def _(s):
             cols = part_of(0, s, tile)
-            for target, product in products:
-                rows = [product(g * count + u, cols).astype(BF16) for u in range(count)]
-                target[cols, part_of(0, g, tile)] = jnp.concatenate(rows, axis=0).T
+            put_turned(step, r_ref, cols, to, g * count, count, "ham", step.minus, c_ref, d_ref)
+            put_turned(step, x_ref, cols, to, g * count, count, "pull", None, d_ref)
 
     @pl.loop(0, n // tile)
     def _(g):
@@ -227,51 +244,57 @@
         def _(s):
             cols = part_of(0, s, tile)
             made = []
-            for u in range(count):
-                c = g * count + u
-                own = pl.ds(pl.multiple_of(c * step.size, step.size), step.size)
-                change = step.ham(step.plus, c, d_ref, c_ref, cols) + step.pull(c, x_ref, cols)
-                change = change + r_ref[own, cols].astype(F32)
-                made.append((c_ref[own, cols].astype(F32) + time_step * change).astype(BF16))
-                c_new[own, cols] = made[u]
+            for q in range(count):
+                pulled = step.pull(g * count + q, x_ref, cols)
+                for v in range(step.group):
+                    c = (g * count + q) * step.group + v
+                    own = pl.ds(pl.multiple_of(c * size, size), size)
+                    change = step.ham(step.plus, c, d_ref, c_ref, cols) + pulled[v * size : (v + 1) * size]
+                    change = change + r_ref[own, cols].astype(F32)
+                    made.append((c_ref[own, cols].astype(F32) + time_step * change).astype(BF16))
+                    c_new[own, cols] = made[-1]
             d_new[cols, part_of(0, g, tile)] = jnp.concatenate(made, axis=0).T
 
 
 def own_step(step, start, width, c_ref, d_ref, turned, tile, base, out):
     n = c_ref.shape[0]
     part = min(tile, width)
-    products = (
-        lambda c, cols: step.ham(step.minus, c, c_ref, d_ref, cols),
-        lambda c, cols: step.ham(step.plus, c, d_ref, c_ref, cols),
-        lambda c, cols: step.pull(c, d_ref, cols),
-        lambda c, cols: step.pull(c, c_ref, cols),
+    size = step.size
+    deep = step.group * size
+    count = part // deep
+    kinds = (
+        ("ham", step.minus, c_ref, d_ref),
+        ("ham", step.plus, d_ref, c_ref),
+        ("pull", None, d_ref),
+        ("pull", None, c_ref),
     )
 
     @pl.loop(0, width // part)
     def _(g):
-        first = start // step.size + g * (part // step.size)
-
         @pl.loop(0, n // tile)
         def _(s):
-            cols = part_of(0, s, tile)
-            for k, product in enumerate(products):
-                rows = [product(first + u, cols).astype(BF16) for u in range(part // step.size)]
-                turned[cols, part_of(k * width, g, part)] = jnp.concatenate(rows, axis=0).T
-
-    @pl.loop(0, n // step.size, unroll=4)
-    def _(c):
-        own = pl.ds(pl.multiple_of(c * step.size, step.size), step.size)
+            for k, kind in enumerate(kinds):
+                to = part_of(k * width, g, part)
+                put_turned(step, turned, part_of(0, s, tile), to, start // deep + g * count, count, *kind)
+
+    @pl.loop(0, n // deep)
+    def _(q):
         for s in range(width // part):
             cols = pl.ds(pl.multiple_of(start + s * part, part), part)
             to = pl.ds(s * part, part)
             of = [pl.ds(k * width + s * part, part) for k in range(4)]
-            change = step.ham(step.plus, c, d_ref, c_ref, cols) + step.pull(c, turned, of[2])
-            second = step.ham(step.minus, c, c_ref, d_ref, cols) + step.pull(c, turned, of[3])
-            change = change + turned[own, of[0]].astype(F32)
-            second = second + turned[own, of[1]].astype(F32)
-            real, imag = base(own, cols, to)
-            out[0, 0, own, to] = (real + 0.5 * time_step * (change + second)).astype(BF16)
-            out[0, 1, own, to] = (imag + 0.5 * time_step * (change - second)).astype(BF16)
+            pulled = [step.pull(q, turned, of[k]) for k in (2, 3)]
+            for v in range(step.group):
+                c = q * step.group + v
+                own = pl.ds(pl.multiple_of(c * size, size), size)
+                here = slice(v * size, (v + 1) * size)
+                change = step.ham(step.plus, c, d_ref, c_ref, cols) + pulled[0][here]
+                second = step.ham(step.minus, c, c_ref, d_ref, cols) + pulled[1][here]
+                change = change + turned[own, of[0]].astype(F32)
+                second = second + turned[own, of[1]].astype(F32)
+                real, imag = base(own, cols, to)
+                out[0, 0, own, to] = (real + 0.5 * time_step * (change + second)).astype(BF16)
+                out[0, 1, own, to] = (imag + 0.5 * time_step * (change - second)).astype(BF16)
 
 
 def fill_whole(piece, c_ref, d_ref, sems, tile):
@@ -359,15 +382,18 @@
         size = (1, 1, 2 * width, width)
         mine = [lax.dynamic_slice(terminal, (0, k, here, 0), size)[0, 0].astype(F32) for k in range(2)]
         mixed = (mine[0] + mine[1]).astype(BF16)
+        far = swapped(mixed, 2)
+        mixed, _ = lax.optimization_barrier((mixed, controls_next))
+        mixed = shifted_down(mixed, "tm")
         apart = lax.dynamic_slice(terminal, (0, 0, 2 * width - here, 0), (1, 2, 2 * width, width))[0]
-        far = swapped(mixed, 2)
-        mixed, apart, _ = lax.optimization_barrier((mixed, apart, controls_next))
-        mixed, apart = shifted_down(mixed, "tm"), shifted_down(apart, "tm")
-        far, rows, mixed = lax.optimization_barrier((far, rows, mixed))
+        apart = shifted_down(apart, "tm")
+        far, rows = lax.optimization_barrier((far, rows))
+        far_pair = swapped(far, 1)
+        rows, mixed = lax.optimization_barrier((rows, mixed))
         far_next = swapped(mixed, 2)
-        new_fpoint = step_call(inner_kernel, "inner_point", vmem, 4, first, [terminal, near_pair, far, swapped(far, 1)])
+        new_fpoint = step_call(inner_kernel, "inner_point", vmem, 4, first, [terminal, near_pair, far, far_pair])
         mixed_pair = swapped(mixed, 1)
-        apart, far_next, new_fpoint = lax.optimization_barrier((apart, far_next, new_fpoint))
+        apart, far_next, mixed_pair, new_fpoint = lax.optimization_barrier((apart, far_next, mixed_pair, new_fpoint))
         pieces = [mixed, apart, far_next, mixed_pair, swapped(apart, 1), swapped(far_next, 1)]
     else:
         mixed = (terminal[0, 0].astype(F32) + terminal[0, 1].astype(F32)).astype(BF16)

time: 164 us -> 162 us (0.988)
  waiting for transfers between devices: 26.5 us -> 23.7 us
    ppermute x7, waiting for transfers between devices: 9.78 us -> 5.16 us  [swapped(): lax.ppermute(block, 'row', [(i, i ^ bit) for i in range(lax.axis_size('ro...]
    ppermute x3, waiting for transfers between devices: 16.7 us -> 18.6 us  [shifted_down(): return lax.ppermute(block, axis, route)]
  transfers between devices with their start and end apart: 10 -> 10, of which waited for: 6 -> 4; matrix products, arithmetic and copies ran while one was open for 8% -> 9% of each run, Pallas kernels for 26% -> 27%
where the time goes in v6:
time: 162 us; the launch traced here: 161 us
  Pallas kernels  114 us (70%)
  waiting for transfers between devices  23.7 us (15%)
  local copies, waits for them, and re-layouts  12 us (7%)
  starting transfers between devices  7.6 us (5%)
  other arithmetic  3.49 us (2%)
    pallas_call x2, Pallas kernels, step_call(): pl.pallas_call(functools.partial(kernel, counts, tile, len(pieces)), out_...  103 us
    ppermute x3, waiting for transfers between devices, shifted_down(): return lax.ppermute(block, axis, route)  18.6 us
    pallas_call x1, Pallas kernels, operator_tables(): pl.pallas_call(functools.partial(table_kernel, which), out_shape=[jax.Sha...  11.1 us
    unnamed x16, local copies, waits for them, and re-layouts  8.99 us
    ppermute x7, waiting for transfers between devices, swapped(): lax.ppermute(block, 'row', [(i, i ^ bit) for i in range(lax.axis_size('ro...  5.16 us
    ppermute x3, starting transfers between devices, shifted_down(): return lax.ppermute(block, axis, route)  3.84 us
    ppermute x7, starting transfers between devices, swapped(): lax.ppermute(block, 'row', [(i, i ^ bit) for i in range(lax.axis_size('ro...  3.75 us
  transfers between devices with their start and end apart: 10, of which 4 were waited for; matrix products, arithmetic and copies ran while one was open for 9% of the time, Pallas kernels for 27%

profile of v6, /device:TPU:0, one launch (start us, length us, event | category | flops | bytes accessed | tf_op | source)
XLA Modules:
  0.0 161.4 jit_solution(14179061773042830801)
XLA Ops:
  0.6 0.0 copy-start.5
  0.6 0.5 collective-permute-start.6
  1.2 2.8 %fusion = bf16[1024,512]{1,0:T(8,128)(2,1)} fusion(bf16[1,2,2048,512]{3,2,1,0:T(8,128)(2,1)} %terminal.3, s32[]{:T(128)S(6)} %select_n.19), kind=kLoop, calls=%fused_computation.2 | loop fusion | flops 2097152 | bytes 3145732 | tf_op jit(solution)/shard_map/convert_element_type | solution.py:384
  4.0 2.5 %collective-permute-start = (bf16[1024,512]{1,0:T(8,128)(2,1)}, bf16[1024,512]{1,0:T(8,128)(2,1)}, u32[]{:S(2)}, u32[]{:S(2)}) collective-permute-start(bf16[1024,512]{1,0:T(8,128)(2,1)} %fusion), channel_id=1, source_target_pairs={{0,2},{1,3},{2,0},{3,1},{4,6},{5,7},{6,4},{7,5},{8,10},{9,11},{10,... | collective-permute-start | bytes 3145736 | tf_op jit(solution)/shard_map/ppermute | solution.py:346
  6.5 0.0 copy-done.5
  6.5 1.3 collective-permute-start.1
  7.8 0.0 copy-start.2
  7.8 4.1 %collective-permute-done.1.controls_next = f32[1,2]{1,0:T(1,128)S(1)} collective-permute-done((f32[1,2]{1,0:T(1,128)S(1)}, f32[1,2]{1,0:T(1,128)S(1)}, u32[]{:S(2)}, u32[]{:S(2)}) %collective-permute-start.1) | collective-permute-done | bytes 40 | tf_op jit(solution)/shard_map/ppermute | solution.py:17
  11.9 0.0 copy-start.6
  11.9 1.3 collective-permute-start.2
  13.2 3.1 %dynamic-slice_bitcast_fusion = bf16[2,1024,512]{2,1,0:T(8,128)(2,1)} fusion(bf16[1,2,2048,512]{3,2,1,0:T(8,128)(2,1)} %terminal.3, s32[]{:T(128)S(6)} %select_n.21), kind=kLoop, calls=%fused_computation | loop fusion | bytes 4194308 | tf_op jit(solution)/shard_map/squeeze | solution.py:388
  16.3 0.0 copy-done.6
  16.3 1.3 collective-permute-start.3
  17.6 0.0 copy-done.2
  17.6 3.9 %copy.8.ham = bf16[2,64,2,32,32]{4,3,2,1,0:T(8,128)(2,1)} copy(bf16[2,64,2,32,32]{1,4,3,2,0:T(8,128)(2,1)S(1)} %copy-done.2) | data formatting | bytes 1048576 | tf_op args[2]
  21.5 3.4 %copy.9.jump = bf16[64,2,32,32]{3,2,1,0:T(8,128)(2,1)} copy(bf16[64,2,32,32]{0,3,2,1:T(8,128)(2,1)} %param.10) | data formatting | bytes 524288 | tf_op args[4]
  24.9 11.1 %operator_tables.1 = (s32[9,64]{1,0:T(8,128)}, bf16[16,128,256]{2,1,0:T(8,128)(2,1)}, bf16[64,32,224]{2,1,0:T(8,128)(2,1)}, bf16[64,32,224]{2,1,0:T(8,128)(2,1)}...) custom-call(s32[2,64]{1,0:T(2,128)} %ham_cols.1, ...), custom_call_target="tpu_custom_call" | custom-call | flops 1 | bytes 1 | tf_op jit(solution)/shard_map/operator_tables/pallas_call | solution.py:83
  36.0 0.0 collective-permute-done.refs_2_
  36.0 0.1 collective-permute-start.7
  36.1 4.1 %collective-permute-done.2.refs_0_ = bf16[1024,512]{1,0:T(8,128)(2,1)} collective-permute-done((bf16[1024,512]{1,0:T(8,128)(2,1)}, bf16[1024,512]{1,0:T(8,128)(2,1)}, u32[]{:S(2)}, u32[]{:S(2)}) %collective-permute-start.2) | collective-permute-done | bytes 1048608 | tf_op jit(solution)/shard_map/ppermute | solution.py:17
  40.2 0.1 collective-permute-start.4
  40.3 0.0 collective-permute-start.5
  40.3 0.7 pad_add_fusion.place
  41.0 0.0 collective-permute-done.7.refs_3_
  41.0 0.0 collective-permute-done.6.refs_1_
  41.0 32.2 %inner_point.1 = bf16[1,2,2048,512]{3,2,1,0:T(8,128)(2,1)} custom-call(s32[9,64]{1,0:T(8,128)} %get-tuple-element.22.rows, s32[4]{0:T(128)} %pad_add_fusion.place, bf16[1,2,2048,512]{3,2,1,0:T(8,128)(2,1)} %terminal.3, bf16[64,32,224]{2,1,0:T(8,128)(2,1)} %get-tuple-element.29.plus, bf16[64,32,224]{2,1,0:T(8,128)(2,1)} %get-tuple-element.30.minus, ...), custom_call_target="tpu_custom_call" | custom-call | flops 1 | bytes 1 | tf_op jit(solution)/shard_map/inner_point/pallas_call | solution.py:367
  73.2 10.3 %collective-permute-done.3.refs_1_ = bf16[2,1024,512]{2,1,0:T(8,128)(2,1)S(1)} collective-permute-done((bf16[2,1024,512]{2,1,0:T(8,128)(2,1)}, bf16[2,1024,512]{2,1,0:T(8,128)(2,1)S(1)}, u32[]{:S(2)}, u32[]{:S(2)}) %collective-permute-start.3) | collective-permute-done | bytes 2097184 | tf_op jit(solution)/shard_map/ppermute | solution.py:17
  83.5 0.0 copy-start
  83.5 0.0 collective-permute-done.4.refs_2_
  83.5 0.0 copy-start.3
  83.5 0.0 collective-permute-done.5.refs_3_
  83.5 0.1 collective-permute-start.8
  83.6 0.5 collective-permute-start.9
  84.1 5.1 %collective-permute-done.9.refs_5_ = bf16[1024,512]{1,0:T(8,128)(2,1)S(1)} collective-permute-done((bf16[1024,512]{1,0:T(8,128)(2,1)S(1)}, bf16[1024,512]{1,0:T(8,128)(2,1)S(1)}, u32[]{:S(2)}, u32[]{:S(2)}) %collective-permute-start.9) | collective-permute-done | bytes 1048608 | tf_op jit(solution)/shard_map/ppermute | solution.py:346
  89.2 0.0 copy-start.4
  89.2 0.0 collective-permute-done.8.refs_4_
  89.2 0.0 copy-start.1
  89.2 1.4 copy-done.1
  90.6 0.3 copy-done.4
  90.9 0.0 copy-done
  90.9 0.0 copy-done.3
  90.9 70.5 %left_end.1 = bf16[1,2,2048,512]{3,2,1,0:T(8,128)(2,1)} custom-call(s32[9,64]{1,0:T(8,128)} %get-tuple-element.22.rows, s32[4]{0:T(128)} %pad_add_fusion.place, bf16[1,2,2048,512]{3,2,1,0:T(8,128)(2,1)} %terminal.3, bf16[64,32,224]{2,1,0:T(8,128)(2,1)} %get-tuple-element.23.plus, bf16[64,32,224]{2,1,0:T(8,128)(2,1)} %get-tuple-element.24.minus, ...), custom_call_target="tpu_custom_call" | custom-call | flops 1 | bytes 1 | tf_op jit(solution)/shard_map/left_end/pallas_call | solution.py:367
Async XLA Ops:
  0.6 5.9 %copy-start.5 = (f32[1,2]{1,0:T(1,128)S(1)}, f32[1,2]{1,0:T(1,128)}, u32[]{:S(2)}) copy-start(f32[1,2]{1,0:T(1,128)} %controls.1) | copy-start | bytes 28
  0.6 40.3 %collective-permute-start.6 = (bf16[1,2,2048,512]{3,2,1,0:T(8,128)(2,1)}, bf16[1,2,2048,512]{3,2,1,0:T(8,128)(2,1)}, u32[]{:S(2)}, u32[]{:S(2)}) collective-permute-start(bf16[1,2,2048,512]{3,2,1,0:T(8,128)(2,1)} %terminal.3), channel_id=1, source_target_pairs={{0,1},{1,0},{2,3},{3,2},{4,5},{5,4},{6,7},{7,6},{8,9},{9,8},{10,11... | collective-permute-start | bytes 12582920 | tf_op jit(solution)/shard_map/ppermute | solution.py:346
  4.0 32.0 %collective-permute-start = (bf16[1024,512]{1,0:T(8,128)(2,1)}, bf16[1024,512]{1,0:T(8,128)(2,1)}, u32[]{:S(2)}, u32[]{:S(2)}) collective-permute-start(bf16[1024,512]{1,0:T(8,128)(2,1)} %fusion), channel_id=1, source_target_pairs={{0,2},{1,3},{2,0},{3,1},{4,6},{5,7},{6,4},{7,5},{8,10},{9,11},{10,... | collective-permute-start | bytes 3145736 | tf_op jit(solution)/shard_map/ppermute | solution.py:346
  6.5 5.4 %collective-permute-start.1 = (f32[1,2]{1,0:T(1,128)S(1)}, f32[1,2]{1,0:T(1,128)S(1)}, u32[]{:S(2)}, u32[]{:S(2)}) collective-permute-start(f32[1,2]{1,0:T(1,128)S(1)} %copy-done.5), channel_id=1, source_target_pairs={{4,0},{8,4},{12,8},{5,1},{9,5},{13,9},{6,2},{10,6},{14,10},{7,3},{... | collective-permute-start | bytes 32 | tf_op jit(solution)/shard_map/ppermute | solution.py:17
  7.8 9.8 %copy-start.2 = (bf16[2,64,2,32,32]{1,4,3,2,0:T(8,128)(2,1)S(1)}, bf16[2,64,2,32,32]{1,4,3,2,0:T(8,128)(2,1)}, u32[]{:S(2)}) copy-start(bf16[2,64,2,32,32]{1,4,3,2,0:T(8,128)(2,1)} %param.8) | copy-start | bytes 1572868
  11.9 4.3 %copy-start.6 = (f32[1,2]{1,0:T(1,128)}, f32[1,2]{1,0:T(1,128)S(1)}, u32[]{:S(2)}) copy-start(f32[1,2]{1,0:T(1,128)S(1)} %collective-permute-done.1.controls_next) | copy-start | bytes 28
  11.9 28.3 %collective-permute-start.2 = (bf16[1024,512]{1,0:T(8,128)(2,1)}, bf16[1024,512]{1,0:T(8,128)(2,1)}, u32[]{:S(2)}, u32[]{:S(2)}) collective-permute-start(bf16[1024,512]{1,0:T(8,128)(2,1)} %fusion), channel_id=1, source_target_pairs={{4,0},{8,4},{12,8},{5,1},{9,5},{13,9},{6,2},{10,6},{14,10},{7,3},{... | collective-permute-start | bytes 3145736 | tf_op jit(solution)/shard_map/ppermute | solution.py:17
  16.3 67.2 %collective-permute-start.3 = (bf16[2,1024,512]{2,1,0:T(8,128)(2,1)}, bf16[2,1024,512]{2,1,0:T(8,128)(2,1)S(1)}, u32[]{:S(2)}, u32[]{:S(2)}) collective-permute-start(bf16[2,1024,512]{2,1,0:T(8,128)(2,1)} %dynamic-slice_bitcast_fusion), channel_id=1, source_target_pairs={{4,0},{8,4},{12,8},{5,1},{9,5},{13,9},{6,2},{10,6},{14,10},{7,3},{... | collective-permute-start | bytes 6291464 | tf_op jit(solution)/shard_map/ppermute | solution.py:17
  36.0 4.9 %collective-permute-start.7 = (bf16[1024,512]{1,0:T(8,128)(2,1)}, bf16[1024,512]{1,0:T(8,128)(2,1)}, u32[]{:S(2)}, u32[]{:S(2)}) collective-permute-start(bf16[1024,512]{1,0:T(8,128)(2,1)} %collective-permute-done.refs_2_), channel_id=1, source_target_pairs={{0,1},{1,0},{2,3},{3,2},{4,5},{5,4},{6,7},{7,6},{8,9},{9,8},{10,11... | collective-permute-start | bytes 3145736 | tf_op jit(solution)/shard_map/ppermute | solution.py:346
  40.2 43.2 %collective-permute-start.4 = (bf16[1024,512]{1,0:T(8,128)(2,1)}, bf16[1024,512]{1,0:T(8,128)(2,1)S(1)}, u32[]{:S(2)}, u32[]{:S(2)}) collective-permute-start(bf16[1024,512]{1,0:T(8,128)(2,1)} %collective-permute-done.2.refs_0_), channel_id=1, source_target_pairs={{0,2},{1,3},{2,0},{3,1},{4,6},{5,7},{6,4},{7,5},{8,10},{9,11},{10,... | collective-permute-start | bytes 3145736 | tf_op jit(solution)/shard_map/ppermute | solution.py:346
  40.3 43.2 %collective-permute-start.5 = (bf16[1024,512]{1,0:T(8,128)(2,1)}, bf16[1024,512]{1,0:T(8,128)(2,1)}, u32[]{:S(2)}, u32[]{:S(2)}) collective-permute-start(bf16[1024,512]{1,0:T(8,128)(2,1)} %collective-permute-done.2.refs_0_), channel_id=1, source_target_pairs={{0,1},{1,0},{2,3},{3,2},{4,5},{5,4},{6,7},{7,6},{8,9},{9,8},{10,11... | collective-permute-start | bytes 3145736 | tf_op jit(solution)/shard_map/ppermute | solution.py:346
  83.5 7.4 %copy-start = (bf16[2,1024,512]{2,1,0:T(8,128)(2,1)}, bf16[2,1024,512]{2,1,0:T(8,128)(2,1)S(1)}, u32[]{:S(2)}) copy-start(bf16[2,1024,512]{2,1,0:T(8,128)(2,1)S(1)} %collective-permute-done.3.refs_1_) | copy-start | bytes 6291460
  83.5 7.4 %copy-start.3 = (bf16[1024,512]{1,0:T(8,128)(2,1)}, bf16[1024,512]{1,0:T(8,128)(2,1)S(1)}, u32[]{:S(2)}) copy-start(bf16[1024,512]{1,0:T(8,128)(2,1)S(1)} %collective-permute-done.4.refs_2_) | copy-start | bytes 3145732
  83.5 5.7 %collective-permute-start.8 = (bf16[2,1024,512]{2,1,0:T(8,128)(2,1)S(1)}, bf16[2,1024,512]{2,1,0:T(8,128)(2,1)S(1)}, u32[]{:S(2)}, u32[]{:S(2)}) collective-permute-start(bf16[2,1024,512]{2,1,0:T(8,128)(2,1)S(1)} %collective-permute-done.3.refs_1_), channel_id=1, source_target_pairs={{0,1},{1,0},{2,3},{3,2},{4,5},{5,4},{6,7},{7,6},{8,9},{9,8},{10,11... | collective-permute-start | bytes 6291464 | tf_op jit(solution)/shard_map/ppermute | solution.py:346
  83.6 5.6 %collective-permute-start.9 = (bf16[1024,512]{1,0:T(8,128)(2,1)S(1)}, bf16[1024,512]{1,0:T(8,128)(2,1)S(1)}, u32[]{:S(2)}, u32[]{:S(2)}) collective-permute-start(bf16[1024,512]{1,0:T(8,128)(2,1)S(1)} %collective-permute-done.4.refs_2_), channel_id=1, source_target_pairs={{0,1},{1,0},{2,3},{3,2},{4,5},{5,4},{6,7},{7,6},{8,9},{9,8},{10,11... | collective-permute-start | bytes 3145736 | tf_op jit(solution)/shard_map/ppermute | solution.py:346
  89.2 1.6 %copy-start.4 = (bf16[1024,512]{1,0:T(8,128)(2,1)}, bf16[1024,512]{1,0:T(8,128)(2,1)S(1)}, u32[]{:S(2)}) copy-start(bf16[1024,512]{1,0:T(8,128)(2,1)S(1)} %collective-permute-done.9.refs_5_) | copy-start | bytes 3145732
  89.2 1.4 copy-start.1

commit v7 on v6

--- a/solution.py
+++ b/solution.py
@@ -92,7 +92,7 @@
         cost_estimate=pl.CostEstimate(flops=1, bytes_accessed=1, transcendentals=0),
         name="operator_tables",
     )(ham_cols, jump_cols, controls, controls_next, ham_blocks, jump_blocks)
-    return (2 * layers_h, layers_k, layers_j), rows, jump_row, tables[0::2], tables[1::2]
+    return (2 * layers_h, layers_k, layers_j), rows, jump_row, *tables
 
 
 class Step:
@@ -302,22 +302,29 @@
     turn_whole(c_ref, d_ref, tile)
 
 
-def inner_kernel(counts, tile, number, rows, place, terminal, plus, minus, jump, *refs):
+def inner_kernel(counts, tile, number, rows, place, terminal, jump, plus, minus, *refs):
     pieces, refs = refs[:number], refs[number:]
     out, c_ref, d_ref, stage, turned, sems = refs
+    n, width = out.shape[2], out.shape[3]
     if number == 1:
         fill_whole(pieces[0], c_ref, d_ref, sems, tile)
+        load_all([(terminal.at[0, k], stage.at[:, pl.ds(k * width, width)]) for k in range(2)], sems)
+        starts = (0, width)
     else:
-        assemble_first(place, *pieces, c_ref, d_ref, stage, turned, sems, tile)
+        assemble_first(place, terminal, *pieces, c_ref, d_ref, stage, turned, sems, tile)
+        starts = (place[3], place[3] + 2 * width)
     step = Step(rows, counts, plus.shape[1], plus, minus, jump)
 
     def base(own, _, cols):
-        return terminal[0, 0, own, cols].astype(F32), terminal[0, 1, own, cols].astype(F32)
-
-    own_step(step, place[0], out.shape[3], c_ref, d_ref, turned, tile, base, out)
-
-
-def start_kernel(counts, tile, number, rows, place, terminal, plus, minus, jump, plus_two, minus_two, *refs):
+        part = cols.size
+        return [
+            stage[own, pl.ds(pl.multiple_of(first + cols.start, part), part)].astype(F32) for first in starts
+        ]
+
+    own_step(step, place[0], width, c_ref, d_ref, turned, tile, base, out)
+
+
+def start_kernel(counts, tile, number, rows, place, terminal, jump, plus, minus, plus_two, minus_two, *refs):
     pieces, refs = refs[:number], refs[number:]
     out, c_ref, d_ref, r_ref, x_ref, c_new, d_new, sems = refs
     size = plus.shape[1]
@@ -355,19 +362,18 @@
     is_last = lax.axis_index("tm") == lax.axis_size("tm") - 1
     place = jnp.stack([row * width, is_last.astype(jnp.int32), here, row % 2 * width]).astype(jnp.int32)
     operators = (ham_blocks, ham_cols, jump_blocks, jump_cols)
-    which = ((0, 1), (1, 1), (1, 0))
-    counts, rows, jump_row, plus, minus = operator_tables(which, *operators, controls, controls_next)
+    counts, rows, *first = operator_tables(((0, 1),), *operators, controls, controls)
 
     smem = pl.BlockSpec(memory_space=pltpu.SMEM)
     vmem = pl.BlockSpec(memory_space=pltpu.VMEM)
     anywhere = pl.BlockSpec(memory_space=pl.ANY)
     square = pltpu.VMEM((n, n), BF16)
 
-    def step_call(kernel, name, state_spec, squares, tables, pieces):
+    def step_call(kernel, name, squares, rows, tables, pieces):
         return pl.pallas_call(
             functools.partial(kernel, counts, tile, len(pieces)),
             out_shape=jax.ShapeDtypeStruct(terminal.shape, BF16),
-            in_specs=[smem, smem, state_spec] + [vmem] * len(tables) + [anywhere] * len(pieces),
+            in_specs=[smem, smem, anywhere] + [vmem] * len(tables) + [anywhere] * len(pieces),
             out_specs=vmem,
             scratch_shapes=[square] * squares + [pltpu.SemaphoreType.DMA((8,))],
             compiler_params=pltpu.CompilerParams(vmem_limit_bytes=60 * 2**20),
@@ -375,15 +381,18 @@
             name=name,
         )(rows, place, terminal, *tables, *pieces)
 
-    first = [plus[0], minus[0], jump_row]
-    second = [plus[1], minus[1], jump_row, plus[2], minus[2]]
+
+    def second_tables(controls_next, after):
+        later, _ = lax.optimization_barrier((controls_next, after))
+        return operator_tables(((1, 1), (1, 0)), *operators, controls, later)[1:]
+
     if lax.axis_size("row") == 4:
         near_pair = swapped(terminal, 1)
         size = (1, 1, 2 * width, width)
         mine = [lax.dynamic_slice(terminal, (0, k, here, 0), size)[0, 0].astype(F32) for k in range(2)]
         mixed = (mine[0] + mine[1]).astype(BF16)
+        mixed, controls_next = lax.optimization_barrier((mixed, controls_next))
         far = swapped(mixed, 2)
-        mixed, _ = lax.optimization_barrier((mixed, controls_next))
         mixed = shifted_down(mixed, "tm")
         apart = lax.dynamic_slice(terminal, (0, 0, 2 * width - here, 0), (1, 2, 2 * width, width))[0]
         apart = shifted_down(apart, "tm")
@@ -391,7 +400,7 @@
         far_pair = swapped(far, 1)
         rows, mixed = lax.optimization_barrier((rows, mixed))
         far_next = swapped(mixed, 2)
-        new_fpoint = step_call(inner_kernel, "inner_point", vmem, 4, first, [terminal, near_pair, far, far_pair])
+        new_fpoint = step_call(inner_kernel, "inner_point", 4, rows, first, [near_pair, far, far_pair])
         mixed_pair = swapped(mixed, 1)
         apart, far_next, mixed_pair, new_fpoint = lax.optimization_barrier((apart, far_next, mixed_pair, new_fpoint))
         pieces = [mixed, apart, far_next, mixed_pair, swapped(apart, 1), swapped(far_next, 1)]
@@ -401,9 +410,10 @@
         def gathered(piece):
             return [lax.all_gather(piece, "row", axis=1, tiled=True)]
 
-        new_fpoint = step_call(inner_kernel, "inner_point", vmem, 4, first, gathered(mixed))
+        new_fpoint = step_call(inner_kernel, "inner_point", 4, rows, first, gathered(mixed))
         pieces = gathered(shifted_down(mixed, "tm"))
-    new_cpoint = step_call(start_kernel, "left_end", anywhere, 6, second, pieces)
+    rows, *second = second_tables(controls_next, new_fpoint)
+    new_cpoint = step_call(start_kernel, "left_end", 6, rows, second, pieces)
     return (new_cpoint, new_fpoint)
 
 

time: 162 us -> 163 us (level)
  Pallas kernels: 114 us -> 122 us
  waiting for transfers between devices: 23.7 us -> 19 us
    pallas_call x1 -> x2, Pallas kernels: 11.1 us -> 20.6 us  [operator_tables(): pl.pallas_call(functools.partial(table_kernel, which), out_shape=[jax.Sha...]
    ppermute x7, waiting for transfers between devices: 5.16 us -> 0.26 us  [swapped(): lax.ppermute(block, 'row', [(i, i ^ bit) for i in range(lax.axis_size('ro...]
    unnamed x16 -> x10, local copies, waits for them, and re-layouts: 8.99 us -> 7.36 us
  transfers between devices with their start and end apart: 10 -> 10, of which waited for: 4 -> 4; matrix products, arithmetic and copies ran while one was open for 9% -> 9% of each run, Pallas kernels for 27% -> 32%
where the time goes in v7:
time: 163 us
  Pallas kernels  122 us (75%)
  waiting for transfers between devices  19 us (12%)
  local copies, waits for them, and re-layouts  10.4 us (6%)
  starting transfers between devices  6.9 us (4%)
  other arithmetic  3.44 us (2%)
    pallas_call x2, Pallas kernels, step_call(): pl.pallas_call(functools.partial(kernel, counts, tile, len(pieces)), out_...  102 us
    pallas_call x2, Pallas kernels, operator_tables(): pl.pallas_call(functools.partial(table_kernel, which), out_shape=[jax.Sha...  20.6 us
    ppermute x3, waiting for transfers between devices, shifted_down(): return lax.ppermute(block, axis, route)  18.8 us
    unnamed x10, local copies, waits for them, and re-layouts  7.36 us
    ppermute x3, starting transfers between devices, shifted_down(): return lax.ppermute(block, axis, route)  3.84 us
  transfers between devices with their start and end apart: 10, of which 4 were waited for; matrix products, arithmetic and copies ran while one was open for 9% of the time, Pallas kernels for 32%

profile of v7, /device:TPU:0, one launch (start us, length us, event | category | flops | bytes accessed | tf_op | source)
XLA Modules:
  0.0 162.8 jit_solution(5605944583124098305)
XLA Ops:
  0.6 0.5 collective-permute-start.6
  1.1 1.3 collective-permute-start
  2.5 2.8 %fusion = bf16[1024,512]{1,0:T(8,128)(2,1)} fusion(bf16[1,2,2048,512]{3,2,1,0:T(8,128)(2,1)} %terminal.3, s32[]{:T(128)S(6)} %select_n.19), kind=kLoop, calls=%fused_computation.2 | loop fusion | flops 2097152 | bytes 3145732 | tf_op jit(solution)/shard_map/convert_element_type | solution.py:393
  5.3 0.0 copy-start.1
  5.3 2.0 %collective-permute-done.controls_next = f32[1,2]{1,0:T(1,128)S(1)} collective-permute-done((f32[1,2]{1,0:T(1,128)}, f32[1,2]{1,0:T(1,128)S(1)}, u32[]{:S(2)}, u32[]{:S(2)}) %collective-permute-start) | collective-permute-done | bytes 40 | tf_op jit(solution)/shard_map/ppermute | solution.py:17
  7.3 0.0 copy-start.3
  7.3 1.9 %collective-permute-start.2 = (bf16[1024,512]{1,0:T(8,128)(2,1)}, bf16[1024,512]{1,0:T(8,128)(2,1)}, u32[]{:S(2)}, u32[]{:S(2)}) collective-permute-start(bf16[1024,512]{1,0:T(8,128)(2,1)} %fusion), channel_id=1, source_target_pairs={{0,2},{1,3},{2,0},{3,1},{4,6},{5,7},{6,4},{7,5},{8,10},{9,11},{10,... | collective-permute-start | bytes 3145736 | tf_op jit(solution)/shard_map/ppermute | solution.py:353
  9.2 1.3 collective-permute-start.3
  10.5 3.1 %dynamic-slice_bitcast_fusion = bf16[2,1024,512]{2,1,0:T(8,128)(2,1)} fusion(bf16[1,2,2048,512]{3,2,1,0:T(8,128)(2,1)} %terminal.3, s32[]{:T(128)S(6)} %select_n.20), kind=kLoop, calls=%fused_computation | loop fusion | bytes 4194308 | tf_op jit(solution)/shard_map/squeeze | solution.py:397
  13.6 0.0 copy-done.3
  13.6 1.3 collective-permute-start.1
  14.9 0.0 copy-done.1
  14.9 3.9 %copy.8.ham = bf16[2,64,2,32,32]{4,3,2,1,0:T(8,128)(2,1)} copy(bf16[2,64,2,32,32]{1,4,3,2,0:T(8,128)(2,1)S(1)} %copy-done.1) | data formatting | bytes 1048576 | tf_op args[2]
  18.8 3.5 %copy.9.jump = bf16[64,2,32,32]{3,2,1,0:T(8,128)(2,1)} copy(bf16[64,2,32,32]{0,3,2,1:T(8,128)(2,1)} %param.10) | data formatting | bytes 524288 | tf_op args[4]
  22.2 9.8 %operator_tables.2 = (s32[9,64]{1,0:T(8,128)}, bf16[16,128,256]{2,1,0:T(8,128)(2,1)}, bf16[64,32,224]{2,1,0:T(8,128)(2,1)}, bf16[64,32,224]{2,1,0:T(8,128)(2,1)}) custom-call(s32[2,64]{1,0:T(2,128)} %ham_cols.3, s32[2,64]{1,0:T(2,128)} %jump_cols.3, f32[1,2]{1,0:T(1,128)} %controls.3, f32[1,2]{1,0:T(1,128)} %controls.3, ...), custom_call_target="tpu_custom_call" | custom-call | flops 1 | bytes 1 | tf_op jit(solution)/shard_map/operator_tables/pallas_call | solution.py:83
  32.0 0.2 collective-permute-done.2.refs_1_
  32.3 0.0 collective-permute-start.7
  32.3 5.2 %collective-permute-done.3.refs_0_ = bf16[1024,512]{1,0:T(8,128)(2,1)} collective-permute-done((bf16[1024,512]{1,0:T(8,128)(2,1)}, bf16[1024,512]{1,0:T(8,128)(2,1)}, u32[]{:S(2)}, u32[]{:S(2)}) %collective-permute-start.3) | collective-permute-done | bytes 1048608 | tf_op jit(solution)/shard_map/ppermute | solution.py:17
  37.5 0.0 collective-permute-start.4
  37.6 0.0 collective-permute-start.5
  37.6 0.6 pad_add_fusion.place
  38.2 0.0 collective-permute-done.7.refs_2_
  38.2 0.0 collective-permute-done.6.refs_0_
  38.2 31.0 %inner_point.1 = bf16[1,2,2048,512]{3,2,1,0:T(8,128)(2,1)} custom-call(s32[9,64]{1,0:T(8,128)} %get-tuple-element.28.rows, s32[4]{0:T(128)} %pad_add_fusion.place, bf16[1,2,2048,512]{3,2,1,0:T(8,128)(2,1)} %terminal.3, bf16[16,128,256]{2,1,0:T(8,128)(2,1)} %get-tuple-element.29.jump, bf16[64,32,224]{2,1,0:T(8,128)(2,1)} %get-tuple-element.30.plus, ...), custom_call_target="tpu_custom_call" | custom-call | flops 1 | bytes 1 | tf_op jit(solution)/shard_map/inner_point/pallas_call | solution.py:373
  69.3 11.5 %collective-permute-done.1.refs_1_ = bf16[2,1024,512]{2,1,0:T(8,128)(2,1)S(1)} collective-permute-done((bf16[2,1024,512]{2,1,0:T(8,128)(2,1)}, bf16[2,1024,512]{2,1,0:T(8,128)(2,1)S(1)}, u32[]{:S(2)}, u32[]{:S(2)}) %collective-permute-start.1) | collective-permute-done | bytes 2097184 | tf_op jit(solution)/shard_map/ppermute | solution.py:17
  80.8 0.0 copy-start
  80.8 0.0 collective-permute-done.4.refs_2_
  80.8 0.0 copy-start.2
  80.8 0.0 collective-permute-done.5.refs_3_
  80.8 0.1 collective-permute-start.8
  80.9 0.5 collective-permute-start.9
  81.4 10.9 %operator_tables.3 = (s32[9,64]{1,0:T(8,128)}, bf16[16,128,256]{2,1,0:T(8,128)(2,1)}, bf16[64,32,224]{2,1,0:T(8,128)(2,1)}, bf16[64,32,224]{2,1,0:T(8,128)(2,1)}...) custom-call(s32[2,64]{1,0:T(2,128)} %ham_cols.3, s32[2,64]{1,0:T(2,128)} %jump_cols.3, f32[1,2]{1,0:T(1,128)} %controls.3, ...), custom_call_target="tpu_custom_call" | custom-call | flops 1 | bytes 1 | tf_op jit(solution)/shard_map/operator_tables/pallas_call | solution.py:83
  92.2 0.0 collective-permute-done.9.refs_5_
  92.2 0.0 collective-permute-done.8.refs_4_
  92.3 0.0 copy-done
  92.3 0.0 copy-done.2
  92.3 70.5 %left_end.1 = bf16[1,2,2048,512]{3,2,1,0:T(8,128)(2,1)} custom-call(s32[9,64]{1,0:T(8,128)} %get-tuple-element.35.rows, s32[4]{0:T(128)} %pad_add_fusion.place, bf16[1,2,2048,512]{3,2,1,0:T(8,128)(2,1)} %terminal.3, bf16[16,128,256]{2,1,0:T(8,128)(2,1)} %get-tuple-element.36.jump, bf16[64,32,224]{2,1,0:T(8,128)(2,1)} %get-tuple-element.37.plus, ...), custom_call_target="tpu_custom_call" | custom-call | flops 1 | bytes 1 | tf_op jit(solution)/shard_map/left_end/pallas_call | solution.py:373
Async XLA Ops:
  0.6 37.6 %collective-permute-start.6 = (bf16[1,2,2048,512]{3,2,1,0:T(8,128)(2,1)}, bf16[1,2,2048,512]{3,2,1,0:T(8,128)(2,1)}, u32[]{:S(2)}, u32[]{:S(2)}) collective-permute-start(bf16[1,2,2048,512]{3,2,1,0:T(8,128)(2,1)} %terminal.3), channel_id=1, source_target_pairs={{0,1},{1,0},{2,3},{3,2},{4,5},{5,4},{6,7},{7,6},{8,9},{9,8},{10,11... | collective-permute-start | bytes 12582920 | tf_op jit(solution)/shard_map/ppermute | solution.py:353
  1.1 6.1 %collective-permute-start = (f32[1,2]{1,0:T(1,128)}, f32[1,2]{1,0:T(1,128)S(1)}, u32[]{:S(2)}, u32[]{:S(2)}) collective-permute-start(f32[1,2]{1,0:T(1,128)} %controls.3), channel_id=1, source_target_pairs={{4,0},{8,4},{12,8},{5,1},{9,5},{13,9},{6,2},{10,6},{14,10},{7,3},{... | collective-permute-start | bytes 32 | tf_op jit(solution)/shard_map/ppermute | solution.py:17
  5.3 9.6 %copy-start.1 = (bf16[2,64,2,32,32]{1,4,3,2,0:T(8,128)(2,1)S(1)}, bf16[2,64,2,32,32]{1,4,3,2,0:T(8,128)(2,1)}, u32[]{:S(2)}) copy-start(bf16[2,64,2,32,32]{1,4,3,2,0:T(8,128)(2,1)} %param.8) | copy-start | bytes 1572868
  7.3 6.3 %copy-start.3 = (f32[1,2]{1,0:T(1,128)}, f32[1,2]{1,0:T(1,128)S(1)}, u32[]{:S(2)}) copy-start(f32[1,2]{1,0:T(1,128)S(1)} %collective-permute-done.controls_next) | copy-start | bytes 28
  7.3 25.0 %collective-permute-start.2 = (bf16[1024,512]{1,0:T(8,128)(2,1)}, bf16[1024,512]{1,0:T(8,128)(2,1)}, u32[]{:S(2)}, u32[]{:S(2)}) collective-permute-start(bf16[1024,512]{1,0:T(8,128)(2,1)} %fusion), channel_id=1, source_target_pairs={{0,2},{1,3},{2,0},{3,1},{4,6},{5,7},{6,4},{7,5},{8,10},{9,11},{10,... | collective-permute-start | bytes 3145736 | tf_op jit(solution)/shard_map/ppermute | solution.py:353
  9.2 28.3 %collective-permute-start.3 = (bf16[1024,512]{1,0:T(8,128)(2,1)}, bf16[1024,512]{1,0:T(8,128)(2,1)}, u32[]{:S(2)}, u32[]{:S(2)}) collective-permute-start(bf16[1024,512]{1,0:T(8,128)(2,1)} %fusion), channel_id=1, source_target_pairs={{4,0},{8,4},{12,8},{5,1},{9,5},{13,9},{6,2},{10,6},{14,10},{7,3},{... | collective-permute-start | bytes 3145736 | tf_op jit(solution)/shard_map/ppermute | solution.py:17
  13.6 67.2 %collective-permute-start.1 = (bf16[2,1024,512]{2,1,0:T(8,128)(2,1)}, bf16[2,1024,512]{2,1,0:T(8,128)(2,1)S(1)}, u32[]{:S(2)}, u32[]{:S(2)}) collective-permute-start(bf16[2,1024,512]{2,1,0:T(8,128)(2,1)} %dynamic-slice_bitcast_fusion), channel_id=1, source_target_pairs={{4,0},{8,4},{12,8},{5,1},{9,5},{13,9},{6,2},{10,6},{14,10},{7,3},{... | collective-permute-start | bytes 6291464 | tf_op jit(solution)/shard_map/ppermute | solution.py:17
  32.3 5.9 %collective-permute-start.7 = (bf16[1024,512]{1,0:T(8,128)(2,1)}, bf16[1024,512]{1,0:T(8,128)(2,1)}, u32[]{:S(2)}, u32[]{:S(2)}) collective-permute-start(bf16[1024,512]{1,0:T(8,128)(2,1)} %collective-permute-done.2.refs_1_), channel_id=1, source_target_pairs={{0,1},{1,0},{2,3},{3,2},{4,5},{5,4},{6,7},{7,6},{8,9},{9,8},{10,11... | collective-permute-start | bytes 3145736 | tf_op jit(solution)/shard_map/ppermute | solution.py:353
  37.5 43.3 %collective-permute-start.4 = (bf16[1024,512]{1,0:T(8,128)(2,1)}, bf16[1024,512]{1,0:T(8,128)(2,1)S(1)}, u32[]{:S(2)}, u32[]{:S(2)}) collective-permute-start(bf16[1024,512]{1,0:T(8,128)(2,1)} %collective-permute-done.3.refs_0_), channel_id=1, source_target_pairs={{0,2},{1,3},{2,0},{3,1},{4,6},{5,7},{6,4},{7,5},{8,10},{9,11},{10,... | collective-permute-start | bytes 3145736 | tf_op jit(solution)/shard_map/ppermute | solution.py:353
  37.6 43.2 %collective-permute-start.5 = (bf16[1024,512]{1,0:T(8,128)(2,1)}, bf16[1024,512]{1,0:T(8,128)(2,1)}, u32[]{:S(2)}, u32[]{:S(2)}) collective-permute-start(bf16[1024,512]{1,0:T(8,128)(2,1)} %collective-permute-done.3.refs_0_), channel_id=1, source_target_pairs={{0,1},{1,0},{2,3},{3,2},{4,5},{5,4},{6,7},{7,6},{8,9},{9,8},{10,11... | collective-permute-start | bytes 3145736 | tf_op jit(solution)/shard_map/ppermute | solution.py:353
  80.8 11.5 %copy-start = (bf16[2,1024,512]{2,1,0:T(8,128)(2,1)}, bf16[2,1024,512]{2,1,0:T(8,128)(2,1)S(1)}, u32[]{:S(2)}) copy-start(bf16[2,1024,512]{2,1,0:T(8,128)(2,1)S(1)} %collective-permute-done.1.refs_1_) | copy-start | bytes 6291460
  80.8 11.5 %copy-start.2 = (bf16[1024,512]{1,0:T(8,128)(2,1)}, bf16[1024,512]{1,0:T(8,128)(2,1)S(1)}, u32[]{:S(2)}) copy-start(bf16[1024,512]{1,0:T(8,128)(2,1)S(1)} %collective-permute-done.4.refs_2_) | copy-start | bytes 3145732
  80.8 11.5 %collective-permute-start.8 = (bf16[2,1024,512]{2,1,0:T(8,128)(2,1)S(1)}, bf16[2,1024,512]{2,1,0:T(8,128)(2,1)}, u32[]{:S(2)}, u32[]{:S(2)}) collective-permute-start(bf16[2,1024,512]{2,1,0:T(8,128)(2,1)S(1)} %collective-permute-done.1.refs_1_), channel_id=1, source_target_pairs={{0,1},{1,0},{2,3},{3,2},{4,5},{5,4},{6,7},{7,6},{8,9},{9,8},{10,11... | collective-permute-start | bytes 6291464 | tf_op jit(solution)/shard_map/ppermute | solution.py:353
  80.9 11.4 %collective-permute-start.9 = (bf16[1024,512]{1,0:T(8,128)(2,1)S(1)}, bf16[1024,512]{1,0:T(8,128)(2,1)}, u32[]{:S(2)}, u32[]{:S(2)}) collective-permute-start(bf16[1024,512]{1,0:T(8,128)(2,1)S(1)} %collective-permute-done.4.refs_2_), channel_id=1, source_target_pairs={{0,1},{1,0},{2,3},{3,2},{4,5},{5,4},{6,7},{7,6},{8,9},{9,8},{10,11... | collective-permute-start | bytes 3145736 | tf_op jit(solution)/shard_map/ppermute | solution.py:353

commit v8 on v7

--- a/solution.py
+++ b/solution.py
@@ -189,12 +189,15 @@
     half, width = pieces[0].shape
     here, there = place[2], half - place[2]
     copies = []
-    for (near, apart, far), core in ((pieces[:3], place[3]), (pieces[3:], width - place[3])):
+    for (near, upper, lower, far), core in ((pieces[:4], place[3]), (pieces[4:], width - place[3])):
         low = pl.ds(pl.multiple_of(core, width), width)
         high = pl.ds(pl.multiple_of(half + core, width), width)
         rows = pl.ds(0, half)
         copies += [(near, other.at[rows, low]), (far, other.at[rows, high])]
-        copies += [(apart.at[0], stage.at[rows, low]), (apart.at[1], stage.at[rows, high])]
+        top = upper.shape[1]
+        for k, to in enumerate((low, high)):
+            copies.append((upper.at[k], stage.at[pl.ds(0, top), to]))
+            copies.append((lower.at[k], stage.at[pl.ds(top, half - top), to]))
     load_all(copies, sems)
 
     @pl.loop(0, half // tile)
@@ -362,7 +365,6 @@
     is_last = lax.axis_index("tm") == lax.axis_size("tm") - 1
     place = jnp.stack([row * width, is_last.astype(jnp.int32), here, row % 2 * width]).astype(jnp.int32)
     operators = (ham_blocks, ham_cols, jump_blocks, jump_cols)
-    counts, rows, *first = operator_tables(((0, 1),), *operators, controls, controls)
 
     smem = pl.BlockSpec(memory_space=pltpu.SMEM)
     vmem = pl.BlockSpec(memory_space=pltpu.VMEM)
@@ -375,17 +377,14 @@
             out_shape=jax.ShapeDtypeStruct(terminal.shape, BF16),
             in_specs=[smem, smem, anywhere] + [vmem] * len(tables) + [anywhere] * len(pieces),
             out_specs=vmem,
-            scratch_shapes=[square] * squares + [pltpu.SemaphoreType.DMA((8,))],
+            scratch_shapes=[square] * squares + [pltpu.SemaphoreType.DMA((12,))],
             compiler_params=pltpu.CompilerParams(vmem_limit_bytes=60 * 2**20),
             cost_estimate=pl.CostEstimate(flops=1, bytes_accessed=1, transcendentals=0),
             name=name,
         )(rows, place, terminal, *tables, *pieces)
 
-
-    def second_tables(controls_next, after):
-        later, _ = lax.optimization_barrier((controls_next, after))
-        return operator_tables(((1, 1), (1, 0)), *operators, controls, later)[1:]
-
+    counts, rows, *tables = operator_tables(((0, 1), (1, 1), (1, 0)), *operators, controls, controls_next)
+    first, second = tables[:3], tables[:1] + tables[3:]
     if lax.axis_size("row") == 4:
         near_pair = swapped(terminal, 1)
         size = (1, 1, 2 * width, width)
@@ -394,16 +393,20 @@
         mixed, controls_next = lax.optimization_barrier((mixed, controls_next))
         far = swapped(mixed, 2)
         mixed = shifted_down(mixed, "tm")
-        apart = lax.dynamic_slice(terminal, (0, 0, 2 * width - here, 0), (1, 2, 2 * width, width))[0]
-        apart = shifted_down(apart, "tm")
+        there = 2 * width - here
+        top = 5 * width // 4
+        upper = lax.dynamic_slice(terminal, (0, 0, there, 0), (1, 2, top, width))[0]
+        lower = lax.dynamic_slice(terminal, (0, 0, there + top, 0), (1, 2, 2 * width - top, width))[0]
+        upper, lower = shifted_down(upper, "tm"), shifted_down(lower, "tm")
         far, rows = lax.optimization_barrier((far, rows))
         far_pair = swapped(far, 1)
         rows, mixed = lax.optimization_barrier((rows, mixed))
         far_next = swapped(mixed, 2)
         new_fpoint = step_call(inner_kernel, "inner_point", 4, rows, first, [near_pair, far, far_pair])
         mixed_pair = swapped(mixed, 1)
-        apart, far_next, mixed_pair, new_fpoint = lax.optimization_barrier((apart, far_next, mixed_pair, new_fpoint))
-        pieces = [mixed, apart, far_next, mixed_pair, swapped(apart, 1), swapped(far_next, 1)]
+        upper, far_next, mixed_pair, new_fpoint = lax.optimization_barrier((upper, far_next, mixed_pair, new_fpoint))
+        pieces = [mixed, upper, lower, far_next]
+        pieces += [mixed_pair] + [swapped(piece, 1) for piece in pieces[1:]]
     else:
         mixed = (terminal[0, 0].astype(F32) + terminal[0, 1].astype(F32)).astype(BF16)
 
@@ -412,7 +415,6 @@
 
         new_fpoint = step_call(inner_kernel, "inner_point", 4, rows, first, gathered(mixed))
         pieces = gathered(shifted_down(mixed, "tm"))
-    rows, *second = second_tables(controls_next, new_fpoint)
     new_cpoint = step_call(start_kernel, "left_end", 6, rows, second, pieces)
     return (new_cpoint, new_fpoint)
 

time: 163 us -> 156 us (0.957)
  Pallas kernels: 122 us -> 113 us
  local copies, waits for them, and re-layouts: 10.4 us -> 12.7 us
  starting transfers between devices: 6.9 us -> 8.65 us
    pallas_call x2 -> x1, Pallas kernels: 20.6 us -> 11.2 us  [operator_tables(): pl.pallas_call(functools.partial(table_kernel, which), out_shape=[jax.Sha...]
    ppermute x3 -> x4, waiting for transfers between devices: 18.8 us -> 14.5 us  [shifted_down(): return lax.ppermute(block, axis, route)]
    ppermute x7 -> x8, waiting for transfers between devices: 0.26 us -> 2.96 us  [swapped(): lax.ppermute(block, 'row', [(i, i ^ bit) for i in range(lax.axis_size('ro...]
    unnamed x10 -> x14, local copies, waits for them, and re-layouts: 7.36 us -> 9.28 us
    ppermute x3 -> x4, starting transfers between devices: 3.84 us -> 5.26 us  [shifted_down(): return lax.ppermute(block, axis, route)]
    squeeze x1 -> x2, local copies, waits for them, and re-layouts: 3.08 us -> 3.47 us  [the longest x1 2.06 us: on_device(): lax.dynamic_slice(terminal, (0, 0, there + top, 0), (1, 2, 2 * width - to...]
    ppermute x7 -> x8, starting transfers between devices: 3.06 us -> 3.38 us  [swapped(): lax.ppermute(block, 'row', [(i, i ^ bit) for i in range(lax.axis_size('ro...]
  transfers between devices with their start and end apart: 10 -> 12, of which waited for: 4 -> 5; matrix products, arithmetic and copies ran while one was open for 9% -> 9% of each run, Pallas kernels for 32% -> 27%
where the time goes in v8:
time: 156 us
  Pallas kernels  113 us (72%)
  waiting for transfers between devices  17.4 us (11%)
  local copies, waits for them, and re-layouts  12.7 us (8%)
  starting transfers between devices  8.65 us (6%)
  other arithmetic  3.46 us (2%)
    pallas_call x2, Pallas kernels, step_call(): pl.pallas_call(functools.partial(kernel, counts, tile, len(pieces)), out_...  102 us
    ppermute x4, waiting for transfers between devices, shifted_down(): return lax.ppermute(block, axis, route)  14.5 us
    pallas_call x1, Pallas kernels, operator_tables(): pl.pallas_call(functools.partial(table_kernel, which), out_shape=[jax.Sha...  11.2 us
    unnamed x14, local copies, waits for them, and re-layouts  9.28 us
    ppermute x4, starting transfers between devices, shifted_down(): return lax.ppermute(block, axis, route)  5.26 us
    ppermute x8, starting transfers between devices, swapped(): lax.ppermute(block, 'row', [(i, i ^ bit) for i in range(lax.axis_size('ro...  3.38 us
  transfers between devices with their start and end apart: 12, of which 5 were waited for; matrix products, arithmetic and copies ran while one was open for 9% of the time, Pallas kernels for 27%

profile of v8, /device:TPU:0, one launch (start us, length us, event | category | flops | bytes accessed | tf_op | source)
XLA Modules:
  0.0 155.8 jit_solution(11562744578971118217)
XLA Ops:
  0.6 0.5 collective-permute-start.6
  1.1 1.3 collective-permute-start
  2.5 2.8 %fusion = bf16[1024,512]{1,0:T(8,128)(2,1)} fusion(bf16[1,2,2048,512]{3,2,1,0:T(8,128)(2,1)} %terminal.3, s32[]{:T(128)S(6)} %select_n.22), kind=kLoop, calls=%fused_computation.2 | loop fusion | flops 2097152 | bytes 3145732 | tf_op jit(solution)/shard_map/convert_element_type | solution.py:392
  5.3 2.0 %collective-permute-done.controls_next = f32[1,2]{1,0:T(1,128)S(1)} collective-permute-done((f32[1,2]{1,0:T(1,128)}, f32[1,2]{1,0:T(1,128)S(1)}, u32[]{:S(2)}, u32[]{:S(2)}) %collective-permute-start) | collective-permute-done | bytes 40 | tf_op jit(solution)/shard_map/ppermute | solution.py:17
  7.3 0.0 copy-start.5
  7.3 1.9 %collective-permute-start.1 = (bf16[1024,512]{1,0:T(8,128)(2,1)}, bf16[1024,512]{1,0:T(8,128)(2,1)}, u32[]{:S(2)}, u32[]{:S(2)}) collective-permute-start(bf16[1024,512]{1,0:T(8,128)(2,1)} %fusion), channel_id=1, source_target_pairs={{0,2},{1,3},{2,0},{3,1},{4,6},{5,7},{6,4},{7,5},{8,10},{9,11},{10,... | collective-permute-start | bytes 3145736 | tf_op jit(solution)/shard_map/ppermute | solution.py:356
  9.2 1.3 collective-permute-start.2
  10.5 1.4 dynamic-slice_bitcast_fusion
  11.9 0.0 copy-start.4
  11.9 1.4 collective-permute-start.3
  13.4 4.8 %copy.8.ham = bf16[2,64,2,32,32]{4,3,2,1,0:T(8,128)(2,1)} copy(bf16[2,64,2,32,32]{1,4,3,2,0:T(8,128)(2,1)} %param.8) | data formatting | bytes 1048576 | tf_op args[2]
  18.2 0.0 copy-done.5
  18.2 0.0 copy-done.4
  18.2 2.4 %copy.9.jump = bf16[64,2,32,32]{3,2,1,0:T(8,128)(2,1)} copy(bf16[64,2,32,32]{0,3,2,1:T(8,128)(2,1)S(1)} %copy-done.4) | data formatting | bytes 524288 | tf_op args[4]
  20.6 11.2 %operator_tables.1 = (s32[9,64]{1,0:T(8,128)}, bf16[16,128,256]{2,1,0:T(8,128)(2,1)}, bf16[64,32,224]{2,1,0:T(8,128)(2,1)}, bf16[64,32,224]{2,1,0:T(8,128)(2,1)}...) custom-call(s32[2,64]{1,0:T(2,128)} %ham_cols.1, ...), custom_call_target="tpu_custom_call" | custom-call | flops 1 | bytes 1 | tf_op jit(solution)/shard_map/operator_tables/pallas_call | solution.py:83
  31.8 0.5 collective-permute-done.1.refs_1_
  32.3 0.0 collective-permute-start.7
  32.3 5.2 %collective-permute-done.2.refs_0_ = bf16[1024,512]{1,0:T(8,128)(2,1)} collective-permute-done((bf16[1024,512]{1,0:T(8,128)(2,1)}, bf16[1024,512]{1,0:T(8,128)(2,1)}, u32[]{:S(2)}, u32[]{:S(2)}) %collective-permute-start.2) | collective-permute-done | bytes 1048608 | tf_op jit(solution)/shard_map/ppermute | solution.py:17
  37.5 0.1 collective-permute-start.4
  37.6 0.0 collective-permute-start.5
  37.6 2.1 %dynamic-slice_bitcast_fusion.1 = bf16[2,384,512]{2,1,0:T(8,128)(2,1)} fusion(bf16[1,2,2048,512]{3,2,1,0:T(8,128)(2,1)} %terminal.3, s32[]{:T(128)S(6)} %select_n.25), kind=kLoop, calls=%fused_computation.3 | loop fusion | bytes 1572868 | tf_op jit(solution)/shard_map/squeeze | solution.py:399
  39.7 0.0 collective-permute-done.7.refs_2_
  39.7 1.3 collective-permute-start.8
  41.0 0.7 pad_add_fusion.place
  41.6 0.0 collective-permute-done.6.refs_0_
  41.6 31.1 %inner_point.1 = bf16[1,2,2048,512]{3,2,1,0:T(8,128)(2,1)} custom-call(s32[9,64]{1,0:T(8,128)} %get-tuple-element.22.rows, s32[4]{0:T(128)} %pad_add_fusion.place, bf16[1,2,2048,512]{3,2,1,0:T(8,128)(2,1)} %terminal.3, bf16[16,128,256]{2,1,0:T(8,128)(2,1)} %get-tuple-element.23.jump, bf16[64,32,224]{2,1,0:T(8,128)(2,1)} %get-tuple-element.29.plus, ...), custom_call_target="tpu_custom_call" | custom-call | flops 1 | bytes 1 | tf_op jit(solution)/shard_map/inner_point/pallas_call | solution.py:375
  72.7 0.0 collective-permute-done.3.refs_1_
  72.7 0.0 copy-start
  72.7 0.0 collective-permute-done.4.refs_3_
  72.7 0.0 collective-permute-done.5.refs_4_
  72.8 0.8 collective-permute-start.9
  73.5 0.1 collective-permute-start.11
  73.6 7.2 %collective-permute-done.8.refs_2_ = bf16[2,384,512]{2,1,0:T(8,128)(2,1)} collective-permute-done((bf16[2,384,512]{2,1,0:T(8,128)(2,1)}, bf16[2,384,512]{2,1,0:T(8,128)(2,1)}, u32[]{:S(2)}, u32[]{:S(2)}) %collective-permute-start.8) | collective-permute-done | bytes 786464 | tf_op jit(solution)/shard_map/ppermute | solution.py:17
  80.8 0.0 collective-permute-start.10
  80.8 2.5 %collective-permute-done.10.refs_6_ = bf16[2,384,512]{2,1,0:T(8,128)(2,1)S(1)} collective-permute-done((bf16[2,384,512]{2,1,0:T(8,128)(2,1)}, bf16[2,384,512]{2,1,0:T(8,128)(2,1)S(1)}, u32[]{:S(2)}, u32[]{:S(2)}) %collective-permute-start.10) | collective-permute-done | bytes 786464 | tf_op jit(solution)/shard_map/ppermute | solution.py:356
  83.3 0.0 copy-start.3
  83.3 0.0 collective-permute-done.11.refs_7_
  83.3 0.0 copy-start.2
  83.3 0.0 collective-permute-done.9.refs_5_
  83.3 0.9 copy-done.3
  84.3 0.0 copy-start.1
  84.3 0.0 copy-done
  84.3 0.3 copy-done.2
  84.5 0.8 copy-done.1
  85.3 70.5 %left_end.1 = bf16[1,2,2048,512]{3,2,1,0:T(8,128)(2,1)} custom-call(s32[9,64]{1,0:T(8,128)} %get-tuple-element.22.rows, s32[4]{0:T(128)} %pad_add_fusion.place, bf16[1,2,2048,512]{3,2,1,0:T(8,128)(2,1)} %terminal.3, bf16[16,128,256]{2,1,0:T(8,128)(2,1)} %get-tuple-element.23.jump, bf16[64,32,224]{2,1,0:T(8,128)(2,1)} %get-tuple-element.24.plus, ...), custom_call_target="tpu_custom_call" | custom-call | flops 1 | bytes 1 | tf_op jit(solution)/shard_map/left_end/pallas_call | solution.py:375
Async XLA Ops:
  0.6 41.0 %collective-permute-start.6 = (bf16[1,2,2048,512]{3,2,1,0:T(8,128)(2,1)}, bf16[1,2,2048,512]{3,2,1,0:T(8,128)(2,1)}, u32[]{:S(2)}, u32[]{:S(2)}) collective-permute-start(bf16[1,2,2048,512]{3,2,1,0:T(8,128)(2,1)} %terminal.3), channel_id=1, source_target_pairs={{0,1},{1,0},{2,3},{3,2},{4,5},{5,4},{6,7},{7,6},{8,9},{9,8},{10,11... | collective-permute-start | bytes 12582920 | tf_op jit(solution)/shard_map/ppermute | solution.py:356
  1.1 6.1 %collective-permute-start = (f32[1,2]{1,0:T(1,128)}, f32[1,2]{1,0:T(1,128)S(1)}, u32[]{:S(2)}, u32[]{:S(2)}) collective-permute-start(f32[1,2]{1,0:T(1,128)} %controls.1), channel_id=1, source_target_pairs={{4,0},{8,4},{12,8},{5,1},{9,5},{13,9},{6,2},{10,6},{14,10},{7,3},{... | collective-permute-start | bytes 32 | tf_op jit(solution)/shard_map/ppermute | solution.py:17
  7.3 10.9 %copy-start.5 = (f32[1,2]{1,0:T(1,128)}, f32[1,2]{1,0:T(1,128)S(1)}, u32[]{:S(2)}) copy-start(f32[1,2]{1,0:T(1,128)S(1)} %collective-permute-done.controls_next) | copy-start | bytes 28
  7.3 25.0 %collective-permute-start.1 = (bf16[1024,512]{1,0:T(8,128)(2,1)}, bf16[1024,512]{1,0:T(8,128)(2,1)}, u32[]{:S(2)}, u32[]{:S(2)}) collective-permute-start(bf16[1024,512]{1,0:T(8,128)(2,1)} %fusion), channel_id=1, source_target_pairs={{0,2},{1,3},{2,0},{3,1},{4,6},{5,7},{6,4},{7,5},{8,10},{9,11},{10,... | collective-permute-start | bytes 3145736 | tf_op jit(solution)/shard_map/ppermute | solution.py:356
  9.2 28.3 %collective-permute-start.2 = (bf16[1024,512]{1,0:T(8,128)(2,1)}, bf16[1024,512]{1,0:T(8,128)(2,1)}, u32[]{:S(2)}, u32[]{:S(2)}) collective-permute-start(bf16[1024,512]{1,0:T(8,128)(2,1)} %fusion), channel_id=1, source_target_pairs={{4,0},{8,4},{12,8},{5,1},{9,5},{13,9},{6,2},{10,6},{14,10},{7,3},{... | collective-permute-start | bytes 3145736 | tf_op jit(solution)/shard_map/ppermute | solution.py:17
  11.9 6.3 %copy-start.4 = (bf16[64,2,32,32]{0,3,2,1:T(8,128)(2,1)S(1)}, bf16[64,2,32,32]{0,3,2,1:T(8,128)(2,1)}, u32[]{:S(2)}) copy-start(bf16[64,2,32,32]{0,3,2,1:T(8,128)(2,1)} %param.10) | copy-start | bytes 786436
  11.9 60.8 %collective-permute-start.3 = (bf16[2,640,512]{2,1,0:T(8,128)(2,1)S(1)}, bf16[2,640,512]{2,1,0:T(8,128)(2,1)S(1)}, u32[]{:S(2)}, u32[]{:S(2)}) collective-permute-start(bf16[2,640,512]{2,1,0:T(8,128)(2,1)S(1)} %dynamic-slice_bitcast_fusion), channel_id=1, source_target_pairs={{4,0},{8,4},{12,8},{5,1},{9,5},{13,9},{6,2},{10,6},{14,10},{7,3},{... | collective-permute-start | bytes 3932168 | tf_op jit(solution)/shard_map/ppermute | solution.py:17
  32.3 7.4 %collective-permute-start.7 = (bf16[1024,512]{1,0:T(8,128)(2,1)}, bf16[1024,512]{1,0:T(8,128)(2,1)}, u32[]{:S(2)}, u32[]{:S(2)}) collective-permute-start(bf16[1024,512]{1,0:T(8,128)(2,1)} %collective-permute-done.1.refs_1_), channel_id=1, source_target_pairs={{0,1},{1,0},{2,3},{3,2},{4,5},{5,4},{6,7},{7,6},{8,9},{9,8},{10,11... | collective-permute-start | bytes 3145736 | tf_op jit(solution)/shard_map/ppermute | solution.py:356
  37.5 35.2 %collective-permute-start.4 = (bf16[1024,512]{1,0:T(8,128)(2,1)}, bf16[1024,512]{1,0:T(8,128)(2,1)}, u32[]{:S(2)}, u32[]{:S(2)}) collective-permute-start(bf16[1024,512]{1,0:T(8,128)(2,1)} %collective-permute-done.2.refs_0_), channel_id=1, source_target_pairs={{0,2},{1,3},{2,0},{3,1},{4,6},{5,7},{6,4},{7,5},{8,10},{9,11},{10,... | collective-permute-start | bytes 3145736 | tf_op jit(solution)/shard_map/ppermute | solution.py:356
  37.6 35.2 %collective-permute-start.5 = (bf16[1024,512]{1,0:T(8,128)(2,1)}, bf16[1024,512]{1,0:T(8,128)(2,1)}, u32[]{:S(2)}, u32[]{:S(2)}) collective-permute-start(bf16[1024,512]{1,0:T(8,128)(2,1)} %collective-permute-done.2.refs_0_), channel_id=1, source_target_pairs={{0,1},{1,0},{2,3},{3,2},{4,5},{5,4},{6,7},{7,6},{8,9},{9,8},{10,11... | collective-permute-start | bytes 3145736 | tf_op jit(solution)/shard_map/ppermute | solution.py:356
  39.7 41.2 %collective-permute-start.8 = (bf16[2,384,512]{2,1,0:T(8,128)(2,1)}, bf16[2,384,512]{2,1,0:T(8,128)(2,1)}, u32[]{:S(2)}, u32[]{:S(2)}) collective-permute-start(bf16[2,384,512]{2,1,0:T(8,128)(2,1)} %dynamic-slice_bitcast_fusion.1), channel_id=1, source_target_pairs={{4,0},{8,4},{12,8},{5,1},{9,5},{13,9},{6,2},{10,6},{14,10},{7,3},{... | collective-permute-start | bytes 2359304 | tf_op jit(solution)/shard_map/ppermute | solution.py:17
  72.7 11.6 %copy-start = (bf16[2,640,512]{2,1,0:T(8,128)(2,1)}, bf16[2,640,512]{2,1,0:T(8,128)(2,1)S(1)}, u32[]{:S(2)}) copy-start(bf16[2,640,512]{2,1,0:T(8,128)(2,1)S(1)} %collective-permute-done.3.refs_1_) | copy-start | bytes 3932164
  72.8 10.6 %collective-permute-start.9 = (bf16[2,640,512]{2,1,0:T(8,128)(2,1)S(1)}, bf16[2,640,512]{2,1,0:T(8,128)(2,1)S(1)}, u32[]{:S(2)}, u32[]{:S(2)}) collective-permute-start(bf16[2,640,512]{2,1,0:T(8,128)(2,1)S(1)} %collective-permute-done.3.refs_1_), channel_id=1, source_target_pairs={{0,1},{1,0},{2,3},{3,2},{4,5},{5,4},{6,7},{7,6},{8,9},{9,8},{10,11... | collective-permute-start | bytes 3932168 | tf_op jit(solution)/shard_map/ppermute | solution.py:356
  73.5 9.8 %collective-permute-start.11 = (bf16[1024,512]{1,0:T(8,128)(2,1)}, bf16[1024,512]{1,0:T(8,128)(2,1)S(1)}, u32[]{:S(2)}, u32[]{:S(2)}) collective-permute-start(bf16[1024,512]{1,0:T(8,128)(2,1)} %collective-permute-done.4.refs_3_), channel_id=1, source_target_pairs={{0,1},{1,0},{2,3},{3,2},{4,5},{5,4},{6,7},{7,6},{8,9},{9,8},{10,11... | collective-permute-start | bytes 3145736 | tf_op jit(solution)/shard_map/ppermute | solution.py:356
  80.8 2.5 %collective-permute-start.10 = (bf16[2,384,512]{2,1,0:T(8,128)(2,1)}, bf16[2,384,512]{2,1,0:T(8,128)(2,1)S(1)}, u32[]{:S(2)}, u32[]{:S(2)}) collective-permute-start(bf16[2,384,512]{2,1,0:T(8,128)(2,1)} %collective-permute-done.8.refs_2_), channel_id=1, source_target_pairs={{0,1},{1,0},{2,3},{3,2},{4,5},{5,4},{6,7},{7,6},{8,9},{9,8},{10,11... | collective-permute-start | bytes 2359304 | tf_op jit(solution)/shard_map/ppermute | solution.py:356
  83.3 1.0 copy-start.3
  83.3 1.2 copy-start.2
  84.3 1.1 copy-start.1

commit v9 on v8

--- a/solution.py
+++ b/solution.py
@@ -21,27 +21,30 @@
     return max(256 // (layers_j * size), 1)
 
 
-def table_kernel(which, ham_cols, jump_cols, controls, controls_next, ham, jump, rows, jump_row, *tables):
+def table_kernel(which, ham_cols, jump_cols, controls, controls_next, ham, jump, rows, jump_row, *refs):
     layers_h, count = ham_cols.shape
     layers_j = jump_cols.shape[0]
     size = ham.shape[-1]
     crossed = [(k, other) for k in range(layers_j) for other in range(layers_j) if k != other]
+    *tables, came = refs
     group = jump_row.shape[1] // size
     first_k = 2 * layers_h
     first_j = first_k + 1 + len(crossed)
 
-    @pl.loop(0, count)
+    @pl.loop(0, count, unroll=4)
     def _(b):
         for k in range(layers_h):
             rows[k, b] = ham_cols[k, b] * size
             rows[layers_h + k, ham_cols[k, b]] = b * size
+            came[k, ham_cols[k, b]] = b
         for k in range(layers_j):
             rows[first_j + k, jump_cols[k, b]] = b * size
-
-    @pl.loop(0, count, unroll=8)
-    def _(c):
-        came_h = [rows[layers_h + k, c] // size for k in range(layers_h)]
-        came_j = [rows[first_j + k, c] // size for k in range(layers_j)]
+            came[layers_h + k, jump_cols[k, b]] = b
+
+    def block_row(q, v):
+        c = q * group + v
+        came_h = [came[k, c] for k in range(layers_h)]
+        came_j = [came[layers_h + k, c] for k in range(layers_j)]
         rows[first_k, c] = c * size
         for at, (k, other) in enumerate(crossed):
             rows[first_k + 1 + at, c] = jump_cols[other, came_j[k]] * size
@@ -51,16 +54,12 @@
             parts += [ham[term, came_h[k], k].astype(F32).T for k in range(layers_h)]
             return jnp.concatenate(parts, axis=1)
 
-        turned = [jump[came_j[k], k].astype(F32).T.astype(BF16) for k in range(layers_j)]
-        jump_row[c // group, pl.ds(c % group * size, size), :] = jnp.concatenate(
-            [jnp.where(c % group == v, piece, jnp.zeros_like(piece)) for v in range(group) for piece in turned], axis=1
-        )
-        square = sum(
-            jnp.dot(turned[k], jump[came_j[k], k], preferred_element_type=F32) for k in range(layers_j)
-        )
-        blocks = [square] + [
-            jnp.dot(turned[k], jump[came_j[k], other], preferred_element_type=F32) for k, other in crossed
-        ]
+        stored = [[jump[came_j[k], other] for other in range(layers_j)] for k in range(layers_j)]
+        turned = [stored[k][k].astype(F32).T.astype(BF16) for k in range(layers_j)]
+        empty = [jnp.zeros_like(piece) for piece in turned]
+        jump_row[q, v * size : (v + 1) * size, :] = jnp.concatenate(empty * v + turned + empty * (group - 1 - v), axis=1)
+        square = sum(jnp.dot(turned[k], stored[k][k], preferred_element_type=F32) for k in range(layers_j))
+        blocks = [square] + [jnp.dot(turned[k], stored[k][other], preferred_element_type=F32) for k, other in crossed]
         decay = -0.5 * jnp.concatenate(blocks, axis=1)
         drift, steer = ham_row(0), ham_row(1)
         for at, (later, fine) in enumerate(which):
@@ -68,6 +67,11 @@
             coeffs = drift + amplitude * steer
             tables[2 * at][c] = jnp.concatenate([coeffs, decay], axis=1).astype(BF16)
             tables[2 * at + 1][c] = jnp.concatenate([-coeffs, decay], axis=1).astype(BF16)
+
+    @pl.loop(0, count // group, unroll=2)
+    def _(q):
+        for v in range(group):
+            block_row(q, v)
 
 
 def operator_tables(which, ham_blocks, ham_cols, jump_blocks, jump_cols, controls, controls_next):
@@ -88,6 +92,7 @@
         ] + [table] * (2 * number),
         in_specs=[smem, smem, smem, smem, vmem, vmem],
         out_specs=[smem, vmem] + [vmem] * (2 * number),
+        scratch_shapes=[pltpu.SMEM((layers_h + layers_j, count), jnp.int32)],
         compiler_params=pltpu.CompilerParams(vmem_limit_bytes=60 * 2**20),
         cost_estimate=pl.CostEstimate(flops=1, bytes_accessed=1, transcendentals=0),
         name="operator_tables",
@@ -235,7 +240,7 @@
     def _(g):
         to = part_of(0, g, tile)
 
-        @pl.loop(0, n // tile, unroll=2)
+        @pl.loop(0, n // tile, unroll=4)
         def _(s):
             cols = part_of(0, s, tile)
             put_turned(step, r_ref, cols, to, g * count, count, "ham", step.minus, c_ref, d_ref)
@@ -243,7 +248,7 @@
 
     @pl.loop(0, n // tile)
     def _(g):
-        @pl.loop(0, n // tile, unroll=2)
+        @pl.loop(0, n // tile, unroll=4)
         def _(s):
             cols = part_of(0, s, tile)
             made = []
@@ -274,13 +279,13 @@
 
     @pl.loop(0, width // part)
     def _(g):
-        @pl.loop(0, n // tile)
+        @pl.loop(0, n // tile, unroll=2)
         def _(s):
             for k, kind in enumerate(kinds):
                 to = part_of(k * width, g, part)
                 put_turned(step, turned, part_of(0, s, tile), to, start // deep + g * count, count, *kind)
 
-    @pl.loop(0, n // deep)
+    @pl.loop(0, n // deep, unroll=2)
     def _(q):
         for s in range(width // part):
             cols = pl.ds(pl.multiple_of(start + s * part, part), part)
@@ -387,20 +392,20 @@
     first, second = tables[:3], tables[:1] + tables[3:]
     if lax.axis_size("row") == 4:
         near_pair = swapped(terminal, 1)
-        size = (1, 1, 2 * width, width)
-        mine = [lax.dynamic_slice(terminal, (0, k, here, 0), size)[0, 0].astype(F32) for k in range(2)]
-        mixed = (mine[0] + mine[1]).astype(BF16)
+        halves = terminal.reshape(2, 2, 2 * width, width)
+        chip, top = row // 2, 5 * width // 4
+
+        def cut(first, count, which, low, high):
+            return lax.dynamic_slice(halves, (first, which, low, 0), (count, 1, high - low, width))[:, 0]
+
+        mixed = (cut(0, 1, chip, 0, 2 * width)[0].astype(F32) + cut(1, 1, chip, 0, 2 * width)[0].astype(F32)).astype(BF16)
         mixed, controls_next = lax.optimization_barrier((mixed, controls_next))
-        far = swapped(mixed, 2)
-        mixed = shifted_down(mixed, "tm")
-        there = 2 * width - here
-        top = 5 * width // 4
-        upper = lax.dynamic_slice(terminal, (0, 0, there, 0), (1, 2, top, width))[0]
-        lower = lax.dynamic_slice(terminal, (0, 0, there + top, 0), (1, 2, 2 * width - top, width))[0]
-        upper, lower = shifted_down(upper, "tm"), shifted_down(lower, "tm")
+        upper = shifted_down(cut(0, 2, 1 - chip, 0, top), "tm")
+        lower = shifted_down(cut(0, 2, 1 - chip, top, 2 * width), "tm")
+        near, far = shifted_down(mixed, "tm"), swapped(mixed, 2)
         far, rows = lax.optimization_barrier((far, rows))
         far_pair = swapped(far, 1)
-        rows, mixed = lax.optimization_barrier((rows, mixed))
+        rows, mixed = lax.optimization_barrier((rows, near))
         far_next = swapped(mixed, 2)
         new_fpoint = step_call(inner_kernel, "inner_point", 4, rows, first, [near_pair, far, far_pair])
         mixed_pair = swapped(mixed, 1)

time: 156 us -> 148 us (0.949)
  Pallas kernels: 113 us -> 101 us
  waiting for transfers between devices: 17.4 us -> 20.9 us
    pallas_call x2, Pallas kernels: 102 us -> 90.4 us  [step_call(): pl.pallas_call(functools.partial(kernel, counts, tile, len(pieces)), out_...]
    ppermute x4, waiting for transfers between devices: 14.5 us -> 17.1 us  [shifted_down(): return lax.ppermute(block, axis, route)]
  transfers between devices with their start and end apart: 12 -> 12, of which waited for: 5 -> 5; matrix products, arithmetic and copies ran while one was open for 9% -> 10% of each run, Pallas kernels for 27% -> 26%
where the time goes in v9:
time: 148 us
  Pallas kernels  101 us (68%)
  waiting for transfers between devices  20.9 us (14%)
  local copies, waits for them, and re-layouts  12.7 us (9%)
  starting transfers between devices  8.71 us (6%)
  other arithmetic  3.46 us (2%)
    pallas_call x2, Pallas kernels, step_call(): pl.pallas_call(functools.partial(kernel, counts, tile, len(pieces)), out_...  90.4 us
    ppermute x4, waiting for transfers between devices, shifted_down(): return lax.ppermute(block, axis, route)  17.1 us
    pallas_call x1, Pallas kernels, operator_tables(): pl.pallas_call(functools.partial(table_kernel, which), out_shape=[jax.Sha...  10.3 us
    unnamed x14, local copies, waits for them, and re-layouts  9.28 us
    ppermute x4, starting transfers between devices, shifted_down(): return lax.ppermute(block, axis, route)  5.26 us
    ppermute x8, waiting for transfers between devices, swapped(): lax.ppermute(block, 'row', [(i, i ^ bit) for i in range(lax.axis_size('ro...  3.84 us
    squeeze x2, local copies, waits for them, and re-layouts, cut(): lax.dynamic_slice(halves, (first, which, low, 0), (count, 1, high - low,...  3.47 us
    ppermute x8, starting transfers between devices, swapped(): lax.ppermute(block, 'row', [(i, i ^ bit) for i in range(lax.axis_size('ro...  3.44 us
  transfers between devices with their start and end apart: 12, of which 5 were waited for; matrix products, arithmetic and copies ran while one was open for 10% of the time, Pallas kernels for 26%

profile of v9, /device:TPU:0, one launch (start us, length us, event | category | flops | bytes accessed | tf_op | source)
XLA Modules:
  0.0 147.6 jit_solution(2940676807956207130)
XLA Ops:
  0.6 0.5 collective-permute-start.6
  1.1 1.3 collective-permute-start
  2.5 2.8 %fusion = bf16[1024,512]{1,0:T(8,128)(2,1)} fusion(bf16[2,2,1024,512]{3,2,1,0:T(8,128)(2,1)} %bitcast.11, s32[]{:T(128)S(6)} %select_n.21), kind=kLoop, calls=%fused_computation.2 | loop fusion | flops 2097152 | bytes 3145732 | tf_op jit(solution)/shard_map/convert_element_type | solution.py:401
  5.3 2.0 %collective-permute-done.controls_next = f32[1,2]{1,0:T(1,128)S(1)} collective-permute-done((f32[1,2]{1,0:T(1,128)}, f32[1,2]{1,0:T(1,128)S(1)}, u32[]{:S(2)}, u32[]{:S(2)}) %collective-permute-start) | collective-permute-done | bytes 40 | tf_op jit(solution)/shard_map/ppermute | solution.py:17
  7.3 0.0 copy-start.5
  7.3 1.9 %collective-permute-start.1 = (bf16[1024,512]{1,0:T(8,128)(2,1)}, bf16[1024,512]{1,0:T(8,128)(2,1)}, u32[]{:S(2)}, u32[]{:S(2)}) collective-permute-start(bf16[1024,512]{1,0:T(8,128)(2,1)} %fusion), channel_id=1, source_target_pairs={{0,2},{1,3},{2,0},{3,1},{4,6},{5,7},{6,4},{7,5},{8,10},{9,11},{10,... | collective-permute-start | bytes 3145736 | tf_op jit(solution)/shard_map/ppermute | solution.py:361
  9.2 1.3 collective-permute-start.2
  10.5 1.4 dynamic-slice_bitcast_fusion
  11.9 0.0 copy-start.4
  11.9 1.4 collective-permute-start.3
  13.4 4.8 %copy.8.ham = bf16[2,64,2,32,32]{4,3,2,1,0:T(8,128)(2,1)} copy(bf16[2,64,2,32,32]{1,4,3,2,0:T(8,128)(2,1)} %param.8) | data formatting | bytes 1048576 | tf_op args[2]
  18.2 0.0 copy-done.5
  18.2 0.0 copy-done.4
  18.2 2.4 %copy.9.jump = bf16[64,2,32,32]{3,2,1,0:T(8,128)(2,1)} copy(bf16[64,2,32,32]{0,3,2,1:T(8,128)(2,1)S(1)} %copy-done.4) | data formatting | bytes 524288 | tf_op args[4]
  20.6 10.3 %operator_tables.1 = (s32[9,64]{1,0:T(8,128)}, bf16[16,128,256]{2,1,0:T(8,128)(2,1)}, bf16[64,32,224]{2,1,0:T(8,128)(2,1)}, bf16[64,32,224]{2,1,0:T(8,128)(2,1)}...) custom-call(s32[2,64]{1,0:T(2,128)} %ham_cols.1, ...), custom_call_target="tpu_custom_call" | custom-call | flops 1 | bytes 1 | tf_op jit(solution)/shard_map/operator_tables/pallas_call | solution.py:87
  31.0 1.3 collective-permute-done.1.refs_1_
  32.3 0.0 collective-permute-start.7
  32.3 5.2 %collective-permute-done.2.refs_0_ = bf16[1024,512]{1,0:T(8,128)(2,1)} collective-permute-done((bf16[1024,512]{1,0:T(8,128)(2,1)}, bf16[1024,512]{1,0:T(8,128)(2,1)}, u32[]{:S(2)}, u32[]{:S(2)}) %collective-permute-start.2) | collective-permute-done | bytes 1048608 | tf_op jit(solution)/shard_map/ppermute | solution.py:17
  37.5 0.1 collective-permute-start.4
  37.6 0.0 collective-permute-start.5
  37.6 2.1 %dynamic-slice_bitcast_fusion.1 = bf16[2,384,512]{2,1,0:T(8,128)(2,1)} fusion(bf16[2,2,1024,512]{3,2,1,0:T(8,128)(2,1)} %bitcast.13, s32[]{:T(128)S(6)} %select_n.23), kind=kLoop, calls=%fused_computation.3 | loop fusion | bytes 1572868 | tf_op jit(solution)/shard_map/squeeze | solution.py:399
  39.7 0.0 collective-permute-done.7.refs_2_
  39.7 1.3 collective-permute-start.8
  41.0 0.7 pad_add_fusion.place
  41.6 0.0 collective-permute-done.6.refs_0_
  41.6 28.4 %inner_point.1 = bf16[1,2,2048,512]{3,2,1,0:T(8,128)(2,1)} custom-call(s32[9,64]{1,0:T(8,128)} %get-tuple-element.22.rows, s32[4]{0:T(128)} %pad_add_fusion.place, bf16[1,2,2048,512]{3,2,1,0:T(8,128)(2,1)} %terminal.3, bf16[16,128,256]{2,1,0:T(8,128)(2,1)} %get-tuple-element.23.jump, bf16[64,32,224]{2,1,0:T(8,128)(2,1)} %get-tuple-element.29.plus, ...), custom_call_target="tpu_custom_call" | custom-call | flops 1 | bytes 1 | tf_op jit(solution)/shard_map/inner_point/pallas_call | solution.py:380
  70.0 0.0 collective-permute-done.3.refs_1_
  70.0 0.0 copy-start
  70.0 0.0 collective-permute-done.4.refs_3_
  70.1 0.0 collective-permute-done.5.refs_4_
  70.1 0.8 collective-permute-start.9
  70.9 0.1 collective-permute-start.11
  71.0 9.8 %collective-permute-done.8.refs_2_ = bf16[2,384,512]{2,1,0:T(8,128)(2,1)} collective-permute-done((bf16[2,384,512]{2,1,0:T(8,128)(2,1)}, bf16[2,384,512]{2,1,0:T(8,128)(2,1)}, u32[]{:S(2)}, u32[]{:S(2)}) %collective-permute-start.8) | collective-permute-done | bytes 786464 | tf_op jit(solution)/shard_map/ppermute | solution.py:17
  80.8 0.0 collective-permute-start.10
  80.8 2.5 %collective-permute-done.10.refs_6_ = bf16[2,384,512]{2,1,0:T(8,128)(2,1)S(1)} collective-permute-done((bf16[2,384,512]{2,1,0:T(8,128)(2,1)}, bf16[2,384,512]{2,1,0:T(8,128)(2,1)S(1)}, u32[]{:S(2)}, u32[]{:S(2)}) %collective-permute-start.10) | collective-permute-done | bytes 786464 | tf_op jit(solution)/shard_map/ppermute | solution.py:361
  83.3 0.0 copy-start.3
  83.3 0.0 collective-permute-done.11.refs_7_
  83.3 0.0 copy-start.2
  83.3 0.0 collective-permute-done.9.refs_5_
  83.3 0.9 copy-done.3
  84.3 0.0 copy-start.1
  84.3 0.0 copy-done
  84.3 0.3 copy-done.2
  84.5 0.8 copy-done.1
  85.3 62.0 %left_end.1 = bf16[1,2,2048,512]{3,2,1,0:T(8,128)(2,1)} custom-call(s32[9,64]{1,0:T(8,128)} %get-tuple-element.22.rows, s32[4]{0:T(128)} %pad_add_fusion.place, bf16[1,2,2048,512]{3,2,1,0:T(8,128)(2,1)} %terminal.3, bf16[16,128,256]{2,1,0:T(8,128)(2,1)} %get-tuple-element.23.jump, bf16[64,32,224]{2,1,0:T(8,128)(2,1)} %get-tuple-element.24.plus, ...), custom_call_target="tpu_custom_call" | custom-call | flops 1 | bytes 1 | tf_op jit(solution)/shard_map/left_end/pallas_call | solution.py:380
Async XLA Ops:
  0.6 41.0 %collective-permute-start.6 = (bf16[1,2,2048,512]{3,2,1,0:T(8,128)(2,1)}, bf16[1,2,2048,512]{3,2,1,0:T(8,128)(2,1)}, u32[]{:S(2)}, u32[]{:S(2)}) collective-permute-start(bf16[1,2,2048,512]{3,2,1,0:T(8,128)(2,1)} %terminal.3), channel_id=1, source_target_pairs={{0,1},{1,0},{2,3},{3,2},{4,5},{5,4},{6,7},{7,6},{8,9},{9,8},{10,11... | collective-permute-start | bytes 12582920 | tf_op jit(solution)/shard_map/ppermute | solution.py:361
  1.1 6.1 %collective-permute-start = (f32[1,2]{1,0:T(1,128)}, f32[1,2]{1,0:T(1,128)S(1)}, u32[]{:S(2)}, u32[]{:S(2)}) collective-permute-start(f32[1,2]{1,0:T(1,128)} %controls.1), channel_id=1, source_target_pairs={{4,0},{8,4},{12,8},{5,1},{9,5},{13,9},{6,2},{10,6},{14,10},{7,3},{... | collective-permute-start | bytes 32 | tf_op jit(solution)/shard_map/ppermute | solution.py:17
  7.3 10.9 %copy-start.5 = (f32[1,2]{1,0:T(1,128)}, f32[1,2]{1,0:T(1,128)S(1)}, u32[]{:S(2)}) copy-start(f32[1,2]{1,0:T(1,128)S(1)} %collective-permute-done.controls_next) | copy-start | bytes 28
  7.3 25.0 %collective-permute-start.1 = (bf16[1024,512]{1,0:T(8,128)(2,1)}, bf16[1024,512]{1,0:T(8,128)(2,1)}, u32[]{:S(2)}, u32[]{:S(2)}) collective-permute-start(bf16[1024,512]{1,0:T(8,128)(2,1)} %fusion), channel_id=1, source_target_pairs={{0,2},{1,3},{2,0},{3,1},{4,6},{5,7},{6,4},{7,5},{8,10},{9,11},{10,... | collective-permute-start | bytes 3145736 | tf_op jit(solution)/shard_map/ppermute | solution.py:361
  9.2 28.3 %collective-permute-start.2 = (bf16[1024,512]{1,0:T(8,128)(2,1)}, bf16[1024,512]{1,0:T(8,128)(2,1)}, u32[]{:S(2)}, u32[]{:S(2)}) collective-permute-start(bf16[1024,512]{1,0:T(8,128)(2,1)} %fusion), channel_id=1, source_target_pairs={{4,0},{8,4},{12,8},{5,1},{9,5},{13,9},{6,2},{10,6},{14,10},{7,3},{... | collective-permute-start | bytes 3145736 | tf_op jit(solution)/shard_map/ppermute | solution.py:17
  11.9 6.3 %copy-start.4 = (bf16[64,2,32,32]{0,3,2,1:T(8,128)(2,1)S(1)}, bf16[64,2,32,32]{0,3,2,1:T(8,128)(2,1)}, u32[]{:S(2)}) copy-start(bf16[64,2,32,32]{0,3,2,1:T(8,128)(2,1)} %param.10) | copy-start | bytes 786436
  11.9 58.1 %collective-permute-start.3 = (bf16[2,640,512]{2,1,0:T(8,128)(2,1)S(1)}, bf16[2,640,512]{2,1,0:T(8,128)(2,1)S(1)}, u32[]{:S(2)}, u32[]{:S(2)}) collective-permute-start(bf16[2,640,512]{2,1,0:T(8,128)(2,1)S(1)} %dynamic-slice_bitcast_fusion), channel_id=1, source_target_pairs={{4,0},{8,4},{12,8},{5,1},{9,5},{13,9},{6,2},{10,6},{14,10},{7,3},{... | collective-permute-start | bytes 3932168 | tf_op jit(solution)/shard_map/ppermute | solution.py:17
  32.3 7.4 %collective-permute-start.7 = (bf16[1024,512]{1,0:T(8,128)(2,1)}, bf16[1024,512]{1,0:T(8,128)(2,1)}, u32[]{:S(2)}, u32[]{:S(2)}) collective-permute-start(bf16[1024,512]{1,0:T(8,128)(2,1)} %collective-permute-done.1.refs_1_), channel_id=1, source_target_pairs={{0,1},{1,0},{2,3},{3,2},{4,5},{5,4},{6,7},{7,6},{8,9},{9,8},{10,11... | collective-permute-start | bytes 3145736 | tf_op jit(solution)/shard_map/ppermute | solution.py:361
  37.5 32.5 %collective-permute-start.4 = (bf16[1024,512]{1,0:T(8,128)(2,1)}, bf16[1024,512]{1,0:T(8,128)(2,1)}, u32[]{:S(2)}, u32[]{:S(2)}) collective-permute-start(bf16[1024,512]{1,0:T(8,128)(2,1)} %collective-permute-done.2.refs_0_), channel_id=1, source_target_pairs={{0,2},{1,3},{2,0},{3,1},{4,6},{5,7},{6,4},{7,5},{8,10},{9,11},{10,... | collective-permute-start | bytes 3145736 | tf_op jit(solution)/shard_map/ppermute | solution.py:361
  37.6 32.5 %collective-permute-start.5 = (bf16[1024,512]{1,0:T(8,128)(2,1)}, bf16[1024,512]{1,0:T(8,128)(2,1)}, u32[]{:S(2)}, u32[]{:S(2)}) collective-permute-start(bf16[1024,512]{1,0:T(8,128)(2,1)} %collective-permute-done.2.refs_0_), channel_id=1, source_target_pairs={{0,1},{1,0},{2,3},{3,2},{4,5},{5,4},{6,7},{7,6},{8,9},{9,8},{10,11... | collective-permute-start | bytes 3145736 | tf_op jit(solution)/shard_map/ppermute | solution.py:361
  39.7 41.2 %collective-permute-start.8 = (bf16[2,384,512]{2,1,0:T(8,128)(2,1)}, bf16[2,384,512]{2,1,0:T(8,128)(2,1)}, u32[]{:S(2)}, u32[]{:S(2)}) collective-permute-start(bf16[2,384,512]{2,1,0:T(8,128)(2,1)} %dynamic-slice_bitcast_fusion.1), channel_id=1, source_target_pairs={{4,0},{8,4},{12,8},{5,1},{9,5},{13,9},{6,2},{10,6},{14,10},{7,3},{... | collective-permute-start | bytes 2359304 | tf_op jit(solution)/shard_map/ppermute | solution.py:17
  70.0 14.2 %copy-start = (bf16[2,640,512]{2,1,0:T(8,128)(2,1)}, bf16[2,640,512]{2,1,0:T(8,128)(2,1)S(1)}, u32[]{:S(2)}) copy-start(bf16[2,640,512]{2,1,0:T(8,128)(2,1)S(1)} %collective-permute-done.3.refs_1_) | copy-start | bytes 3932164
  70.1 13.3 %collective-permute-start.9 = (bf16[2,640,512]{2,1,0:T(8,128)(2,1)S(1)}, bf16[2,640,512]{2,1,0:T(8,128)(2,1)S(1)}, u32[]{:S(2)}, u32[]{:S(2)}) collective-permute-start(bf16[2,640,512]{2,1,0:T(8,128)(2,1)S(1)} %collective-permute-done.3.refs_1_), channel_id=1, source_target_pairs={{0,1},{1,0},{2,3},{3,2},{4,5},{5,4},{6,7},{7,6},{8,9},{9,8},{10,11... | collective-permute-start | bytes 3932168 | tf_op jit(solution)/shard_map/ppermute | solution.py:361
  70.9 12.4 %collective-permute-start.11 = (bf16[1024,512]{1,0:T(8,128)(2,1)}, bf16[1024,512]{1,0:T(8,128)(2,1)S(1)}, u32[]{:S(2)}, u32[]{:S(2)}) collective-permute-start(bf16[1024,512]{1,0:T(8,128)(2,1)} %collective-permute-done.4.refs_3_), channel_id=1, source_target_pairs={{0,1},{1,0},{2,3},{3,2},{4,5},{5,4},{6,7},{7,6},{8,9},{9,8},{10,11... | collective-permute-start | bytes 3145736 | tf_op jit(solution)/shard_map/ppermute | solution.py:361
  80.8 2.5 %collective-permute-start.10 = (bf16[2,384,512]{2,1,0:T(8,128)(2,1)}, bf16[2,384,512]{2,1,0:T(8,128)(2,1)S(1)}, u32[]{:S(2)}, u32[]{:S(2)}) collective-permute-start(bf16[2,384,512]{2,1,0:T(8,128)(2,1)} %collective-permute-done.8.refs_2_), channel_id=1, source_target_pairs={{0,1},{1,0},{2,3},{3,2},{4,5},{5,4},{6,7},{7,6},{8,9},{9,8},{10,11... | collective-permute-start | bytes 2359304 | tf_op jit(solution)/shard_map/ppermute | solution.py:361
  83.3 1.0 copy-start.3
  83.3 1.2 copy-start.2
  84.3 1.1 copy-start.1

commit v10 on v9

--- a/solution.py
+++ b/solution.py
@@ -240,7 +240,7 @@
     def _(g):
         to = part_of(0, g, tile)
 
-        @pl.loop(0, n // tile, unroll=4)
+        @pl.loop(0, n // tile, unroll=8)
         def _(s):
             cols = part_of(0, s, tile)
             put_turned(step, r_ref, cols, to, g * count, count, "ham", step.minus, c_ref, d_ref)
@@ -248,7 +248,7 @@
 
     @pl.loop(0, n // tile)
     def _(g):
-        @pl.loop(0, n // tile, unroll=4)
+        @pl.loop(0, n // tile, unroll=8)
         def _(s):
             cols = part_of(0, s, tile)
             made = []
@@ -279,13 +279,13 @@
 
     @pl.loop(0, width // part)
     def _(g):
-        @pl.loop(0, n // tile, unroll=2)
+        @pl.loop(0, n // tile, unroll=4)
         def _(s):
             for k, kind in enumerate(kinds):
                 to = part_of(k * width, g, part)
                 put_turned(step, turned, part_of(0, s, tile), to, start // deep + g * count, count, *kind)
 
-    @pl.loop(0, n // deep, unroll=2)
+    @pl.loop(0, n // deep, unroll=4)
     def _(q):
         for s in range(width // part):
             cols = pl.ds(pl.multiple_of(start + s * part, part), part)
@@ -399,10 +399,11 @@
             return lax.dynamic_slice(halves, (first, which, low, 0), (count, 1, high - low, width))[:, 0]
 
         mixed = (cut(0, 1, chip, 0, 2 * width)[0].astype(F32) + cut(1, 1, chip, 0, 2 * width)[0].astype(F32)).astype(BF16)
-        mixed, controls_next = lax.optimization_barrier((mixed, controls_next))
+        near = shifted_down(mixed, "tm")
+        across, controls_next = lax.optimization_barrier((mixed, controls_next))
+        far = swapped(across, 2)
         upper = shifted_down(cut(0, 2, 1 - chip, 0, top), "tm")
         lower = shifted_down(cut(0, 2, 1 - chip, top, 2 * width), "tm")
-        near, far = shifted_down(mixed, "tm"), swapped(mixed, 2)
         far, rows = lax.optimization_barrier((far, rows))
         far_pair = swapped(far, 1)
         rows, mixed = lax.optimization_barrier((rows, near))

time: 148 us -> 140 us (0.946)
  Pallas kernels: 101 us -> 91.4 us
    pallas_call x2, Pallas kernels: 90.4 us -> 81.1 us  [step_call(): pl.pallas_call(functools.partial(kernel, counts, tile, len(pieces)), out_...]
  transfers between devices with their start and end apart: 12 -> 12, of which waited for: 5 -> 5; matrix products, arithmetic and copies ran while one was open for 10% -> 10% of each run, Pallas kernels for 26% -> 27%
where the time goes in v10:
time: 140 us
  Pallas kernels  91.4 us (65%)
  waiting for transfers between devices  22.3 us (16%)
  local copies, waits for them, and re-layouts  12.7 us (9%)
  starting transfers between devices  8.75 us (6%)
  other arithmetic  3.46 us (2%)
    pallas_call x2, Pallas kernels, step_call(): pl.pallas_call(functools.partial(kernel, counts, tile, len(pieces)), out_...  81.1 us
    ppermute x4, waiting for transfers between devices, shifted_down(): return lax.ppermute(block, axis, route)  18.4 us
    pallas_call x1, Pallas kernels, operator_tables(): pl.pallas_call(functools.partial(table_kernel, which), out_shape=[jax.Sha...  10.3 us
    unnamed x14, local copies, waits for them, and re-layouts  9.28 us
    ppermute x4, starting transfers between devices, shifted_down(): return lax.ppermute(block, axis, route)  5.26 us
    ppermute x8, waiting for transfers between devices, swapped(): lax.ppermute(block, 'row', [(i, i ^ bit) for i in range(lax.axis_size('ro...  3.84 us
    ppermute x8, starting transfers between devices, swapped(): lax.ppermute(block, 'row', [(i, i ^ bit) for i in range(lax.axis_size('ro...  3.48 us
    squeeze x2, local copies, waits for them, and re-layouts, cut(): lax.dynamic_slice(halves, (first, which, low, 0), (count, 1, high - low,...  3.47 us
  transfers between devices with their start and end apart: 12, of which 5 were waited for; matrix products, arithmetic and copies ran while one was open for 10% of the time, Pallas kernels for 27%

profile of v10, /device:TPU:0, one launch (start us, length us, event | category | flops | bytes accessed | tf_op | source)
XLA Modules:
  0.0 139.6 jit_solution(5578675707969832566)
XLA Ops:
  0.6 0.5 collective-permute-start.6
  1.1 1.3 collective-permute-start
  2.5 2.8 %fusion = bf16[1024,512]{1,0:T(8,128)(2,1)} fusion(bf16[2,2,1024,512]{3,2,1,0:T(8,128)(2,1)} %bitcast.11, s32[]{:T(128)S(6)} %select_n.21), kind=kLoop, calls=%fused_computation.2 | loop fusion | flops 2097152 | bytes 3145732 | tf_op jit(solution)/shard_map/convert_element_type | solution.py:401
  5.3 2.0 %collective-permute-done.controls_next = f32[1,2]{1,0:T(1,128)S(1)} collective-permute-done((f32[1,2]{1,0:T(1,128)}, f32[1,2]{1,0:T(1,128)S(1)}, u32[]{:S(2)}, u32[]{:S(2)}) %collective-permute-start) | collective-permute-done | bytes 40 | tf_op jit(solution)/shard_map/ppermute | solution.py:17
  7.3 0.0 copy-start.5
  7.3 1.9 %collective-permute-start.1 = (bf16[1024,512]{1,0:T(8,128)(2,1)}, bf16[1024,512]{1,0:T(8,128)(2,1)}, u32[]{:S(2)}, u32[]{:S(2)}) collective-permute-start(bf16[1024,512]{1,0:T(8,128)(2,1)} %fusion), channel_id=1, source_target_pairs={{0,2},{1,3},{2,0},{3,1},{4,6},{5,7},{6,4},{7,5},{8,10},{9,11},{10,... | collective-permute-start | bytes 3145736 | tf_op jit(solution)/shard_map/ppermute | solution.py:361
  9.2 1.3 collective-permute-start.2
  10.5 1.4 %dynamic-slice_bitcast_fusion = bf16[2,640,512]{2,1,0:T(8,128)(2,1)S(1)} fusion(bf16[2,2,1024,512]{3,2,1,0:T(8,128)(2,1)} %bitcast.12, s32[]{:T(128)S(6)} %select_n.23), kind=kLoop, calls=%fused_computation.1 | loop fusion | bytes 2621444 | tf_op jit(solution)/shard_map/squeeze | solution.py:399
  11.9 0.0 copy-start.4
  11.9 1.4 %collective-permute-start.3 = (bf16[2,640,512]{2,1,0:T(8,128)(2,1)S(1)}, bf16[2,640,512]{2,1,0:T(8,128)(2,1)S(1)}, u32[]{:S(2)}, u32[]{:S(2)}) collective-permute-start(bf16[2,640,512]{2,1,0:T(8,128)(2,1)S(1)} %dynamic-slice_bitcast_fusion), channel_id=1, source_target_pairs={{4,0},{8,4},{12,8},{5,1},{9,5},{13,9},{6,2},{10,6},{14,10},{7,3},{... | collective-permute-start | bytes 3932168 | tf_op jit(solution)/shard_map/ppermute | solution.py:17
  13.4 4.8 %copy.8.ham = bf16[2,64,2,32,32]{4,3,2,1,0:T(8,128)(2,1)} copy(bf16[2,64,2,32,32]{1,4,3,2,0:T(8,128)(2,1)} %param.8) | data formatting | bytes 1048576 | tf_op args[2]
  18.2 0.0 copy-done.5
  18.2 0.0 copy-done.4
  18.2 2.4 %copy.9.jump = bf16[64,2,32,32]{3,2,1,0:T(8,128)(2,1)} copy(bf16[64,2,32,32]{0,3,2,1:T(8,128)(2,1)S(1)} %copy-done.4) | data formatting | bytes 524288 | tf_op args[4]
  20.6 10.3 %operator_tables.1 = (s32[9,64]{1,0:T(8,128)}, bf16[16,128,256]{2,1,0:T(8,128)(2,1)}, bf16[64,32,224]{2,1,0:T(8,128)(2,1)}, bf16[64,32,224]{2,1,0:T(8,128)(2,1)}...) custom-call(s32[2,64]{1,0:T(2,128)} %ham_cols.1, ...), custom_call_target="tpu_custom_call" | custom-call | flops 1 | bytes 1 | tf_op jit(solution)/shard_map/operator_tables/pallas_call | solution.py:87
  31.0 1.3 collective-permute-done.1.refs_1_
  32.3 0.0 collective-permute-start.7
  32.3 5.2 %collective-permute-done.2.refs_0_ = bf16[1024,512]{1,0:T(8,128)(2,1)} collective-permute-done((bf16[1024,512]{1,0:T(8,128)(2,1)}, bf16[1024,512]{1,0:T(8,128)(2,1)}, u32[]{:S(2)}, u32[]{:S(2)}) %collective-permute-start.2) | collective-permute-done | bytes 1048608 | tf_op jit(solution)/shard_map/ppermute | solution.py:17
  37.5 0.1 collective-permute-start.4
  37.6 0.0 collective-permute-start.5
  37.6 2.1 %dynamic-slice_bitcast_fusion.1 = bf16[2,384,512]{2,1,0:T(8,128)(2,1)} fusion(bf16[2,2,1024,512]{3,2,1,0:T(8,128)(2,1)} %bitcast.13, s32[]{:T(128)S(6)} %select_n.23), kind=kLoop, calls=%fused_computation.3 | loop fusion | bytes 1572868 | tf_op jit(solution)/shard_map/squeeze | solution.py:399
  39.7 0.0 collective-permute-done.7.refs_2_
  39.7 1.3 collective-permute-start.8
  41.0 0.7 pad_add_fusion.place
  41.6 0.0 collective-permute-done.6.refs_0_
  41.6 27.0 %inner_point.1 = bf16[1,2,2048,512]{3,2,1,0:T(8,128)(2,1)} custom-call(s32[9,64]{1,0:T(8,128)} %get-tuple-element.22.rows, s32[4]{0:T(128)} %pad_add_fusion.place, bf16[1,2,2048,512]{3,2,1,0:T(8,128)(2,1)} %terminal.3, bf16[16,128,256]{2,1,0:T(8,128)(2,1)} %get-tuple-element.23.jump, bf16[64,32,224]{2,1,0:T(8,128)(2,1)} %get-tuple-element.29.plus, ...), custom_call_target="tpu_custom_call" | custom-call | flops 1 | bytes 1 | tf_op jit(solution)/shard_map/inner_point/pallas_call | solution.py:380
  68.6 0.0 collective-permute-done.3.refs_1_
  68.7 0.0 copy-start
  68.7 0.0 collective-permute-done.4.refs_3_
  68.7 0.0 collective-permute-done.5.refs_4_
  68.7 0.9 collective-permute-start.9
  69.6 0.1 collective-permute-start.11
  69.6 11.2 %collective-permute-done.8.refs_2_ = bf16[2,384,512]{2,1,0:T(8,128)(2,1)} collective-permute-done((bf16[2,384,512]{2,1,0:T(8,128)(2,1)}, bf16[2,384,512]{2,1,0:T(8,128)(2,1)}, u32[]{:S(2)}, u32[]{:S(2)}) %collective-permute-start.8) | collective-permute-done | bytes 786464 | tf_op jit(solution)/shard_map/ppermute | solution.py:17
  80.8 0.0 collective-permute-start.10
  80.8 2.5 %collective-permute-done.10.refs_6_ = bf16[2,384,512]{2,1,0:T(8,128)(2,1)S(1)} collective-permute-done((bf16[2,384,512]{2,1,0:T(8,128)(2,1)}, bf16[2,384,512]{2,1,0:T(8,128)(2,1)S(1)}, u32[]{:S(2)}, u32[]{:S(2)}) %collective-permute-start.10) | collective-permute-done | bytes 786464 | tf_op jit(solution)/shard_map/ppermute | solution.py:361
  83.3 0.0 copy-start.3
  83.3 0.0 collective-permute-done.11.refs_7_
  83.3 0.0 copy-start.2
  83.3 0.0 collective-permute-done.9.refs_5_
  83.3 0.9 copy-done.3
  84.3 0.0 copy-start.1
  84.3 0.0 copy-done
  84.3 0.3 copy-done.2
  84.5 0.8 copy-done.1
  85.3 54.1 %left_end.1 = bf16[1,2,2048,512]{3,2,1,0:T(8,128)(2,1)} custom-call(s32[9,64]{1,0:T(8,128)} %get-tuple-element.22.rows, s32[4]{0:T(128)} %pad_add_fusion.place, bf16[1,2,2048,512]{3,2,1,0:T(8,128)(2,1)} %terminal.3, bf16[16,128,256]{2,1,0:T(8,128)(2,1)} %get-tuple-element.23.jump, bf16[64,32,224]{2,1,0:T(8,128)(2,1)} %get-tuple-element.24.plus, ...), custom_call_target="tpu_custom_call" | custom-call | flops 1 | bytes 1 | tf_op jit(solution)/shard_map/left_end/pallas_call | solution.py:380
Async XLA Ops:
  0.6 41.0 %collective-permute-start.6 = (bf16[1,2,2048,512]{3,2,1,0:T(8,128)(2,1)}, bf16[1,2,2048,512]{3,2,1,0:T(8,128)(2,1)}, u32[]{:S(2)}, u32[]{:S(2)}) collective-permute-start(bf16[1,2,2048,512]{3,2,1,0:T(8,128)(2,1)} %terminal.3), channel_id=1, source_target_pairs={{0,1},{1,0},{2,3},{3,2},{4,5},{5,4},{6,7},{7,6},{8,9},{9,8},{10,11... | collective-permute-start | bytes 12582920 | tf_op jit(solution)/shard_map/ppermute | solution.py:361
  1.1 6.1 %collective-permute-start = (f32[1,2]{1,0:T(1,128)}, f32[1,2]{1,0:T(1,128)S(1)}, u32[]{:S(2)}, u32[]{:S(2)}) collective-permute-start(f32[1,2]{1,0:T(1,128)} %controls.1), channel_id=1, source_target_pairs={{4,0},{8,4},{12,8},{5,1},{9,5},{13,9},{6,2},{10,6},{14,10},{7,3},{... | collective-permute-start | bytes 32 | tf_op jit(solution)/shard_map/ppermute | solution.py:17
  7.3 10.9 %copy-start.5 = (f32[1,2]{1,0:T(1,128)}, f32[1,2]{1,0:T(1,128)S(1)}, u32[]{:S(2)}) copy-start(f32[1,2]{1,0:T(1,128)S(1)} %collective-permute-done.controls_next) | copy-start | bytes 28
  7.3 25.0 %collective-permute-start.1 = (bf16[1024,512]{1,0:T(8,128)(2,1)}, bf16[1024,512]{1,0:T(8,128)(2,1)}, u32[]{:S(2)}, u32[]{:S(2)}) collective-permute-start(bf16[1024,512]{1,0:T(8,128)(2,1)} %fusion), channel_id=1, source_target_pairs={{0,2},{1,3},{2,0},{3,1},{4,6},{5,7},{6,4},{7,5},{8,10},{9,11},{10,... | collective-permute-start | bytes 3145736 | tf_op jit(solution)/shard_map/ppermute | solution.py:361
  9.2 28.3 %collective-permute-start.2 = (bf16[1024,512]{1,0:T(8,128)(2,1)}, bf16[1024,512]{1,0:T(8,128)(2,1)}, u32[]{:S(2)}, u32[]{:S(2)}) collective-permute-start(bf16[1024,512]{1,0:T(8,128)(2,1)} %fusion), channel_id=1, source_target_pairs={{4,0},{8,4},{12,8},{5,1},{9,5},{13,9},{6,2},{10,6},{14,10},{7,3},{... | collective-permute-start | bytes 3145736 | tf_op jit(solution)/shard_map/ppermute | solution.py:17
  11.9 6.3 %copy-start.4 = (bf16[64,2,32,32]{0,3,2,1:T(8,128)(2,1)S(1)}, bf16[64,2,32,32]{0,3,2,1:T(8,128)(2,1)}, u32[]{:S(2)}) copy-start(bf16[64,2,32,32]{0,3,2,1:T(8,128)(2,1)} %param.10) | copy-start | bytes 786436
  11.9 56.7 %collective-permute-start.3 = (bf16[2,640,512]{2,1,0:T(8,128)(2,1)S(1)}, bf16[2,640,512]{2,1,0:T(8,128)(2,1)S(1)}, u32[]{:S(2)}, u32[]{:S(2)}) collective-permute-start(bf16[2,640,512]{2,1,0:T(8,128)(2,1)S(1)} %dynamic-slice_bitcast_fusion), channel_id=1, source_target_pairs={{4,0},{8,4},{12,8},{5,1},{9,5},{13,9},{6,2},{10,6},{14,10},{7,3},{... | collective-permute-start | bytes 3932168 | tf_op jit(solution)/shard_map/ppermute | solution.py:17
  32.3 7.4 %collective-permute-start.7 = (bf16[1024,512]{1,0:T(8,128)(2,1)}, bf16[1024,512]{1,0:T(8,128)(2,1)}, u32[]{:S(2)}, u32[]{:S(2)}) collective-permute-start(bf16[1024,512]{1,0:T(8,128)(2,1)} %collective-permute-done.1.refs_1_), channel_id=1, source_target_pairs={{0,1},{1,0},{2,3},{3,2},{4,5},{5,4},{6,7},{7,6},{8,9},{9,8},{10,11... | collective-permute-start | bytes 3145736 | tf_op jit(solution)/shard_map/ppermute | solution.py:361
  37.5 31.1 %collective-permute-start.4 = (bf16[1024,512]{1,0:T(8,128)(2,1)}, bf16[1024,512]{1,0:T(8,128)(2,1)}, u32[]{:S(2)}, u32[]{:S(2)}) collective-permute-start(bf16[1024,512]{1,0:T(8,128)(2,1)} %collective-permute-done.2.refs_0_), channel_id=1, source_target_pairs={{0,2},{1,3},{2,0},{3,1},{4,6},{5,7},{6,4},{7,5},{8,10},{9,11},{10,... | collective-permute-start | bytes 3145736 | tf_op jit(solution)/shard_map/ppermute | solution.py:361
  37.6 31.1 %collective-permute-start.5 = (bf16[1024,512]{1,0:T(8,128)(2,1)}, bf16[1024,512]{1,0:T(8,128)(2,1)}, u32[]{:S(2)}, u32[]{:S(2)}) collective-permute-start(bf16[1024,512]{1,0:T(8,128)(2,1)} %collective-permute-done.2.refs_0_), channel_id=1, source_target_pairs={{0,1},{1,0},{2,3},{3,2},{4,5},{5,4},{6,7},{7,6},{8,9},{9,8},{10,11... | collective-permute-start | bytes 3145736 | tf_op jit(solution)/shard_map/ppermute | solution.py:361
  39.7 41.2 %collective-permute-start.8 = (bf16[2,384,512]{2,1,0:T(8,128)(2,1)}, bf16[2,384,512]{2,1,0:T(8,128)(2,1)}, u32[]{:S(2)}, u32[]{:S(2)}) collective-permute-start(bf16[2,384,512]{2,1,0:T(8,128)(2,1)} %dynamic-slice_bitcast_fusion.1), channel_id=1, source_target_pairs={{4,0},{8,4},{12,8},{5,1},{9,5},{13,9},{6,2},{10,6},{14,10},{7,3},{... | collective-permute-start | bytes 2359304 | tf_op jit(solution)/shard_map/ppermute | solution.py:17
  68.7 15.6 %copy-start = (bf16[2,640,512]{2,1,0:T(8,128)(2,1)}, bf16[2,640,512]{2,1,0:T(8,128)(2,1)S(1)}, u32[]{:S(2)}) copy-start(bf16[2,640,512]{2,1,0:T(8,128)(2,1)S(1)} %collective-permute-done.3.refs_1_) | copy-start | bytes 3932164
  68.7 14.6 %collective-permute-start.9 = (bf16[2,640,512]{2,1,0:T(8,128)(2,1)S(1)}, bf16[2,640,512]{2,1,0:T(8,128)(2,1)S(1)}, u32[]{:S(2)}, u32[]{:S(2)}) collective-permute-start(bf16[2,640,512]{2,1,0:T(8,128)(2,1)S(1)} %collective-permute-done.3.refs_1_), channel_id=1, source_target_pairs={{0,1},{1,0},{2,3},{3,2},{4,5},{5,4},{6,7},{7,6},{8,9},{9,8},{10,11... | collective-permute-start | bytes 3932168 | tf_op jit(solution)/shard_map/ppermute | solution.py:361
  69.6 13.8 %collective-permute-start.11 = (bf16[1024,512]{1,0:T(8,128)(2,1)}, bf16[1024,512]{1,0:T(8,128)(2,1)S(1)}, u32[]{:S(2)}, u32[]{:S(2)}) collective-permute-start(bf16[1024,512]{1,0:T(8,128)(2,1)} %collective-permute-done.4.refs_3_), channel_id=1, source_target_pairs={{0,1},{1,0},{2,3},{3,2},{4,5},{5,4},{6,7},{7,6},{8,9},{9,8},{10,11... | collective-permute-start | bytes 3145736 | tf_op jit(solution)/shard_map/ppermute | solution.py:361
  80.8 2.5 %collective-permute-start.10 = (bf16[2,384,512]{2,1,0:T(8,128)(2,1)}, bf16[2,384,512]{2,1,0:T(8,128)(2,1)S(1)}, u32[]{:S(2)}, u32[]{:S(2)}) collective-permute-start(bf16[2,384,512]{2,1,0:T(8,128)(2,1)} %collective-permute-done.8.refs_2_), channel_id=1, source_target_pairs={{0,1},{1,0},{2,3},{3,2},{4,5},{5,4},{6,7},{7,6},{8,9},{9,8},{10,11... | collective-permute-start | bytes 2359304 | tf_op jit(solution)/shard_map/ppermute | solution.py:361
  83.3 1.0 copy-start.3
  83.3 1.2 copy-start.2
  84.3 1.1 copy-start.1

commit v11 on v10

--- a/solution.py
+++ b/solution.py
@@ -279,13 +279,13 @@
 
     @pl.loop(0, width // part)
     def _(g):
-        @pl.loop(0, n // tile, unroll=4)
+        @pl.loop(0, n // tile, unroll=8)
         def _(s):
             for k, kind in enumerate(kinds):
                 to = part_of(k * width, g, part)
                 put_turned(step, turned, part_of(0, s, tile), to, start // deep + g * count, count, *kind)
 
-    @pl.loop(0, n // deep, unroll=4)
+    @pl.loop(0, n // deep, unroll=8)
     def _(q):
         for s in range(width // part):
             cols = pl.ds(pl.multiple_of(start + s * part, part), part)

time: 140 us -> 139 us (level)
  Pallas kernels: 91.4 us -> 89.6 us
    pallas_call x2, Pallas kernels: 81.1 us -> 79.3 us  [step_call(): pl.pallas_call(functools.partial(kernel, counts, tile, len(pieces)), out_...]
  transfers between devices with their start and end apart: 12 -> 12, of which waited for: 5 -> 5; matrix products, arithmetic and copies ran while one was open for 10% -> 10% of each run, Pallas kernels for 27% -> 26%
where the time goes in v11:
time: 139 us
  Pallas kernels  89.6 us (64%)
  waiting for transfers between devices  23.2 us (17%)
  local copies, waits for them, and re-layouts  12.7 us (9%)
  starting transfers between devices  8.75 us (6%)
  other arithmetic  3.46 us (2%)
    pallas_call x2, Pallas kernels, step_call(): pl.pallas_call(functools.partial(kernel, counts, tile, len(pieces)), out_...  79.3 us
    ppermute x4, waiting for transfers between devices, shifted_down(): return lax.ppermute(block, axis, route)  19.3 us
    pallas_call x1, Pallas kernels, operator_tables(): pl.pallas_call(functools.partial(table_kernel, which), out_shape=[jax.Sha...  10.3 us
    unnamed x14, local copies, waits for them, and re-layouts  9.28 us
    ppermute x4, starting transfers between devices, shifted_down(): return lax.ppermute(block, axis, route)  5.26 us
    ppermute x8, waiting for transfers between devices, swapped(): lax.ppermute(block, 'row', [(i, i ^ bit) for i in range(lax.axis_size('ro...  3.84 us
    ppermute x8, starting transfers between devices, swapped(): lax.ppermute(block, 'row', [(i, i ^ bit) for i in range(lax.axis_size('ro...  3.49 us
    squeeze x2, local copies, waits for them, and re-layouts, cut(): lax.dynamic_slice(halves, (first, which, low, 0), (count, 1, high - low,...  3.47 us
  transfers between devices with their start and end apart: 12, of which 5 were waited for; matrix products, arithmetic and copies ran while one was open for 10% of the time, Pallas kernels for 26%

profile of v11, /device:TPU:0, one launch (start us, length us, event | category | flops | bytes accessed | tf_op | source)
XLA Modules:
  0.0 138.7 jit_solution(6704564699043823580)
XLA Ops:
  0.6 0.5 collective-permute-start.6
  1.1 1.3 collective-permute-start
  2.5 2.8 %fusion = bf16[1024,512]{1,0:T(8,128)(2,1)} fusion(bf16[2,2,1024,512]{3,2,1,0:T(8,128)(2,1)} %bitcast.11, s32[]{:T(128)S(6)} %select_n.21), kind=kLoop, calls=%fused_computation.2 | loop fusion | flops 2097152 | bytes 3145732 | tf_op jit(solution)/shard_map/convert_element_type | solution.py:401
  5.3 2.0 %collective-permute-done.controls_next = f32[1,2]{1,0:T(1,128)S(1)} collective-permute-done((f32[1,2]{1,0:T(1,128)}, f32[1,2]{1,0:T(1,128)S(1)}, u32[]{:S(2)}, u32[]{:S(2)}) %collective-permute-start) | collective-permute-done | bytes 40 | tf_op jit(solution)/shard_map/ppermute | solution.py:17
  7.3 0.0 copy-start.5
  7.3 1.9 %collective-permute-start.1 = (bf16[1024,512]{1,0:T(8,128)(2,1)}, bf16[1024,512]{1,0:T(8,128)(2,1)}, u32[]{:S(2)}, u32[]{:S(2)}) collective-permute-start(bf16[1024,512]{1,0:T(8,128)(2,1)} %fusion), channel_id=1, source_target_pairs={{0,2},{1,3},{2,0},{3,1},{4,6},{5,7},{6,4},{7,5},{8,10},{9,11},{10,... | collective-permute-start | bytes 3145736 | tf_op jit(solution)/shard_map/ppermute | solution.py:361
  9.2 1.3 collective-permute-start.2
  10.5 1.4 %dynamic-slice_bitcast_fusion = bf16[2,640,512]{2,1,0:T(8,128)(2,1)S(1)} fusion(bf16[2,2,1024,512]{3,2,1,0:T(8,128)(2,1)} %bitcast.12, s32[]{:T(128)S(6)} %select_n.23), kind=kLoop, calls=%fused_computation.1 | loop fusion | bytes 2621444 | tf_op jit(solution)/shard_map/squeeze | solution.py:399
  11.9 0.0 copy-start.4
  11.9 1.4 %collective-permute-start.3 = (bf16[2,640,512]{2,1,0:T(8,128)(2,1)S(1)}, bf16[2,640,512]{2,1,0:T(8,128)(2,1)S(1)}, u32[]{:S(2)}, u32[]{:S(2)}) collective-permute-start(bf16[2,640,512]{2,1,0:T(8,128)(2,1)S(1)} %dynamic-slice_bitcast_fusion), channel_id=1, source_target_pairs={{4,0},{8,4},{12,8},{5,1},{9,5},{13,9},{6,2},{10,6},{14,10},{7,3},{... | collective-permute-start | bytes 3932168 | tf_op jit(solution)/shard_map/ppermute | solution.py:17
  13.4 4.8 %copy.8.ham = bf16[2,64,2,32,32]{4,3,2,1,0:T(8,128)(2,1)} copy(bf16[2,64,2,32,32]{1,4,3,2,0:T(8,128)(2,1)} %param.8) | data formatting | bytes 1048576 | tf_op args[2]
  18.2 0.0 copy-done.5
  18.2 0.0 copy-done.4
  18.2 2.4 %copy.9.jump = bf16[64,2,32,32]{3,2,1,0:T(8,128)(2,1)} copy(bf16[64,2,32,32]{0,3,2,1:T(8,128)(2,1)S(1)} %copy-done.4) | data formatting | bytes 524288 | tf_op args[4]
  20.6 10.3 %operator_tables.1 = (s32[9,64]{1,0:T(8,128)}, bf16[16,128,256]{2,1,0:T(8,128)(2,1)}, bf16[64,32,224]{2,1,0:T(8,128)(2,1)}, bf16[64,32,224]{2,1,0:T(8,128)(2,1)}...) custom-call(s32[2,64]{1,0:T(2,128)} %ham_cols.1, ...), custom_call_target="tpu_custom_call" | custom-call | flops 1 | bytes 1 | tf_op jit(solution)/shard_map/operator_tables/pallas_call | solution.py:87
  31.0 1.3 collective-permute-done.1.refs_1_
  32.3 0.0 collective-permute-start.7
  32.3 5.2 %collective-permute-done.2.refs_0_ = bf16[1024,512]{1,0:T(8,128)(2,1)} collective-permute-done((bf16[1024,512]{1,0:T(8,128)(2,1)}, bf16[1024,512]{1,0:T(8,128)(2,1)}, u32[]{:S(2)}, u32[]{:S(2)}) %collective-permute-start.2) | collective-permute-done | bytes 1048608 | tf_op jit(solution)/shard_map/ppermute | solution.py:17
  37.5 0.1 collective-permute-start.4
  37.6 0.0 collective-permute-start.5
  37.6 2.1 %dynamic-slice_bitcast_fusion.1 = bf16[2,384,512]{2,1,0:T(8,128)(2,1)} fusion(bf16[2,2,1024,512]{3,2,1,0:T(8,128)(2,1)} %bitcast.13, s32[]{:T(128)S(6)} %select_n.23), kind=kLoop, calls=%fused_computation.3 | loop fusion | bytes 1572868 | tf_op jit(solution)/shard_map/squeeze | solution.py:399
  39.7 0.0 collective-permute-done.7.refs_2_
  39.7 1.3 collective-permute-start.8
  41.0 0.7 pad_add_fusion.place
  41.6 0.0 collective-permute-done.6.refs_0_
  41.6 26.1 %inner_point.1 = bf16[1,2,2048,512]{3,2,1,0:T(8,128)(2,1)} custom-call(s32[9,64]{1,0:T(8,128)} %get-tuple-element.22.rows, s32[4]{0:T(128)} %pad_add_fusion.place, bf16[1,2,2048,512]{3,2,1,0:T(8,128)(2,1)} %terminal.3, bf16[16,128,256]{2,1,0:T(8,128)(2,1)} %get-tuple-element.23.jump, bf16[64,32,224]{2,1,0:T(8,128)(2,1)} %get-tuple-element.29.plus, ...), custom_call_target="tpu_custom_call" | custom-call | flops 1 | bytes 1 | tf_op jit(solution)/shard_map/inner_point/pallas_call | solution.py:380
  67.7 0.0 collective-permute-done.3.refs_1_
  67.7 0.0 copy-start
  67.7 0.0 collective-permute-done.4.refs_3_
  67.8 0.0 collective-permute-done.5.refs_4_
  67.8 0.9 collective-permute-start.9
  68.7 0.1 collective-permute-start.11
  68.7 12.1 %collective-permute-done.8.refs_2_ = bf16[2,384,512]{2,1,0:T(8,128)(2,1)} collective-permute-done((bf16[2,384,512]{2,1,0:T(8,128)(2,1)}, bf16[2,384,512]{2,1,0:T(8,128)(2,1)}, u32[]{:S(2)}, u32[]{:S(2)}) %collective-permute-start.8) | collective-permute-done | bytes 786464 | tf_op jit(solution)/shard_map/ppermute | solution.py:17
  80.8 0.0 collective-permute-start.10
  80.8 2.5 %collective-permute-done.10.refs_6_ = bf16[2,384,512]{2,1,0:T(8,128)(2,1)S(1)} collective-permute-done((bf16[2,384,512]{2,1,0:T(8,128)(2,1)}, bf16[2,384,512]{2,1,0:T(8,128)(2,1)S(1)}, u32[]{:S(2)}, u32[]{:S(2)}) %collective-permute-start.10) | collective-permute-done | bytes 786464 | tf_op jit(solution)/shard_map/ppermute | solution.py:361
  83.3 0.0 copy-start.3
  83.3 0.0 collective-permute-done.11.refs_7_
  83.3 0.0 copy-start.2
  83.3 0.0 collective-permute-done.9.refs_5_
  83.3 0.9 copy-done.3
  84.3 0.0 copy-start.1
  84.3 0.0 copy-done
  84.3 0.3 copy-done.2
  84.5 0.8 copy-done.1
  85.3 53.2 %left_end.1 = bf16[1,2,2048,512]{3,2,1,0:T(8,128)(2,1)} custom-call(s32[9,64]{1,0:T(8,128)} %get-tuple-element.22.rows, s32[4]{0:T(128)} %pad_add_fusion.place, bf16[1,2,2048,512]{3,2,1,0:T(8,128)(2,1)} %terminal.3, bf16[16,128,256]{2,1,0:T(8,128)(2,1)} %get-tuple-element.23.jump, bf16[64,32,224]{2,1,0:T(8,128)(2,1)} %get-tuple-element.24.plus, ...), custom_call_target="tpu_custom_call" | custom-call | flops 1 | bytes 1 | tf_op jit(solution)/shard_map/left_end/pallas_call | solution.py:380
Async XLA Ops:
  0.6 41.0 %collective-permute-start.6 = (bf16[1,2,2048,512]{3,2,1,0:T(8,128)(2,1)}, bf16[1,2,2048,512]{3,2,1,0:T(8,128)(2,1)}, u32[]{:S(2)}, u32[]{:S(2)}) collective-permute-start(bf16[1,2,2048,512]{3,2,1,0:T(8,128)(2,1)} %terminal.3), channel_id=1, source_target_pairs={{0,1},{1,0},{2,3},{3,2},{4,5},{5,4},{6,7},{7,6},{8,9},{9,8},{10,11... | collective-permute-start | bytes 12582920 | tf_op jit(solution)/shard_map/ppermute | solution.py:361
  1.1 6.1 %collective-permute-start = (f32[1,2]{1,0:T(1,128)}, f32[1,2]{1,0:T(1,128)S(1)}, u32[]{:S(2)}, u32[]{:S(2)}) collective-permute-start(f32[1,2]{1,0:T(1,128)} %controls.1), channel_id=1, source_target_pairs={{4,0},{8,4},{12,8},{5,1},{9,5},{13,9},{6,2},{10,6},{14,10},{7,3},{... | collective-permute-start | bytes 32 | tf_op jit(solution)/shard_map/ppermute | solution.py:17
  7.3 10.9 %copy-start.5 = (f32[1,2]{1,0:T(1,128)}, f32[1,2]{1,0:T(1,128)S(1)}, u32[]{:S(2)}) copy-start(f32[1,2]{1,0:T(1,128)S(1)} %collective-permute-done.controls_next) | copy-start | bytes 28
  7.3 25.0 %collective-permute-start.1 = (bf16[1024,512]{1,0:T(8,128)(2,1)}, bf16[1024,512]{1,0:T(8,128)(2,1)}, u32[]{:S(2)}, u32[]{:S(2)}) collective-permute-start(bf16[1024,512]{1,0:T(8,128)(2,1)} %fusion), channel_id=1, source_target_pairs={{0,2},{1,3},{2,0},{3,1},{4,6},{5,7},{6,4},{7,5},{8,10},{9,11},{10,... | collective-permute-start | bytes 3145736 | tf_op jit(solution)/shard_map/ppermute | solution.py:361
  9.2 28.3 %collective-permute-start.2 = (bf16[1024,512]{1,0:T(8,128)(2,1)}, bf16[1024,512]{1,0:T(8,128)(2,1)}, u32[]{:S(2)}, u32[]{:S(2)}) collective-permute-start(bf16[1024,512]{1,0:T(8,128)(2,1)} %fusion), channel_id=1, source_target_pairs={{4,0},{8,4},{12,8},{5,1},{9,5},{13,9},{6,2},{10,6},{14,10},{7,3},{... | collective-permute-start | bytes 3145736 | tf_op jit(solution)/shard_map/ppermute | solution.py:17
  11.9 6.3 %copy-start.4 = (bf16[64,2,32,32]{0,3,2,1:T(8,128)(2,1)S(1)}, bf16[64,2,32,32]{0,3,2,1:T(8,128)(2,1)}, u32[]{:S(2)}) copy-start(bf16[64,2,32,32]{0,3,2,1:T(8,128)(2,1)} %param.10) | copy-start | bytes 786436
  11.9 55.8 %collective-permute-start.3 = (bf16[2,640,512]{2,1,0:T(8,128)(2,1)S(1)}, bf16[2,640,512]{2,1,0:T(8,128)(2,1)S(1)}, u32[]{:S(2)}, u32[]{:S(2)}) collective-permute-start(bf16[2,640,512]{2,1,0:T(8,128)(2,1)S(1)} %dynamic-slice_bitcast_fusion), channel_id=1, source_target_pairs={{4,0},{8,4},{12,8},{5,1},{9,5},{13,9},{6,2},{10,6},{14,10},{7,3},{... | collective-permute-start | bytes 3932168 | tf_op jit(solution)/shard_map/ppermute | solution.py:17
  32.3 7.4 %collective-permute-start.7 = (bf16[1024,512]{1,0:T(8,128)(2,1)}, bf16[1024,512]{1,0:T(8,128)(2,1)}, u32[]{:S(2)}, u32[]{:S(2)}) collective-permute-start(bf16[1024,512]{1,0:T(8,128)(2,1)} %collective-permute-done.1.refs_1_), channel_id=1, source_target_pairs={{0,1},{1,0},{2,3},{3,2},{4,5},{5,4},{6,7},{7,6},{8,9},{9,8},{10,11... | collective-permute-start | bytes 3145736 | tf_op jit(solution)/shard_map/ppermute | solution.py:361
  37.5 30.2 %collective-permute-start.4 = (bf16[1024,512]{1,0:T(8,128)(2,1)}, bf16[1024,512]{1,0:T(8,128)(2,1)}, u32[]{:S(2)}, u32[]{:S(2)}) collective-permute-start(bf16[1024,512]{1,0:T(8,128)(2,1)} %collective-permute-done.2.refs_0_), channel_id=1, source_target_pairs={{0,2},{1,3},{2,0},{3,1},{4,6},{5,7},{6,4},{7,5},{8,10},{9,11},{10,... | collective-permute-start | bytes 3145736 | tf_op jit(solution)/shard_map/ppermute | solution.py:361
  37.6 30.2 %collective-permute-start.5 = (bf16[1024,512]{1,0:T(8,128)(2,1)}, bf16[1024,512]{1,0:T(8,128)(2,1)}, u32[]{:S(2)}, u32[]{:S(2)}) collective-permute-start(bf16[1024,512]{1,0:T(8,128)(2,1)} %collective-permute-done.2.refs_0_), channel_id=1, source_target_pairs={{0,1},{1,0},{2,3},{3,2},{4,5},{5,4},{6,7},{7,6},{8,9},{9,8},{10,11... | collective-permute-start | bytes 3145736 | tf_op jit(solution)/shard_map/ppermute | solution.py:361
  39.7 41.2 %collective-permute-start.8 = (bf16[2,384,512]{2,1,0:T(8,128)(2,1)}, bf16[2,384,512]{2,1,0:T(8,128)(2,1)}, u32[]{:S(2)}, u32[]{:S(2)}) collective-permute-start(bf16[2,384,512]{2,1,0:T(8,128)(2,1)} %dynamic-slice_bitcast_fusion.1), channel_id=1, source_target_pairs={{4,0},{8,4},{12,8},{5,1},{9,5},{13,9},{6,2},{10,6},{14,10},{7,3},{... | collective-permute-start | bytes 2359304 | tf_op jit(solution)/shard_map/ppermute | solution.py:17
  67.7 16.5 %copy-start = (bf16[2,640,512]{2,1,0:T(8,128)(2,1)}, bf16[2,640,512]{2,1,0:T(8,128)(2,1)S(1)}, u32[]{:S(2)}) copy-start(bf16[2,640,512]{2,1,0:T(8,128)(2,1)S(1)} %collective-permute-done.3.refs_1_) | copy-start | bytes 3932164
  67.8 15.6 %collective-permute-start.9 = (bf16[2,640,512]{2,1,0:T(8,128)(2,1)S(1)}, bf16[2,640,512]{2,1,0:T(8,128)(2,1)S(1)}, u32[]{:S(2)}, u32[]{:S(2)}) collective-permute-start(bf16[2,640,512]{2,1,0:T(8,128)(2,1)S(1)} %collective-permute-done.3.refs_1_), channel_id=1, source_target_pairs={{0,1},{1,0},{2,3},{3,2},{4,5},{5,4},{6,7},{7,6},{8,9},{9,8},{10,11... | collective-permute-start | bytes 3932168 | tf_op jit(solution)/shard_map/ppermute | solution.py:361
  68.7 14.7 %collective-permute-start.11 = (bf16[1024,512]{1,0:T(8,128)(2,1)}, bf16[1024,512]{1,0:T(8,128)(2,1)S(1)}, u32[]{:S(2)}, u32[]{:S(2)}) collective-permute-start(bf16[1024,512]{1,0:T(8,128)(2,1)} %collective-permute-done.4.refs_3_), channel_id=1, source_target_pairs={{0,1},{1,0},{2,3},{3,2},{4,5},{5,4},{6,7},{7,6},{8,9},{9,8},{10,11... | collective-permute-start | bytes 3145736 | tf_op jit(solution)/shard_map/ppermute | solution.py:361
  80.8 2.5 %collective-permute-start.10 = (bf16[2,384,512]{2,1,0:T(8,128)(2,1)}, bf16[2,384,512]{2,1,0:T(8,128)(2,1)S(1)}, u32[]{:S(2)}, u32[]{:S(2)}) collective-permute-start(bf16[2,384,512]{2,1,0:T(8,128)(2,1)} %collective-permute-done.8.refs_2_), channel_id=1, source_target_pairs={{0,1},{1,0},{2,3},{3,2},{4,5},{5,4},{6,7},{7,6},{8,9},{9,8},{10,11... | collective-permute-start | bytes 2359304 | tf_op jit(solution)/shard_map/ppermute | solution.py:361
  83.3 1.0 copy-start.3
  83.3 1.2 copy-start.2
  84.3 1.1 copy-start.1

commit v12 on v11

--- a/solution.py
+++ b/solution.py
@@ -172,7 +172,7 @@
         imag = stage[rows, pl.ds(half + j * tile, tile)].astype(F32)
         return (real + imag).astype(BF16), (real - imag).astype(BF16)
 
-    @pl.loop(0, half // tile)
+    @pl.loop(0, half // tile, unroll=2)
     def _(i):
         here_i, there_i = part_of(here, i, tile), part_of(there, i, tile)
         for j in range(half // tile):
@@ -205,7 +205,7 @@
             copies.append((lower.at[k], stage.at[pl.ds(top, half - top), to]))
     load_all(copies, sems)
 
-    @pl.loop(0, half // tile)
+    @pl.loop(0, half // tile, unroll=2)
     def _(i):
         rows = part_of(0, i, tile)
         here_i, there_i = part_of(here, i, tile), part_of(there, i, tile)

time: 139 us -> 139 us (level)
  no operation moved by 1% of the time
where the time goes in v12:
time: 139 us
  Pallas kernels  89.7 us (65%)
  waiting for transfers between devices  23 us (17%)
  local copies, waits for them, and re-layouts  12.7 us (9%)
  starting transfers between devices  8.95 us (6%)
  other arithmetic  3.46 us (2%)
    pallas_call x2, Pallas kernels, step_call(): pl.pallas_call(functools.partial(kernel, counts, tile, len(pieces)), out_...  79.4 us
    ppermute x4, waiting for transfers between devices, shifted_down(): return lax.ppermute(block, axis, route)  19.2 us
    pallas_call x1, Pallas kernels, operator_tables(): pl.pallas_call(functools.partial(table_kernel, which), out_shape=[jax.Sha...  10.3 us
    unnamed x14, local copies, waits for them, and re-layouts  9.28 us
    ppermute x4, starting transfers between devices, shifted_down(): return lax.ppermute(block, axis, route)  5.45 us
    ppermute x8, waiting for transfers between devices, swapped(): lax.ppermute(block, 'row', [(i, i ^ bit) for i in range(lax.axis_size('ro...  3.84 us
    ppermute x8, starting transfers between devices, swapped(): lax.ppermute(block, 'row', [(i, i ^ bit) for i in range(lax.axis_size('ro...  3.51 us
    squeeze x2, local copies, waits for them, and re-layouts, cut(): lax.dynamic_slice(halves, (first, which, low, 0), (count, 1, high - low,...  3.47 us
  transfers between devices with their start and end apart: 12, of which 5 were waited for; matrix products, arithmetic and copies ran while one was open for 10% of the time, Pallas kernels for 26%

profile of v12, /device:TPU:0, one launch (start us, length us, event | category | flops | bytes accessed | tf_op | source)
XLA Modules:
  0.0 138.8 jit_solution(9511918046198629183)
XLA Ops:
  0.6 0.5 collective-permute-start.6
  1.1 1.3 collective-permute-start
  2.5 2.8 %fusion = bf16[1024,512]{1,0:T(8,128)(2,1)} fusion(bf16[2,2,1024,512]{3,2,1,0:T(8,128)(2,1)} %bitcast.11, s32[]{:T(128)S(6)} %select_n.21), kind=kLoop, calls=%fused_computation.2 | loop fusion | flops 2097152 | bytes 3145732 | tf_op jit(solution)/shard_map/convert_element_type | solution.py:401
  5.3 2.0 %collective-permute-done.controls_next = f32[1,2]{1,0:T(1,128)S(1)} collective-permute-done((f32[1,2]{1,0:T(1,128)}, f32[1,2]{1,0:T(1,128)S(1)}, u32[]{:S(2)}, u32[]{:S(2)}) %collective-permute-start) | collective-permute-done | bytes 40 | tf_op jit(solution)/shard_map/ppermute | solution.py:17
  7.3 0.0 copy-start.5
  7.3 1.9 %collective-permute-start.1 = (bf16[1024,512]{1,0:T(8,128)(2,1)}, bf16[1024,512]{1,0:T(8,128)(2,1)}, u32[]{:S(2)}, u32[]{:S(2)}) collective-permute-start(bf16[1024,512]{1,0:T(8,128)(2,1)} %fusion), channel_id=1, source_target_pairs={{0,2},{1,3},{2,0},{3,1},{4,6},{5,7},{6,4},{7,5},{8,10},{9,11},{10,... | collective-permute-start | bytes 3145736 | tf_op jit(solution)/shard_map/ppermute | solution.py:361
  9.2 1.3 collective-permute-start.2
  10.5 1.4 %dynamic-slice_bitcast_fusion = bf16[2,640,512]{2,1,0:T(8,128)(2,1)S(1)} fusion(bf16[2,2,1024,512]{3,2,1,0:T(8,128)(2,1)} %bitcast.12, s32[]{:T(128)S(6)} %select_n.23), kind=kLoop, calls=%fused_computation.1 | loop fusion | bytes 2621444 | tf_op jit(solution)/shard_map/squeeze | solution.py:399
  11.9 0.0 copy-start.4
  11.9 1.4 %collective-permute-start.3 = (bf16[2,640,512]{2,1,0:T(8,128)(2,1)S(1)}, bf16[2,640,512]{2,1,0:T(8,128)(2,1)S(1)}, u32[]{:S(2)}, u32[]{:S(2)}) collective-permute-start(bf16[2,640,512]{2,1,0:T(8,128)(2,1)S(1)} %dynamic-slice_bitcast_fusion), channel_id=1, source_target_pairs={{4,0},{8,4},{12,8},{5,1},{9,5},{13,9},{6,2},{10,6},{14,10},{7,3},{... | collective-permute-start | bytes 3932168 | tf_op jit(solution)/shard_map/ppermute | solution.py:17
  13.4 4.8 %copy.8.ham = bf16[2,64,2,32,32]{4,3,2,1,0:T(8,128)(2,1)} copy(bf16[2,64,2,32,32]{1,4,3,2,0:T(8,128)(2,1)} %param.8) | data formatting | bytes 1048576 | tf_op args[2]
  18.2 0.0 copy-done.5
  18.2 0.0 copy-done.4
  18.2 2.4 %copy.9.jump = bf16[64,2,32,32]{3,2,1,0:T(8,128)(2,1)} copy(bf16[64,2,32,32]{0,3,2,1:T(8,128)(2,1)S(1)} %copy-done.4) | data formatting | bytes 524288 | tf_op args[4]
  20.6 10.3 %operator_tables.1 = (s32[9,64]{1,0:T(8,128)}, bf16[16,128,256]{2,1,0:T(8,128)(2,1)}, bf16[64,32,224]{2,1,0:T(8,128)(2,1)}, bf16[64,32,224]{2,1,0:T(8,128)(2,1)}...) custom-call(s32[2,64]{1,0:T(2,128)} %ham_cols.1, ...), custom_call_target="tpu_custom_call" | custom-call | flops 1 | bytes 1 | tf_op jit(solution)/shard_map/operator_tables/pallas_call | solution.py:87
  31.0 1.3 collective-permute-done.1.refs_1_
  32.3 0.0 collective-permute-start.7
  32.3 5.2 %collective-permute-done.2.refs_0_ = bf16[1024,512]{1,0:T(8,128)(2,1)} collective-permute-done((bf16[1024,512]{1,0:T(8,128)(2,1)}, bf16[1024,512]{1,0:T(8,128)(2,1)}, u32[]{:S(2)}, u32[]{:S(2)}) %collective-permute-start.2) | collective-permute-done | bytes 1048608 | tf_op jit(solution)/shard_map/ppermute | solution.py:17
  37.5 0.1 collective-permute-start.4
  37.6 0.0 collective-permute-start.5
  37.6 2.1 %dynamic-slice_bitcast_fusion.1 = bf16[2,384,512]{2,1,0:T(8,128)(2,1)} fusion(bf16[2,2,1024,512]{3,2,1,0:T(8,128)(2,1)} %bitcast.13, s32[]{:T(128)S(6)} %select_n.23), kind=kLoop, calls=%fused_computation.3 | loop fusion | bytes 1572868 | tf_op jit(solution)/shard_map/squeeze | solution.py:399
  39.7 0.0 collective-permute-done.7.refs_2_
  39.7 1.5 %collective-permute-start.8 = (bf16[2,384,512]{2,1,0:T(8,128)(2,1)}, bf16[2,384,512]{2,1,0:T(8,128)(2,1)}, u32[]{:S(2)}, u32[]{:S(2)}) collective-permute-start(bf16[2,384,512]{2,1,0:T(8,128)(2,1)} %dynamic-slice_bitcast_fusion.1), channel_id=1, source_target_pairs={{4,0},{8,4},{12,8},{5,1},{9,5},{13,9},{6,2},{10,6},{14,10},{7,3},{... | collective-permute-start | bytes 2359304 | tf_op jit(solution)/shard_map/ppermute | solution.py:17
  41.2 0.7 pad_add_fusion.place
  41.8 0.0 collective-permute-done.6.refs_0_
  41.8 26.1 %inner_point.1 = bf16[1,2,2048,512]{3,2,1,0:T(8,128)(2,1)} custom-call(s32[9,64]{1,0:T(8,128)} %get-tuple-element.22.rows, s32[4]{0:T(128)} %pad_add_fusion.place, bf16[1,2,2048,512]{3,2,1,0:T(8,128)(2,1)} %terminal.3, bf16[16,128,256]{2,1,0:T(8,128)(2,1)} %get-tuple-element.23.jump, bf16[64,32,224]{2,1,0:T(8,128)(2,1)} %get-tuple-element.29.plus, ...), custom_call_target="tpu_custom_call" | custom-call | flops 1 | bytes 1 | tf_op jit(solution)/shard_map/inner_point/pallas_call | solution.py:380
  67.9 0.0 collective-permute-done.3.refs_1_
  67.9 0.0 copy-start
  67.9 0.0 collective-permute-done.4.refs_3_
  67.9 0.0 collective-permute-done.5.refs_4_
  67.9 0.9 collective-permute-start.9
  68.8 0.1 collective-permute-start.11
  68.9 11.9 %collective-permute-done.8.refs_2_ = bf16[2,384,512]{2,1,0:T(8,128)(2,1)} collective-permute-done((bf16[2,384,512]{2,1,0:T(8,128)(2,1)}, bf16[2,384,512]{2,1,0:T(8,128)(2,1)}, u32[]{:S(2)}, u32[]{:S(2)}) %collective-permute-start.8) | collective-permute-done | bytes 786464 | tf_op jit(solution)/shard_map/ppermute | solution.py:17
  80.8 0.0 collective-permute-start.10
  80.8 2.5 %collective-permute-done.10.refs_6_ = bf16[2,384,512]{2,1,0:T(8,128)(2,1)S(1)} collective-permute-done((bf16[2,384,512]{2,1,0:T(8,128)(2,1)}, bf16[2,384,512]{2,1,0:T(8,128)(2,1)S(1)}, u32[]{:S(2)}, u32[]{:S(2)}) %collective-permute-start.10) | collective-permute-done | bytes 786464 | tf_op jit(solution)/shard_map/ppermute | solution.py:361
  83.3 0.0 copy-start.3
  83.3 0.0 collective-permute-done.11.refs_7_
  83.3 0.0 copy-start.2
  83.3 0.0 collective-permute-done.9.refs_5_
  83.3 0.9 copy-done.3
  84.3 0.0 copy-start.1
  84.3 0.0 copy-done
  84.3 0.3 copy-done.2
  84.5 0.8 copy-done.1
  85.3 53.3 %left_end.1 = bf16[1,2,2048,512]{3,2,1,0:T(8,128)(2,1)} custom-call(s32[9,64]{1,0:T(8,128)} %get-tuple-element.22.rows, s32[4]{0:T(128)} %pad_add_fusion.place, bf16[1,2,2048,512]{3,2,1,0:T(8,128)(2,1)} %terminal.3, bf16[16,128,256]{2,1,0:T(8,128)(2,1)} %get-tuple-element.23.jump, bf16[64,32,224]{2,1,0:T(8,128)(2,1)} %get-tuple-element.24.plus, ...), custom_call_target="tpu_custom_call" | custom-call | flops 1 | bytes 1 | tf_op jit(solution)/shard_map/left_end/pallas_call | solution.py:380
Async XLA Ops:
  0.6 41.2 %collective-permute-start.6 = (bf16[1,2,2048,512]{3,2,1,0:T(8,128)(2,1)}, bf16[1,2,2048,512]{3,2,1,0:T(8,128)(2,1)}, u32[]{:S(2)}, u32[]{:S(2)}) collective-permute-start(bf16[1,2,2048,512]{3,2,1,0:T(8,128)(2,1)} %terminal.3), channel_id=1, source_target_pairs={{0,1},{1,0},{2,3},{3,2},{4,5},{5,4},{6,7},{7,6},{8,9},{9,8},{10,11... | collective-permute-start | bytes 12582920 | tf_op jit(solution)/shard_map/ppermute | solution.py:361
  1.1 6.1 %collective-permute-start = (f32[1,2]{1,0:T(1,128)}, f32[1,2]{1,0:T(1,128)S(1)}, u32[]{:S(2)}, u32[]{:S(2)}) collective-permute-start(f32[1,2]{1,0:T(1,128)} %controls.1), channel_id=1, source_target_pairs={{4,0},{8,4},{12,8},{5,1},{9,5},{13,9},{6,2},{10,6},{14,10},{7,3},{... | collective-permute-start | bytes 32 | tf_op jit(solution)/shard_map/ppermute | solution.py:17
  7.3 10.9 %copy-start.5 = (f32[1,2]{1,0:T(1,128)}, f32[1,2]{1,0:T(1,128)S(1)}, u32[]{:S(2)}) copy-start(f32[1,2]{1,0:T(1,128)S(1)} %collective-permute-done.controls_next) | copy-start | bytes 28
  7.3 25.0 %collective-permute-start.1 = (bf16[1024,512]{1,0:T(8,128)(2,1)}, bf16[1024,512]{1,0:T(8,128)(2,1)}, u32[]{:S(2)}, u32[]{:S(2)}) collective-permute-start(bf16[1024,512]{1,0:T(8,128)(2,1)} %fusion), channel_id=1, source_target_pairs={{0,2},{1,3},{2,0},{3,1},{4,6},{5,7},{6,4},{7,5},{8,10},{9,11},{10,... | collective-permute-start | bytes 3145736 | tf_op jit(solution)/shard_map/ppermute | solution.py:361
  9.2 28.3 %collective-permute-start.2 = (bf16[1024,512]{1,0:T(8,128)(2,1)}, bf16[1024,512]{1,0:T(8,128)(2,1)}, u32[]{:S(2)}, u32[]{:S(2)}) collective-permute-start(bf16[1024,512]{1,0:T(8,128)(2,1)} %fusion), channel_id=1, source_target_pairs={{4,0},{8,4},{12,8},{5,1},{9,5},{13,9},{6,2},{10,6},{14,10},{7,3},{... | collective-permute-start | bytes 3145736 | tf_op jit(solution)/shard_map/ppermute | solution.py:17
  11.9 6.3 %copy-start.4 = (bf16[64,2,32,32]{0,3,2,1:T(8,128)(2,1)S(1)}, bf16[64,2,32,32]{0,3,2,1:T(8,128)(2,1)}, u32[]{:S(2)}) copy-start(bf16[64,2,32,32]{0,3,2,1:T(8,128)(2,1)} %param.10) | copy-start | bytes 786436
  11.9 56.0 %collective-permute-start.3 = (bf16[2,640,512]{2,1,0:T(8,128)(2,1)S(1)}, bf16[2,640,512]{2,1,0:T(8,128)(2,1)S(1)}, u32[]{:S(2)}, u32[]{:S(2)}) collective-permute-start(bf16[2,640,512]{2,1,0:T(8,128)(2,1)S(1)} %dynamic-slice_bitcast_fusion), channel_id=1, source_target_pairs={{4,0},{8,4},{12,8},{5,1},{9,5},{13,9},{6,2},{10,6},{14,10},{7,3},{... | collective-permute-start | bytes 3932168 | tf_op jit(solution)/shard_map/ppermute | solution.py:17
  32.3 7.4 %collective-permute-start.7 = (bf16[1024,512]{1,0:T(8,128)(2,1)}, bf16[1024,512]{1,0:T(8,128)(2,1)}, u32[]{:S(2)}, u32[]{:S(2)}) collective-permute-start(bf16[1024,512]{1,0:T(8,128)(2,1)} %collective-permute-done.1.refs_1_), channel_id=1, source_target_pairs={{0,1},{1,0},{2,3},{3,2},{4,5},{5,4},{6,7},{7,6},{8,9},{9,8},{10,11... | collective-permute-start | bytes 3145736 | tf_op jit(solution)/shard_map/ppermute | solution.py:361
  37.5 30.4 %collective-permute-start.4 = (bf16[1024,512]{1,0:T(8,128)(2,1)}, bf16[1024,512]{1,0:T(8,128)(2,1)}, u32[]{:S(2)}, u32[]{:S(2)}) collective-permute-start(bf16[1024,512]{1,0:T(8,128)(2,1)} %collective-permute-done.2.refs_0_), channel_id=1, source_target_pairs={{0,2},{1,3},{2,0},{3,1},{4,6},{5,7},{6,4},{7,5},{8,10},{9,11},{10,... | collective-permute-start | bytes 3145736 | tf_op jit(solution)/shard_map/ppermute | solution.py:361
  37.6 30.3 %collective-permute-start.5 = (bf16[1024,512]{1,0:T(8,128)(2,1)}, bf16[1024,512]{1,0:T(8,128)(2,1)}, u32[]{:S(2)}, u32[]{:S(2)}) collective-permute-start(bf16[1024,512]{1,0:T(8,128)(2,1)} %collective-permute-done.2.refs_0_), channel_id=1, source_target_pairs={{0,1},{1,0},{2,3},{3,2},{4,5},{5,4},{6,7},{7,6},{8,9},{9,8},{10,11... | collective-permute-start | bytes 3145736 | tf_op jit(solution)/shard_map/ppermute | solution.py:361
  39.7 41.2 %collective-permute-start.8 = (bf16[2,384,512]{2,1,0:T(8,128)(2,1)}, bf16[2,384,512]{2,1,0:T(8,128)(2,1)}, u32[]{:S(2)}, u32[]{:S(2)}) collective-permute-start(bf16[2,384,512]{2,1,0:T(8,128)(2,1)} %dynamic-slice_bitcast_fusion.1), channel_id=1, source_target_pairs={{4,0},{8,4},{12,8},{5,1},{9,5},{13,9},{6,2},{10,6},{14,10},{7,3},{... | collective-permute-start | bytes 2359304 | tf_op jit(solution)/shard_map/ppermute | solution.py:17
  67.9 16.4 %copy-start = (bf16[2,640,512]{2,1,0:T(8,128)(2,1)}, bf16[2,640,512]{2,1,0:T(8,128)(2,1)S(1)}, u32[]{:S(2)}) copy-start(bf16[2,640,512]{2,1,0:T(8,128)(2,1)S(1)} %collective-permute-done.3.refs_1_) | copy-start | bytes 3932164
  67.9 15.4 %collective-permute-start.9 = (bf16[2,640,512]{2,1,0:T(8,128)(2,1)S(1)}, bf16[2,640,512]{2,1,0:T(8,128)(2,1)S(1)}, u32[]{:S(2)}, u32[]{:S(2)}) collective-permute-start(bf16[2,640,512]{2,1,0:T(8,128)(2,1)S(1)} %collective-permute-done.3.refs_1_), channel_id=1, source_target_pairs={{0,1},{1,0},{2,3},{3,2},{4,5},{5,4},{6,7},{7,6},{8,9},{9,8},{10,11... | collective-permute-start | bytes 3932168 | tf_op jit(solution)/shard_map/ppermute | solution.py:361
  68.8 14.5 %collective-permute-start.11 = (bf16[1024,512]{1,0:T(8,128)(2,1)}, bf16[1024,512]{1,0:T(8,128)(2,1)S(1)}, u32[]{:S(2)}, u32[]{:S(2)}) collective-permute-start(bf16[1024,512]{1,0:T(8,128)(2,1)} %collective-permute-done.4.refs_3_), channel_id=1, source_target_pairs={{0,1},{1,0},{2,3},{3,2},{4,5},{5,4},{6,7},{7,6},{8,9},{9,8},{10,11... | collective-permute-start | bytes 3145736 | tf_op jit(solution)/shard_map/ppermute | solution.py:361
  80.8 2.5 %collective-permute-start.10 = (bf16[2,384,512]{2,1,0:T(8,128)(2,1)}, bf16[2,384,512]{2,1,0:T(8,128)(2,1)S(1)}, u32[]{:S(2)}, u32[]{:S(2)}) collective-permute-start(bf16[2,384,512]{2,1,0:T(8,128)(2,1)} %collective-permute-done.8.refs_2_), channel_id=1, source_target_pairs={{0,1},{1,0},{2,3},{3,2},{4,5},{5,4},{6,7},{7,6},{8,9},{9,8},{10,11... | collective-permute-start | bytes 2359304 | tf_op jit(solution)/shard_map/ppermute | solution.py:361
  83.3 1.0 copy-start.3
  83.3 1.2 copy-start.2
  84.3 1.1 copy-start.1
